TPU v7x, 32 devices: a whole 2x2x4 slice. The times are simulated.
32 devices in a mesh: exp: 2 (over x), tx: 4 (over z), ty: 4 (over y, core).
Axes of the slice: x: 2, y: 2, z: 4, core: 2. Of those that a mesh axis runs over, the one named last changes fastest.
Arguments:
- exposures: bfloat16 [4, 512, 128, 128], P('ty', ('exp', 'tx')), may hold values from -8 to 8
- block_tile: int32 [4, 512, 1], P('ty', ('exp', 'tx')), may hold values from 0 to 3, as said below
- affine: int32 [4, 512, 2, 4], P('ty', ('exp', 'tx')), may hold values from -512 to 512
- col_mask: int32 [4, 512, 128], P('ty', ('exp', 'tx')), may hold values 0 or 1
- block_weight: float32 [4, 512], P('ty', ('exp', 'tx')), may hold values from 0.5 to 4
- psf: float32 [2, 2, 9], replicated, may hold values from 0.05 to 0.6
Outputs:
- gradients: float32 [4, 512, 2, 4], P('ty', ('exp', 'tx'))
- coadd: float32 [512, 512], P('tx', 'ty')
Inputs may be any that keep to these rules, and one draw needn't show every extreme that they name: `block_tile`: each device's 64 blocks name any tile row at most 32 times, and some tile row exactly 32 times.
All inputs are finite; a program needn't handle non-finite values. No bound on the sum of `col_mask` on one device may be relied on, other than what follows from the above.
Results may differ from a plain program's by a relative error of at most 0.0026.
Values may be sent and summed in bfloat16 or wider, within the bound.
No kernel may reach another device: no remote copies, remote signals or barrier semaphores. Data moves between devices by JAX's collectives and lax.ppermute only.
A program may use at most 128 MiB of HBM per device.

v0:
```python
import jax
import jax.numpy as jnp
from jax import lax
from jax.sharding import PartitionSpec as P

RAD = 4
ITERS = 2


def extended(cells, sides, width):
    for axis, dim in sides:
        count = lax.axis_size(axis)
        ends = count - 1
        head = lax.slice_in_dim(cells, 0, width, axis=dim)
        tail = lax.slice_in_dim(cells, cells.shape[dim] - width, cells.shape[dim], axis=dim)
        cells = jnp.concatenate(
            [
                lax.ppermute(tail, axis, [(i, (i + 1) % count) for i in range(ends)]),
                cells,
                lax.ppermute(head, axis, [((i + 1) % count, i) for i in range(ends)]),
            ],
            axis=dim,
        )
    return cells


def lanczos(offsets):
    inside = jnp.abs(offsets) < 3.0
    return jnp.where(inside, jnp.sinc(offsets) * jnp.sinc(offsets / 3.0), 0.0)


def band_pair(shift, stretch, block_side):
    positions = jnp.arange(block_side, dtype=jnp.float32)
    centre = (block_side - 1) / 2.0
    source = centre + (1.0 + stretch) * (positions - centre) + shift
    offsets = source[:, None] - positions[None, :]
    values, slopes = jax.jvp(lanczos, (offsets,), (jnp.ones_like(offsets),))
    return (values.astype(jnp.bfloat16), slopes.astype(jnp.bfloat16))


def warp_block(block, column_mask, affine_terms, weight):
    block_side = block.shape[0]
    scaled = affine_terms.astype(jnp.float32)
    row_band, row_slope = band_pair(scaled[1] / 256.0, scaled[3] / 51200.0, block_side)
    col_band, col_slope = band_pair(scaled[0] / 256.0, scaled[2] / 51200.0, block_side)
    mask_row = column_mask.astype(jnp.bfloat16)
    masked = block * mask_row[None, :]
    row_pass = jnp.dot(row_band, masked, preferred_element_type=jnp.float32).astype(jnp.bfloat16)
    col_pass = jnp.dot(masked, col_band.T, preferred_element_type=jnp.float32).astype(jnp.bfloat16)
    warped = jnp.dot(row_pass, col_band.T, preferred_element_type=jnp.float32)
    slope_x = jnp.dot(row_pass, col_slope.T, preferred_element_type=jnp.float32)
    slope_y = jnp.dot(row_slope, col_pass, preferred_element_type=jnp.float32)
    rows_sum = jnp.sum(row_band.astype(jnp.float32), axis=1)
    cols_sum = jnp.dot(col_band, mask_row, preferred_element_type=jnp.float32)
    sent = (weight * warped).astype(jnp.bfloat16)
    profile = jnp.stack([(weight * rows_sum).astype(jnp.bfloat16), cols_sum.astype(jnp.bfloat16)])
    return (sent, profile, warped, slope_x, slope_y, rows_sum, cols_sum)


def gradient_terms(warped, slope_x, slope_y, rows_sum, cols_sum, cutout):
    block_side = warped.shape[0]
    centre = (block_side - 1) / 2.0
    coords = (jnp.arange(block_side, dtype=jnp.float32) - centre) / block_side
    residual = (warped - cutout.astype(jnp.float32)) * jax.nn.relu(
        rows_sum[:, None] * cols_sum[None, :]
    )
    first = jnp.sum(residual * slope_x) / block_side
    second = jnp.sum(residual * slope_y) / block_side
    third = jnp.sum(residual * slope_x * coords[None, :]) / block_side
    fourth = jnp.sum(residual * slope_y * coords[:, None]) / block_side
    return jnp.stack([first, second, third, fourth])


def convolve(padded, psf_taps, rows_out, cols_out):
    row_smoothed = psf_taps[0, 0] * padded[0:rows_out, :]
    for offset_index in range(1, psf_taps.shape[1]):
        row_smoothed = (
            row_smoothed
            + psf_taps[0, offset_index] * padded[offset_index : offset_index + rows_out, :]
        )
    smoothed = psf_taps[1, 0] * row_smoothed[:, 0:cols_out]
    for offset_index in range(1, psf_taps.shape[1]):
        smoothed = (
            smoothed
            + psf_taps[1, offset_index] * row_smoothed[:, offset_index : offset_index + cols_out]
        )
    return smoothed


def local(exposures, block_tile, affine, col_mask, block_weight, psf):
    blocks = exposures[0]
    target = block_tile[0, :, 0]
    pixel_masks = col_mask[0]
    weights = block_weight[0]
    block_count = blocks.shape[0]
    block_side = blocks.shape[1]
    tile_rows = lax.axis_size("tx")
    slot_cap = max(2, 2 * block_count // tile_rows)
    one_hot = (target[:, None] == jnp.arange(tile_rows, dtype=jnp.int32)[None, :]).astype(jnp.int32)
    before = jnp.cumsum(one_hot, axis=0) - one_hot
    slot_rank = jnp.sum(before * one_hot, axis=1)
    slot_index = target * slot_cap + slot_rank
    coadd_tile = jnp.zeros((block_side, block_side), jnp.float32)
    gradient_list = []
    for iteration in range(ITERS):
        outputs = jax.vmap(warp_block)(blocks, pixel_masks, affine[0, :, iteration, :], weights)
        sent, profile = (outputs[0], outputs[1])
        profile_slots = (
            jnp.zeros((tile_rows * slot_cap, 2, block_side), jnp.bfloat16)
            .at[slot_index]
            .set(profile)
        )
        block_slots = (
            jnp.zeros((tile_rows * slot_cap, block_side, block_side), jnp.bfloat16)
            .at[slot_index]
            .set(sent)
        )
        got_blocks, got_profiles = (
            lax.all_to_all(block_slots, "tx", split_axis=0, concat_axis=0, tiled=True),
            lax.all_to_all(profile_slots, "tx", split_axis=0, concat_axis=0, tiled=True),
        )
        numerator = jnp.sum(got_blocks, axis=0, dtype=jnp.float32)
        rows_part = got_profiles[:, 0, :].astype(jnp.float32)
        cols_part = got_profiles[:, 1, :].astype(jnp.float32)
        denominator = jnp.dot(
            jax.nn.relu(rows_part).T, jax.nn.relu(cols_part), precision=lax.Precision.HIGHEST
        )
        denominator = denominator + jnp.dot(
            jax.nn.relu(-rows_part).T, jax.nn.relu(-cols_part), precision=lax.Precision.HIGHEST
        )
        numerator, denominator = lax.psum((numerator, denominator), "exp")
        coadd_tile = (numerator + coadd_tile) / (1.0 + denominator)
        padded = extended(coadd_tile, (("tx", 0), ("ty", 1)), RAD)
        model_tile = convolve(padded, psf[iteration], block_side, block_side).astype(jnp.bfloat16)
        column_tiles = lax.all_gather(model_tile[None], "tx", axis=0, tiled=True)
        cutouts = jnp.take(column_tiles, target, axis=0)
        found = jax.vmap(gradient_terms)(
            outputs[2], outputs[3], outputs[4], outputs[5], outputs[6], cutouts
        )
        gradient_list.append(found)
    gradients = jnp.stack(gradient_list, axis=1)[None]
    return (gradients, coadd_tile)


def solution(mesh):
    placed = (
        P("ty", ("exp", "tx"), None, None),
        P("ty", ("exp", "tx"), None),
        P("ty", ("exp", "tx"), None, None),
        P("ty", ("exp", "tx"), None),
        P("ty", ("exp", "tx")),
        P(),
    )
    return jax.shard_map(
        local,
        mesh=mesh,
        in_specs=placed,
        out_specs=(P("ty", ("exp", "tx"), None, None), P("tx", "ty")),
        check_vma=False,
    )
```

profile of v0, /device:TPU:0, one launch (start us, length us, event | category | flops | bytes accessed | tf_op | source)
XLA Modules:
  0.0 581.3 jit_solution(6441333285218683529)
XLA Ops:
  11.7 11.3 %convert_reduce_fusion.2 = f32[64,128]{1,0:T(8,128)S(1)} fusion(f32[64,128]{1,0:T(8,128)S(1)} %get-tuple-element.126), kind=kLoop, calls=%fused_computation.303 | loop fusion | flops 77586432 | bytes 65536 | tf_op jit(solution)/shard_map/vmap()/reduce_sum | solution.py:53
  23.1 11.3 %convert_reduce_fusion.3 = f32[64,128]{1,0:T(8,128)S(1)} fusion(f32[64,128]{1,0:T(8,128)S(1)} %get-tuple-element.128), kind=kLoop, calls=%fused_computation.324 | loop fusion | flops 77586432 | bytes 65536 | tf_op jit(solution)/shard_map/vmap()/reduce_sum | solution.py:53
  34.5 11.4 %fusion.195 = f32[64,1,128]{2,1,0:T(1,128)S(1)} fusion(f32[64,128]{1,0:T(8,128)S(1)} %get-tuple-element.127, bf16[64,128,1]{1,0,2:T(8,128)(2,1)S(1)} %get-tuple-element.65), kind=kOutput, calls=%fused_computation.363 | convolution fusion | flops 77594624 | bytes 81920 | tf_op jit(solution)/shard_map/vmap()/dot_general | solution.py:54
  47.3 7.4 %scatter_fusion.3 = bf16[128,2,128]{2,1,0:T(2,128)(2,1)} fusion(bf16[128,2,128]{2,1,0:T(2,128)(2,1)} %broadcast.404.clone, s32[64]{0:T(128)S(1)} %fusion.251, bf16[64,2,128]{2,1,0:T(2,128)(2,1)S(1)} %copy.11), kind=kCustom, calls=%fused_computation.5 | custom fusion | bytes 98560 | tf_op jit(solution)/shard_map/scatter | solution.py:111
  54.7 6.3 %all-to-all-start.3 = ((bf16[128,2,128]{2,1,0:T(2,128)(2,1)}), bf16[128,2,128]{2,1,0:T(2,128)(2,1)}, u32[]{:S(2)}, u32[]{:S(2)}) async-start(bf16[128,2,128]{2,1,0:T(2,128)(2,1)} %scatter_fusion.3), calls=%async_computation.3 | async-start | bytes 131072 | tf_op jit(solution)/shard_map/all_to_all | solution.py:120
  61.0 11.5 %fusion.201 = bf16[64,128,128]{2,1,0:T(8,128)(2,1)S(1)} fusion(f32[64,128]{1,0:T(8,128)S(1)} %get-tuple-element.126, bf16[1,64,128,128]{3,2,1,0:T(8,128)(2,1)S(1)} %copy-done.31, bf16[64,128]{1,0:T(8,128)(2,1)S(1)} %get-tuple-element.66), kind=kOutput, calls=%fused_computation.370 | convolution fusion | flops 346030080 | bytes 4243456 | tf_op jit(solution)/shard_map/vmap()/dot_general | solution.py:48
  72.5 12.2 %fusion.200 = bf16[64,128,128]{2,1,0:T(8,128)(2,1)} fusion(f32[64,128]{1,0:T(8,128)S(1)} %get-tuple-element.128, bf16[1,64,128,128]{3,2,1,0:T(8,128)(2,1)S(1)} %copy-done.31, bf16[64,128]{1,0:T(8,128)(2,1)S(1)} %get-tuple-element.66), kind=kOutput, calls=%fused_computation.369 | convolution fusion | flops 346030080 | bytes 4243456 | tf_op jit(solution)/shard_map/vmap()/dot_general | solution.py:48
  84.7 12.3 %fusion.196 = f32[64,128,128]{2,1,0:T(8,128)} fusion(bf16[64,128,128]{2,1,0:T(8,128)(2,1)S(1)} %fusion.201, f32[64,128]{1,0:T(8,128)S(1)} %get-tuple-element.127), kind=kOutput, calls=%fused_computation.364 | convolution fusion | flops 343932928 | bytes 6324224 | tf_op jit(solution)/shard_map/vmap()/dot_general | solution.py:50
  97.1 11.4 %fusion.193 = f32[64,1,128]{2,1,0:T(1,128)S(1)} fusion(f32[64,128]{1,0:T(8,128)S(1)} %copy-done.12, bf16[64,128,1]{1,0,2:T(8,128)(2,1)S(1)} %copy-done.19), kind=kOutput, calls=%fused_computation.361 | convolution fusion | flops 77594624 | bytes 81920 | tf_op jit(solution)/shard_map/vmap()/dot_general | solution.py:54
  109.7 7.3 %scatter_fusion.1 = bf16[128,2,128]{2,1,0:T(2,128)(2,1)} fusion(bf16[128,2,128]{2,1,0:T(2,128)(2,1)} %broadcast.404.clone.1, s32[64]{0:T(128)S(1)} %copy-done.25, bf16[64,2,128]{2,1,0:T(2,128)(2,1)S(1)} %copy.10), kind=kCustom, calls=%fused_computation.3 | custom fusion | bytes 98560 | tf_op jit(solution)/shard_map/scatter | solution.py:111
  117.0 5.5 all-to-all-start.1
  122.5 13.5 %multiply_convert_fusion.1 = (bf16[64,128,128]{2,1,0:T(8,128)(2,1)S(1)}, bf16[64,128,128]{2,1,0:T(8,128)(2,1)}, f32[64,128,128]{2,1,0:T(8,128)}) fusion(f32[64]{0:T(128)S(1)} %bitcast.172, f32[64,128,128]{2,1,0:T(8,128)} %fusion.196, bf16[64,128,128]{2,1,0:T(8,128)(2,1)} %fusion.200, f32[64,128]{1,0:T(8,128)S(1)} %copy-done.12), kind=kOutput, calls=%fused_computation.325 | convolution fusion | flops 348127232 | bytes 14713088 | tf_op jit(solution)/shard_map/vmap()/dot_general | solution.py:50
  136.0 3.0 broadcast.400.clone
  139.0 9.9 %scatter_fusion.2 = bf16[128,128,128]{2,1,0:T(8,128)(2,1)} fusion(bf16[128,128,128]{2,1,0:T(8,128)(2,1)} %broadcast.400.clone, s32[64]{0:T(128)S(1)} %copy-done.25, bf16[64,128,128]{2,1,0:T(8,128)(2,1)} %get-tuple-element.124), kind=kCustom, calls=%fused_computation.4 | custom fusion | bytes 6291712 | tf_op jit(solution)/shard_map/scatter | solution.py:116
  148.9 5.1 all-to-all-start.2
  154.0 3.0 broadcast.400.clone.1
  157.0 8.6 %scatter_fusion = bf16[128,128,128]{2,1,0:T(8,128)(2,1)} fusion(bf16[128,128,128]{2,1,0:T(8,128)(2,1)} %broadcast.400.clone.1, s32[64]{0:T(128)S(1)} %copy-done.25, bf16[64,128,128]{2,1,0:T(8,128)(2,1)S(1)} %get-tuple-element.123), kind=kCustom, calls=%fused_computation.2 | custom fusion | bytes 6291712 | tf_op jit(solution)/shard_map/scatter | solution.py:116
  165.6 80.9 %all-to-all-done.2 = bf16[128,128,128]{2,1,0:T(8,128)(2,1)} async-done(((bf16[128,128,128]{2,1,0:T(8,128)(2,1)}), bf16[128,128,128]{2,1,0:T(8,128)(2,1)}, u32[]{:S(2)}, u32[]{:S(2)}) %all-to-all-start.2) | async-done | bytes 4194336 | tf_op jit(solution)/shard_map/all_to_all | solution.py:119
  246.5 4.9 all-to-all-start
  252.9 1.1 negate_maximum_fusion
  254.9 0.9 convolution_add_fusion
  256.7 3.4 convert_reduce_fusion
  260.2 83.9 %all-to-all-done = bf16[128,128,128]{2,1,0:T(8,128)(2,1)} async-done(((bf16[128,128,128]{2,1,0:T(8,128)(2,1)}), bf16[128,128,128]{2,1,0:T(8,128)(2,1)}, u32[]{:S(2)}, u32[]{:S(2)}) %all-to-all-start) | async-done | bytes 4194336 | tf_op jit(solution)/shard_map/all_to_all | solution.py:119
  344.1 3.4 convert_reduce_fusion.1
  348.1 22.4 %all-reduce.3.cloned.1.call-done = (f32[128,128]{1,0:T(8,128)}, f32[128,128]{1,0:T(8,128)}, f32[128,128]{1,0:T(8,128)}, f32[128,128]{1,0:T(8,128)}) async-done(((f32[128,128]{1,0:T(8,128)}, f32[128,128]{1,0:T(8,128)}, f32[128,128]{1,0:T(8,128)}, f32[128,128]{1,0:T(8,128)}), (f32[128,128]{1,0:T(8,128)}, f32[128,128]{1,0:T(8,128)}, f32[128,128]{1,0:T(8,128)}, ...) | async-done | bytes 262160 | tf_op jit(solution)/shard_map/psum | solution.py:131
  370.4 1.0 add_divide_fusion
  371.4 3.4 collective-permute-start.4
  374.8 1.3 collective-permute-start.5
  376.1 4.5 collective-permute-start
  380.7 1.3 collective-permute-start.1
  382.1 1.3 collective-permute-start.6
  383.4 1.3 collective-permute-start.7
  384.7 1.4 collective-permute-done.1
  386.9 3.9 collective-permute-start.2
  390.8 1.3 collective-permute-start.3
  392.3 5.8 fusion.208
  398.1 6.1 %fusion.225 = bf16[128,128]{1,0:T(8,128)(2,1)S(1)} fusion(f32[128,136]{1,0:T(8,128)S(1)} %fusion.208, f32[]{:T(128)} %bitcast.80, f32[]{:T(128)} %bitcast.79, f32[]{:T(128)} %bitcast.78, f32[]{:T(128)} %bitcast.77, f32[]{:T(128)} %bitcast.76, f32[]{:T(128)} %bitcast.75, f32[]{:T(128)} %bitcast.74, f32[]{:T(128)} %bitcast.73, f32[]{:T(128)} %bitcast.54), kind=kLoop, calls=%fused_computation.417 | loop fusion | flops 294912 | bytes 622628 | tf_op jit(solution)/shard_map/convert_element_type | solution.py:134
  404.1 14.8 %all-gather.1 = bf16[512,128]{1,0:T(8,128)(2,1)S(1)} all-gather(bf16[128,128]{1,0:T(8,128)(2,1)S(1)} %fusion.225), channel_id=3, replica_groups=mesh['exp'=2,'tx'=4,'ty'=4] {'tx'}, dimensions={0}, use_global_device_ids=true | all-gather | bytes 163840 | tf_op jit(solution)/shard_map/all_gather | solution.py:135
  419.0 1.0 gather_fusion.1
  419.9 46.4 %convolution_multiply_fusion = f32[64,128,128]{2,1,0:T(8,128)} fusion(f32[64,128,128]{2,1,0:T(8,128)} %fusion.196, f32[64,128]{1,0:T(8,128)S(1)} %bitcast.167, f32[64,128]{1,0:T(8,128)S(1)} %copy-done.7, f32[]{:T(128)S(6)} %neg.79, f32[]{:T(128)S(6)} %neg.75, f32[64,128]{1,0:T(8,128)S(1)} %copy-done.17, f32[64,128]{1,0:T(8,128)S(1)} %get-tuple-element.127, ...), kind=kOutput, calls=%fused_computation.346 | convolution fusion | flops 760217600 | bytes 12730440 | tf_op jit(solution)/shard_map/vmap()/dot_general | solution.py:52
  466.4 22.1 %convolution_multiply_fusion.1 = f32[64,128,128]{2,1,0:T(8,128)} fusion(bf16[64,128,128]{2,1,0:T(8,128)(2,1)} %copy-done.33, f32[64,128,128]{2,1,0:T(8,128)} %fusion.196, f32[64,128]{1,0:T(8,128)S(1)} %bitcast.168, f32[64,128]{1,0:T(8,128)S(1)} %copy-done.7, f32[]{:T(128)S(6)} %neg.79, f32[]{:T(128)S(6)} %neg.75, f32[64,128]{1,0:T(8,128)S(1)} %get-tuple-element.127, ...), kind=kOutput, calls=%fused_computation.347 | convolution fusion | flops 414187520 | bytes 12681288 | tf_op jit(solution)/shard_map/vmap()/dot_general | solution.py:51
  488.5 1.0 pad_maximum_fusion
  489.6 5.7 fusion.216
  495.3 5.7 fusion.234
  501.0 13.4 %all-gather = bf16[512,128]{1,0:T(8,128)(2,1)S(1)} all-gather(bf16[128,128]{1,0:T(8,128)(2,1)S(1)} %fusion.234), channel_id=2, replica_groups=mesh['exp'=2,'tx'=4,'ty'=4] {'tx'}, dimensions={0}, use_global_device_ids=true | all-gather | bytes 163840 | tf_op jit(solution)/shard_map/all_gather | solution.py:135
  514.5 1.1 gather_fusion
  515.6 33.4 %convolution_multiply_fusion.2 = f32[64,128,128]{2,1,0:T(8,128)} fusion(f32[64,128,128]{2,1,0:T(8,128)} %get-tuple-element.129, f32[64,128]{1,0:T(8,128)S(1)} %bitcast.164, f32[64,128]{1,0:T(8,128)S(1)} %copy-done.5, f32[64,128]{1,0:T(8,128)S(1)} %copy-done.13, f32[]{:T(128)S(6)} %neg.79, f32[]{:T(128)S(6)} %neg.75, f32[64,128]{1,0:T(8,128)S(1)} %copy-done.15, ...), kind=kOutput, calls=%fused_computation.348 | convolution fusion | flops 760217600 | bytes 12730440 | tf_op jit(solution)/shard_map/vmap()/dot_general | solution.py:52
  549.1 24.5 %fusion.424 = (f32[64]{0:T(128)S(1)}, f32[64]{0:T(128)S(1)}, f32[64]{0:T(128)S(1)}, f32[64]{0:T(128)S(1)}, f32[64]{0:T(128)S(1)}, /*index=5*/f32[64]{0:T(128)S(1)}, f32[64]{0:T(128)S(1)}, f32[64]{0:T(128)S(1)}) fusion(f32[128]{0:T(128)S(1)} %copy-done.32, f32[64,128,128]{2,1,0:T(8,128)} %convolution_multiply_fusion.1, ...), kind=kOutput, calls=%fused_computation.661 | convolution fusion | flops 426769920 | bytes 21072456 | tf_op jit(solution)/shard_map/vmap()/dot_general | solution.py:51
  (126 shorter events, 12.7 us)
Async XLA Ops:
  8.6 37.2 %copy-start.18 = (bf16[64,128,1]{1,0,2:T(8,128)(2,1)}, bf16[64,128,1]{1,0,2:T(8,128)(2,1)S(1)}, u32[]{:S(2)}) copy-start(bf16[64,128,1]{1,0,2:T(8,128)(2,1)S(1)} %get-tuple-element.65) | copy-start | bytes 49156
  11.0 36.3 %copy-start.24 = (s32[64]{0:T(128)}, s32[64]{0:T(128)S(1)}, u32[]{:S(2)}) copy-start(s32[64]{0:T(128)S(1)} %fusion.251) | copy-start | bytes 772
  11.7 49.3 %copy-start.16 = (f32[64,128]{1,0:T(8,128)}, f32[64,128]{1,0:T(8,128)S(1)}, u32[]{:S(2)}) copy-start(f32[64,128]{1,0:T(8,128)S(1)} %get-tuple-element.126) | copy-start | bytes 98308
  11.7 60.8 %copy-start.14 = (f32[64,128]{1,0:T(8,128)}, f32[64,128]{1,0:T(8,128)S(1)}, u32[]{:S(2)}) copy-start(f32[64,128]{1,0:T(8,128)S(1)} %get-tuple-element.128) | copy-start | bytes 98308
  23.1 22.8 %copy-start.6 = (f32[64,128]{1,0:T(8,128)}, f32[64,128]{1,0:T(8,128)S(1)}, u32[]{:S(2)}) copy-start(f32[64,128]{1,0:T(8,128)S(1)} %convert_reduce_fusion.2) | copy-start | bytes 98308
  34.4 11.4 %copy-start.4 = (f32[64,128]{1,0:T(8,128)}, f32[64,128]{1,0:T(8,128)S(1)}, u32[]{:S(2)}) copy-start(f32[64,128]{1,0:T(8,128)S(1)} %convert_reduce_fusion.3) | copy-start | bytes 98308
  34.4 11.4 %copy-start.29 = (f32[1,64]{1,0:T(1,128)S(1)}, f32[1,64]{1,0:T(1,128)}, u32[]{:S(2)}) copy-start(f32[1,64]{1,0:T(1,128)} %param.14) | copy-start | bytes 772
  34.4 26.6 %copy-start.31 = (bf16[1,64,128,128]{3,2,1,0:T(8,128)(2,1)S(1)}, bf16[1,64,128,128]{3,2,1,0:T(8,128)(2,1)}, u32[]{:S(2)}) copy-start(bf16[1,64,128,128]{3,2,1,0:T(8,128)(2,1)} %param.10) | copy-start | bytes 6291460
  45.8 0.8 copy-start.10
  54.7 62.3 %all-to-all-start.3 = ((bf16[128,2,128]{2,1,0:T(2,128)(2,1)}), bf16[128,2,128]{2,1,0:T(2,128)(2,1)}, u32[]{:S(2)}, u32[]{:S(2)}) async-start(bf16[128,2,128]{2,1,0:T(2,128)(2,1)} %scatter_fusion.3), calls=%async_computation.3 | async-start | bytes 131072 | tf_op jit(solution)/shard_map/all_to_all | solution.py:120
  72.5 12.2 %copy-start.33 = (bf16[64,128,128]{2,1,0:T(8,128)(2,1)}, bf16[64,128,128]{2,1,0:T(8,128)(2,1)S(1)}, u32[]{:S(2)}) copy-start(bf16[64,128,128]{2,1,0:T(8,128)(2,1)S(1)} %fusion.201) | copy-start | bytes 6291460
  84.7 12.3 %copy-start.12 = (f32[64,128]{1,0:T(8,128)S(1)}, f32[64,128]{1,0:T(8,128)}, u32[]{:S(2)}) copy-start(f32[64,128]{1,0:T(8,128)} %get-tuple-element.125) | copy-start | bytes 98308
  84.7 12.3 %copy-start.19 = (bf16[64,128,1]{1,0,2:T(8,128)(2,1)S(1)}, bf16[64,128,1]{1,0,2:T(8,128)(2,1)}, u32[]{:S(2)}) copy-start(bf16[64,128,1]{1,0,2:T(8,128)(2,1)} %copy-done.18) | copy-start | bytes 49156
  97.0 11.4 %copy-start.3 = (bf16[1,64,128]{2,1,0:T(8,128)(2,1)S(1)}, bf16[1,64,128]{2,1,0:T(8,128)(2,1)}, u32[]{:S(2)}) copy-start(bf16[1,64,128]{2,1,0:T(8,128)(2,1)} %get-tuple-element.121) | copy-start | bytes 49156
  97.0 12.6 %copy-start.25 = (s32[64]{0:T(128)S(1)}, s32[64]{0:T(128)}, u32[]{:S(2)}) copy-start(s32[64]{0:T(128)} %copy-done.24) | copy-start | bytes 772
  97.0 25.4 %copy-start.30 = (f32[1,64]{1,0:T(1,128)S(1)}, f32[1,64]{1,0:T(1,128)}, u32[]{:S(2)}) copy-start(f32[1,64]{1,0:T(1,128)} %param.14) | copy-start | bytes 772
  108.4 0.6 copy-start.8
  117.0 32.0 %all-to-all-start.1 = ((bf16[128,2,128]{2,1,0:T(2,128)(2,1)}), bf16[128,2,128]{2,1,0:T(2,128)(2,1)S(1)}, u32[]{:S(2)}, u32[]{:S(2)}) async-start(bf16[128,2,128]{2,1,0:T(2,128)(2,1)} %scatter_fusion.1), calls=%async_computation.1 | async-start | bytes 131072 | tf_op jit(solution)/shard_map/all_to_all | solution.py:120
  148.9 97.6 %all-to-all-start.2 = ((bf16[128,128,128]{2,1,0:T(8,128)(2,1)}), bf16[128,128,128]{2,1,0:T(8,128)(2,1)}, u32[]{:S(2)}, u32[]{:S(2)}) async-start(bf16[128,128,128]{2,1,0:T(8,128)(2,1)} %scatter_fusion.2), calls=%async_computation.2 | async-start | bytes 8388608 | tf_op jit(solution)/shard_map/all_to_all | solution.py:119
  165.6 85.8 %copy-start.27 = (s32[1,64,1]{1,2,0:T(1,128)S(1)}, s32[1,64,1]{1,2,0:T(1,128)}, u32[]{:S(2)}) copy-start(s32[1,64,1]{1,2,0:T(1,128)} %param.11) | copy-start | bytes 772
  165.6 85.9 %copy-start.28 = (f32[2,2,9]{2,1,0:T(2,128)S(1)}, f32[2,2,9]{2,1,0:T(2,128)}, u32[]{:S(2)}) copy-start(f32[2,2,9]{2,1,0:T(2,128)} %param.15) | copy-start | bytes 436
  246.5 97.6 %all-to-all-start = ((bf16[128,128,128]{2,1,0:T(8,128)(2,1)}), bf16[128,128,128]{2,1,0:T(8,128)(2,1)}, u32[]{:S(2)}, u32[]{:S(2)}) async-start(bf16[128,128,128]{2,1,0:T(8,128)(2,1)} %scatter_fusion), calls=%async_computation | async-start | bytes 8388608 | tf_op jit(solution)/shard_map/all_to_all | solution.py:119
  251.4 119.0 %all-reduce.3.cloned.1.call-start = ((), (), s32[]{:S(2)}) async-start(), calls=%async_computation.4 | async-start | bytes 524288 | tf_op jit(solution)/shard_map/psum | solution.py:131
  251.5 167.5 %copy-start.26 = (s32[1024]{0:T(1024)}, s32[1024]{0:T(1024)S(1)}, u32[]{:S(2)}) copy-start(s32[1024]{0:T(1024)S(1)} %pad_clamp_fusion) | copy-start | bytes 12292
  347.5 72.4 %copy-start.7 = (f32[64,128]{1,0:T(8,128)S(1)}, f32[64,128]{1,0:T(8,128)}, u32[]{:S(2)}) copy-start(f32[64,128]{1,0:T(8,128)} %copy-done.6) | copy-start | bytes 98308
  347.5 72.4 %copy-start.11 = (f32[64,1,128]{2,1,0:T(1,128)S(1)}, f32[64,1,128]{2,1,0:T(1,128)}, u32[]{:S(2)}) copy-start(f32[64,1,128]{2,1,0:T(1,128)} %copy-done.10) | copy-start | bytes 98308
  347.5 72.4 %copy-start.17 = (f32[64,128]{1,0:T(8,128)S(1)}, f32[64,128]{1,0:T(8,128)}, u32[]{:S(2)}) copy-start(f32[64,128]{1,0:T(8,128)} %copy-done.16) | copy-start | bytes 98308
  371.4 20.9 %copy-start = (f32[128,128]{1,0:T(8,128)}, f32[128,128]{1,0:T(8,128)S(1)}, u32[]{:S(2)}) copy-start(f32[128,128]{1,0:T(8,128)S(1)} %get-tuple-element.47) | copy-start | bytes 196612
  371.4 20.9 %copy-start.1 = (f32[128,128]{1,0:T(8,128)}, f32[128,128]{1,0:T(8,128)S(1)}, u32[]{:S(2)}) copy-start(f32[128,128]{1,0:T(8,128)S(1)} %get-tuple-element.48) | copy-start | bytes 196612
  371.4 10.6 %collective-permute-start.4 = (f32[4,128]{1,0:T(4,128)S(1)}, f32[4,128]{1,0:T(4,128)S(1)}, u32[]{:S(2)}, u32[]{:S(2)}) collective-permute-start(f32[4,128]{1,0:T(4,128)S(1)} %get-tuple-element.55), channel_id=1, source_target_pairs={{0,4},{4,8},{8,12},{1,5},{5,9},{9,13},{2,6},{6,10},{10,14},{3,7},{... | collective-permute-start | bytes 6152 | tf_op jit(solution)/shard_map/ppermute | solution.py:18
  374.8 7.2 %collective-permute-start.5 = (f32[4,128]{1,0:T(4,128)S(1)}, f32[4,128]{1,0:T(4,128)S(1)}, u32[]{:S(2)}, u32[]{:S(2)}) collective-permute-start(f32[4,128]{1,0:T(4,128)S(1)} %get-tuple-element.56), channel_id=1, source_target_pairs={{4,0},{8,4},{12,8},{5,1},{9,5},{13,9},{6,2},{10,6},{14,10},{7,3},{... | collective-permute-start | bytes 6152 | tf_op jit(solution)/shard_map/ppermute | solution.py:20
  376.1 8.6 %collective-permute-start = (f32[4,128]{1,0:T(4,128)S(1)}, f32[4,128]{1,0:T(4,128)S(1)}, u32[]{:S(2)}, u32[]{:S(2)}) collective-permute-start(f32[4,128]{1,0:T(4,128)S(1)} %get-tuple-element.53), channel_id=1, source_target_pairs={{0,4},{4,8},{8,12},{1,5},{5,9},{9,13},{2,6},{6,10},{10,14},{3,7},{... | collective-permute-start | bytes 6152 | tf_op jit(solution)/shard_map/ppermute | solution.py:18
  380.7 5.5 collective-permute-start.1
  382.1 10.0 %collective-permute-start.6 = (f32[136,4]{1,0:T(8,128)S(1)}, f32[136,4]{1,0:T(8,128)S(1)}, u32[]{:S(2)}, u32[]{:S(2)}) collective-permute-start(f32[136,4]{1,0:T(8,128)S(1)} %get-tuple-element.51), channel_id=1, source_target_pairs={{0,1},{1,2},{2,3},{4,5},{5,6},{6,7},{8,9},{9,10},{10,11},{12,13},{... | collective-permute-start | bytes 6536 | tf_op jit(solution)/shard_map/ppermute | solution.py:18
  383.4 8.7 %collective-permute-start.7 = (f32[136,4]{1,0:T(8,128)S(1)}, f32[136,4]{1,0:T(8,128)S(1)}, u32[]{:S(2)}, u32[]{:S(2)}) collective-permute-start(f32[136,4]{1,0:T(8,128)S(1)} %get-tuple-element.52), channel_id=1, source_target_pairs={{1,0},{2,1},{3,2},{5,4},{6,5},{7,6},{9,8},{10,9},{11,10},{13,12},{... | collective-permute-start | bytes 6536 | tf_op jit(solution)/shard_map/ppermute | solution.py:20
  384.7 7.6 %copy-start.20 = (f32[4,128]{1,0:T(4,128)}, f32[4,128]{1,0:T(4,128)S(1)}, u32[]{:S(2)}) copy-start(f32[4,128]{1,0:T(4,128)S(1)} %collective-permute-done) | copy-start | bytes 6148
  386.2 6.1 %copy-start.22 = (f32[4,128]{1,0:T(4,128)}, f32[4,128]{1,0:T(4,128)S(1)}, u32[]{:S(2)}) copy-start(f32[4,128]{1,0:T(4,128)S(1)} %collective-permute-done.1) | copy-start | bytes 6148
  386.9 101.6 %collective-permute-start.2 = (f32[136,4]{1,0:T(8,128)}, f32[136,4]{1,0:T(8,128)}, u32[]{:S(2)}, u32[]{:S(2)}) collective-permute-start(f32[136,4]{1,0:T(8,128)} %get-tuple-element.49), channel_id=1, source_target_pairs={{0,1},{1,2},{2,3},{4,5},{5,6},{6,7},{8,9},{9,10},{10,11},{12,13},{... | collective-permute-start | bytes 6536 | tf_op jit(solution)/shard_map/ppermute | solution.py:18
  390.8 97.7 %collective-permute-start.3 = (f32[136,4]{1,0:T(8,128)}, f32[136,4]{1,0:T(8,128)}, u32[]{:S(2)}, u32[]{:S(2)}) collective-permute-start(f32[136,4]{1,0:T(8,128)} %get-tuple-element.50), channel_id=1, source_target_pairs={{1,0},{2,1},{3,2},{5,4},{6,5},{7,6},{9,8},{10,9},{11,10},{13,12},{... | collective-permute-start | bytes 6536 | tf_op jit(solution)/shard_map/ppermute | solution.py:20
  466.4 22.1 %copy-start.2 = (f32[128,128]{1,0:T(8,128)S(1)}, f32[128,128]{1,0:T(8,128)}, u32[]{:S(2)}) copy-start(f32[128,128]{1,0:T(8,128)} %copy-done.1) | copy-start | bytes 196612
  466.4 22.1 %copy-start.21 = (f32[4,128]{1,0:T(4,128)S(1)}, f32[4,128]{1,0:T(4,128)}, u32[]{:S(2)}) copy-start(f32[4,128]{1,0:T(4,128)} %copy-done.20) | copy-start | bytes 6148
  466.4 22.1 %copy-start.23 = (f32[4,128]{1,0:T(4,128)S(1)}, f32[4,128]{1,0:T(4,128)}, u32[]{:S(2)}) copy-start(f32[4,128]{1,0:T(4,128)} %copy-done.22) | copy-start | bytes 6148
  488.5 27.1 %copy-start.5 = (f32[64,128]{1,0:T(8,128)S(1)}, f32[64,128]{1,0:T(8,128)}, u32[]{:S(2)}) copy-start(f32[64,128]{1,0:T(8,128)} %copy-done.4) | copy-start | bytes 98308
  488.5 27.1 %copy-start.9 = (f32[64,1,128]{2,1,0:T(1,128)S(1)}, f32[64,1,128]{2,1,0:T(1,128)}, u32[]{:S(2)}) copy-start(f32[64,1,128]{2,1,0:T(1,128)} %copy-done.8) | copy-start | bytes 98308
  488.5 27.1 %copy-start.13 = (f32[64,128]{1,0:T(8,128)S(1)}, f32[64,128]{1,0:T(8,128)}, u32[]{:S(2)}) copy-start(f32[64,128]{1,0:T(8,128)} %get-tuple-element.125) | copy-start | bytes 98308
  488.5 27.1 %copy-start.15 = (f32[64,128]{1,0:T(8,128)S(1)}, f32[64,128]{1,0:T(8,128)}, u32[]{:S(2)}) copy-start(f32[64,128]{1,0:T(8,128)} %copy-done.14) | copy-start | bytes 98308
  515.6 33.5 %copy-start.32 = (f32[128]{0:T(128)S(1)}, f32[128]{0:T(128)}, u32[]{:S(2)}) copy-start(f32[128]{0:T(128)} %broadcast_multiply_fusion) | copy-start | bytes 1540
Sparse Core Ops, SparseCore 0:
  347.7 22.7 all-reduce.2
where the time goes:
time: 592 us; the launch traced here: 581 us
  matrix products  201 us (34%)
  waiting for transfers between devices  189 us (32%)
  other arithmetic  62.7 us (11%)
  local copies, waits for them, and re-layouts  45.5 us (8%)
  starting transfers between devices  40.2 us (7%)
  blocking collectives  28.3 us (5%)
  between operations  14.9 us (3%)
    all_to_all x2, waiting for transfers between devices, local(): lax.all_to_all(block_slots, 'tx', split_axis=0, concat_axis=0, tiled=True)  165 us
    dot_general x2, matrix products, warp_block(): slope_y = jnp.dot(row_slope, col_pass, preferred_element_type=jnp.float32)  79.9 us
    dot_general x2, matrix products, warp_block(): slope_x = jnp.dot(row_pass, col_slope.T, preferred_element_type=jnp.float32)  46.5 us
    all_gather x2, blocking collectives, local(): column_tiles = lax.all_gather(model_tile[None], 'tx', axis=0, tiled=True)  28.3 us
    dot_general x2, matrix products, warp_block(): warped = jnp.dot(row_pass, col_band.T, preferred_element_type=jnp.float32)  25.9 us
    dot_general x2, matrix products, warp_block(): jnp.dot(row_band, masked, preferred_element_type=jnp.float32)  23.7 us
    dot_general x2, matrix products, warp_block(): cols_sum = jnp.dot(col_band, mask_row, preferred_element_type=jnp.float32)  22.7 us
    reduce_sum x2, other arithmetic, warp_block(): rows_sum = jnp.sum(row_band.astype(jnp.float32), axis=1)  22.7 us
  transfers between devices with their start and end apart: 13, of which 4 were waited for; matrix products, arithmetic and copies ran while one was open for 32% of the time, Pallas kernels for 0%

commit v1 on v0

v1 whole, which is shorter than its diff:
```python
import functools

import jax
import jax.numpy as jnp
import numpy as np
from jax import lax
from jax.experimental import pallas as pl
from jax.experimental.pallas import tpu as pltpu
from jax.sharding import PartitionSpec as P

RAD = 4
TAPS = 2 * RAD + 1
DEGREE = 10
F32 = jnp.float32
BF16 = jnp.bfloat16
VMEM_BYTES = 40 * 1024 * 1024


def series():
    count = 64
    nodes = np.cos(np.pi * (np.arange(count) + 0.5) / count)
    table = np.zeros((2, DEGREE + 1, 8), np.float64)
    for row in range(1, 7):
        d = nodes * 0.5 + 0.5 - (row - 3)
        a, b = np.sinc(d), np.sinc(d / 3.0)
        da = (np.cos(np.pi * d) - a) / d
        db = (np.cos(np.pi * d / 3.0) - b) / d
        for which, values in enumerate((a * b, da * b + a * db)):
            fit = np.polynomial.chebyshev.Chebyshev.fit(nodes * 0.5, values, DEGREE, domain=[-0.5, 0.5])
            table[which, :, row] = fit.convert(kind=np.polynomial.Polynomial).coef
    return np.repeat(table.reshape(2 * (DEGREE + 1), 8, 1), 128, axis=2).astype(np.float32)


def taps_of(shift_code, stretch_code, coef_ref, slopes):
    side = 128
    centre = (side - 1) / 2.0
    lane = lax.broadcasted_iota(jnp.int32, (8, side), 1).astype(F32)
    shift = jnp.full((8, side), shift_code, jnp.int32).astype(F32) * (1.0 / 256.0)
    stretch = jnp.full((8, side), stretch_code, jnp.int32).astype(F32) * (1.0 / 51200.0)
    source = centre + (1.0 + stretch) * (lane - centre) + shift
    whole = jnp.floor(source)
    v = (source - whole) - 0.5
    found = []
    for which in range(2 if slopes else 1):
        base = which * (DEGREE + 1)
        total = coef_ref[base + DEGREE]
        for power in range(DEGREE - 1, -1, -1):
            total = total * v + coef_ref[base + power]
        found.append(total)
    return found, whole.astype(jnp.int32)


def spread(tap_list, whole):
    side = 128
    base = lax.broadcasted_iota(jnp.int32, (8, side), 0) + 3 - whole
    indices = [jnp.clip(base + 8 * v, 0, 7) for v in range(side // 8)]
    return [
        jnp.concatenate([jnp.take_along_axis(taps, index, axis=0) for index in indices], axis=0).astype(BF16)
        for taps in tap_list
    ]


def dot(a, b):
    return jnp.dot(a, b, preferred_element_type=F32)


def dot_t(a, b):
    return lax.dot_general(a, b, (((0,), (0,)), ((), ())), preferred_element_type=F32)


def mask_rows(mask_row):
    side = mask_row.shape[1]
    first = lax.broadcasted_iota(jnp.int32, (16, side), 0) == 0
    return jnp.where(first, jnp.broadcast_to(mask_row, (16, side)), 0.0).astype(BF16)


def sums_kernel(tiles, halves, step_blocks, place_ref, tile_ref, affine_ref, weight_ref, coef_ref, mask_ref, block_ref, *rest):
    outs = rest[: tiles * halves]
    acc, rows_sc, cols_sc, den_sc = rest[tiles * halves :]
    step = pl.program_id(0)
    side = 128

    @pl.when(step == 0)
    def _():
        acc[...] = jnp.zeros_like(acc)
        rows_sc[...] = jnp.zeros_like(rows_sc)

    def body(j, carry):
        b = step * step_blocks + j
        tile = tile_ref[0, b]
        weight = weight_ref[0, b]
        mask_row = mask_ref[pl.ds(b, 1), :].astype(F32)
        masked = block_ref[j] * mask_row.astype(BF16)
        extra = mask_rows(mask_row)
        for k in range(2):
            (tap_y,), whole_y = taps_of(affine_ref[b, 4 * k + 1], affine_ref[b, 4 * k + 3], coef_ref, False)
            (tap_x,), whole_x = taps_of(affine_ref[b, 4 * k], affine_ref[b, 4 * k + 2], coef_ref, False)
            (ly_t,) = spread([tap_y], whole_y)
            (lx_t,) = spread([tap_x], whole_x)
            row_pass = dot_t(ly_t, masked).astype(BF16)
            both = dot(jnp.concatenate([row_pass, extra], axis=0), lx_t)
            sent = (weight * both[:side]).astype(BF16).astype(F32)
            acc[k, tile] = acc[k, tile] + sent
            at = whole_y + lax.broadcasted_iota(jnp.int32, (8, side), 0) - 3
            used = jnp.where((at >= 0) & (at < side), tap_y.astype(BF16).astype(F32), 0.0)
            rows_sum = jnp.sum(used, axis=0, keepdims=True)
            rows_sc[k, tile, pl.ds(b, 1), :] = (weight * rows_sum).astype(BF16).astype(F32)
            cols_sc[k, pl.ds(b, 1), :] = both[side : side + 1].astype(BF16).astype(F32)
        return carry

    lax.fori_loop(0, step_blocks, body, 0)

    @pl.when(step == pl.num_programs(0) - 1)
    def _():
        for k in range(2):
            cols = cols_sc[k]
            cols = jnp.concatenate([jnp.maximum(cols, 0.0), jnp.maximum(-cols, 0.0)], axis=0).astype(BF16)

            def one(t, carry, k=k, cols=cols):
                rows = rows_sc[k, t]
                rows = jnp.concatenate([jnp.maximum(rows, 0.0), jnp.maximum(-rows, 0.0)], axis=0).astype(BF16)
                den_sc[k, t] = dot_t(rows, cols)
                return carry

            lax.fori_loop(0, tiles, one, 0)
        height = side // halves
        for de in range(halves):
            for dz in range(tiles):
                half = lax.rem(place_ref[0] + de, halves)
                tile = lax.rem(place_ref[1] + dz, tiles)
                out = outs[de * tiles + dz]
                rows = pl.ds(pl.multiple_of(half * height, height), height)
                for k in range(2):
                    out[k] = acc[k, tile, rows, :].astype(BF16)
                    out[2 + k] = den_sc[k, tile, rows, :].astype(BF16)


def vmem():
    return pl.BlockSpec(memory_space=pltpu.VMEM)


def smem():
    return pl.BlockSpec(memory_space=pltpu.SMEM)


def tile_sums(place, target, affine, weights, coef, masks, blocks, tiles, halves):
    count, side = blocks.shape[0], blocks.shape[1]
    step_blocks = 8
    height = side // halves
    pieces = tiles * halves
    return pl.pallas_call(
        functools.partial(sums_kernel, tiles, halves, step_blocks),
        grid=(count // step_blocks,),
        out_shape=[jax.ShapeDtypeStruct((4, height, side), BF16)] * pieces,
        in_specs=[
            smem(), smem(), smem(), smem(), vmem(), vmem(),
            pl.BlockSpec((step_blocks, side, side), lambda i: (i, 0, 0)),
        ],
        out_specs=[pl.BlockSpec((4, height, side), lambda i: (0, 0, 0))] * pieces,
        scratch_shapes=[
            pltpu.VMEM((2, tiles, side, side), F32),
            pltpu.VMEM((2, tiles, count, side), F32),
            pltpu.VMEM((2, count, side), F32),
            pltpu.VMEM((2, tiles, side, side), F32),
        ],
        compiler_params=pltpu.CompilerParams(vmem_limit_bytes=VMEM_BYTES),
        cost_estimate=pl.CostEstimate(flops=int(2e9), bytes_accessed=int(3e6), transcendentals=0),
        name="tile_sums",
    )(place, target, affine, weights, coef, masks, blocks)


def moments(product_x, product_y):
    side = product_x.shape[0]
    centre = (side - 1) / 2.0
    sum_x = product_x[side - 8 : side]
    sum_y = product_y[side - 8 : side]
    later = sum_y
    for v in range(side // 8 - 2, -1, -1):
        sum_x = sum_x + product_x[8 * v : 8 * v + 8]
        sum_y = sum_y + product_y[8 * v : 8 * v + 8]
        if v:
            later = later + sum_y
    sub = lax.broadcasted_iota(jnp.int32, (8, side), 0).astype(F32) - centre
    lane = lax.broadcasted_iota(jnp.int32, (1, side), 1).astype(F32) - centre
    tilted_y = 8.0 * later + sub * sum_y
    first = jnp.sum(sum_x, axis=0, keepdims=True)
    second = jnp.sum(sum_y, axis=0, keepdims=True)
    fourth = jnp.sum(tilted_y, axis=0, keepdims=True)
    return [first, second, first * lane * (1.0 / side), fourth * (1.0 / side)]


def slopes_kernel(step_blocks, affine_ref, coef_ref, mask_ref, block_ref, slope_ref, part_ref):
    step = pl.program_id(0)
    side = 128

    def body(j, carry):
        b = step * step_blocks + j
        mask_row = mask_ref[pl.ds(b, 1), :].astype(F32)
        masked = block_ref[j] * mask_row.astype(BF16)
        extra = mask_rows(mask_row)
        with_ones = jnp.concatenate([masked, jnp.ones((side, side), BF16)], axis=1)
        bands = []
        for k in range(2):
            taps_y, whole_y = taps_of(affine_ref[b, 4 * k + 1], affine_ref[b, 4 * k + 3], coef_ref, True)
            taps_x, whole_x = taps_of(affine_ref[b, 4 * k], affine_ref[b, 4 * k + 2], coef_ref, True)
            bands.append(spread(taps_y, whole_y) + spread(taps_x, whole_x))
        col_both = dot(jnp.concatenate([masked, extra], axis=0), jnp.concatenate([bands[0][2], bands[1][2]], axis=1))
        for k in range(2):
            ly_t, dy_t, lx_t, dx_t = bands[k]
            row_both = dot_t(ly_t, with_ones)
            row_pass = row_both[:, :side].astype(BF16)
            rows_sum = row_both[:, side:]
            col_pass = col_both[:side, k * side : (k + 1) * side].astype(BF16)
            cols_sum = col_both[side : side + 1, k * side : (k + 1) * side]
            both = dot(row_pass, jnp.concatenate([lx_t, dx_t], axis=1))
            warped = both[:, :side]
            slope_y = dot_t(dy_t, col_pass)
            weight_map = jnp.maximum(rows_sum * cols_sum, 0.0)
            value_x = weight_map * both[:, side:]
            value_y = weight_map * slope_y
            slope_ref[j, 2 * k] = value_x
            slope_ref[j, 2 * k + 1] = value_y
            for m, row in enumerate(moments(warped * value_x, warped * value_y)):
                part_ref[j, 4 * k + m : 4 * k + m + 1, :] = row
        return carry

    lax.fori_loop(0, step_blocks, body, 0)


def slopes_of(affine, coef, masks, blocks):
    count, side = blocks.shape[0], blocks.shape[1]
    step_blocks = 4
    return pl.pallas_call(
        functools.partial(slopes_kernel, step_blocks),
        grid=(count // step_blocks,),
        out_shape=[
            jax.ShapeDtypeStruct((count, 4, side, side), F32),
            jax.ShapeDtypeStruct((count, 8, side), F32),
        ],
        in_specs=[smem(), vmem(), vmem(), pl.BlockSpec((step_blocks, side, side), lambda i: (i, 0, 0))],
        out_specs=[
            pl.BlockSpec((step_blocks, 4, side, side), lambda i: (i, 0, 0, 0)),
            pl.BlockSpec((step_blocks, 8, side), lambda i: (i, 0, 0)),
        ],
        compiler_params=pltpu.CompilerParams(vmem_limit_bytes=VMEM_BYTES),
        cost_estimate=pl.CostEstimate(flops=int(8e9), bytes_accessed=int(20e6), transcendentals=0),
        name="slopes",
    )(affine, coef, masks, blocks)


def coadd_kernel(count, *refs):
    parts, (piece_ref, first_ref, last_ref) = refs[:count], refs[count:]
    total = parts[0][...].astype(F32)
    for part in parts[1:]:
        total = total + part[...].astype(F32)
    one = total[0] / (1.0 + total[2])
    two = (total[1] + one) / (1.0 + total[3])
    piece_ref[0] = one
    piece_ref[1] = two
    side = one.shape[1]
    flipped = [jnp.transpose(one), jnp.transpose(two)]
    first_ref[...] = jnp.concatenate([f[0:8] for f in flipped], axis=0).astype(BF16)
    last_ref[...] = jnp.concatenate([f[side - 8 : side] for f in flipped], axis=0).astype(BF16)


def coadd_of(parts):
    height, side = parts[0].shape[1:]
    return pl.pallas_call(
        functools.partial(coadd_kernel, len(parts)),
        out_shape=[
            jax.ShapeDtypeStruct((2, height, side), F32),
            jax.ShapeDtypeStruct((16, height), BF16),
            jax.ShapeDtypeStruct((16, height), BF16),
        ],
        name="coadd",
    )(*parts)


def join_kernel(place_ref, own_ref, other_ref, left_own, left_other, right_own, right_other, sky_ref, tile_ref):
    here = place_ref[0] == 0
    side = own_ref.shape[2]
    for k in range(2):
        own, other = own_ref[k], other_ref[k]
        tile = jnp.concatenate([jnp.where(here, own, other), jnp.where(here, other, own)], axis=0)
        sky_ref[k, 0:side, :] = tile.astype(BF16)
        if k == 1:
            tile_ref[...] = tile
        edges = []
        for mine, theirs in ((left_own, left_other), (right_own, right_other)):
            a = mine[8 * k : 8 * k + 8, :].astype(F32)
            c = theirs[8 * k : 8 * k + 8, :].astype(F32)
            edges.append(jnp.concatenate([jnp.where(here, a, c), jnp.where(here, c, a)], axis=1))
        sky_ref[k, side : side + 16, :] = jnp.concatenate(edges, axis=0).astype(BF16)


def join(place, own, other, edges):
    side = own.shape[2]
    return pl.pallas_call(
        join_kernel,
        out_shape=[jax.ShapeDtypeStruct((2, side + 16, side), BF16), jax.ShapeDtypeStruct((side, side), F32)],
        in_specs=[smem()] + [vmem()] * 6,
        out_specs=[vmem(), vmem()],
        name="join",
    )(place, own, other, *edges)


def band_of(values, diagonal):
    total = jnp.zeros(diagonal.shape, F32)
    for q, value in enumerate(values):
        total = jnp.where(diagonal == q, value, total)
    high = total.astype(BF16)
    return jnp.concatenate([high, (total - high.astype(F32)).astype(BF16)], axis=1)


def gradient_kernel(tiles, step_blocks, place_ref, tile_ref, psf_ref, *rest):
    skies = rest[:tiles]
    slope_ref, part_ref, out_ref, smooth, model = rest[tiles:]
    step = pl.program_id(0)
    side = 128

    @pl.when(step == 0)
    def _():
        along = lax.broadcasted_iota(jnp.int32, (side, side), 0)
        across = lax.broadcasted_iota(jnp.int32, (side, side), 1)
        edge = lax.broadcasted_iota(jnp.int32, (16, side), 0)
        edge = jnp.where(edge < 8, edge - 8, edge + side - 8)
        for k in range(2):
            taps = [psf_ref[k, 1, q] for q in range(TAPS)]
            inner = band_of(taps, along - across + RAD)
            outer = band_of(taps, edge - across[:16] + RAD)
            smooth[k, 0:8, :] = jnp.zeros((8, side), F32)
            smooth[k, 8 + tiles * side : 16 + tiles * side, :] = jnp.zeros((8, side), F32)
            for turn in range(tiles):
                tile = lax.rem(place_ref[1] + tiles - turn, tiles)
                both = dot(skies[turn][k, 0:side, :], inner) + dot_t(skies[turn][k, side : side + 16, :], outer)
                smooth[k, pl.ds(pl.multiple_of(8 + tile * side, 8), side), :] = both[:, :side] + both[:, side:]
            chunk = 64

            def rows(c, carry, k=k):
                start = pl.multiple_of(c * chunk, chunk)
                seen = smooth[k, pl.ds(start, chunk + 16), :]
                total = psf_ref[k, 0, 0] * seen[4 : 4 + chunk]
                for p in range(1, TAPS):
                    total = total + psf_ref[k, 0, p] * seen[4 + p : 4 + p + chunk]
                model[k, pl.ds(start, chunk), :] = total.astype(BF16).astype(F32)
                return carry

            lax.fori_loop(0, tiles * side // chunk, rows, 0)

    def body(j, carry):
        b = step * step_blocks + j
        start = pl.multiple_of(tile_ref[0, b] * side, side)
        for k in range(2):
            cutout = model[k, pl.ds(start, side), :]
            rows = moments(cutout * slope_ref[j, 2 * k], cutout * slope_ref[j, 2 * k + 1])
            for m, row in enumerate(rows):
                out_ref[j, 4 * k + m : 4 * k + m + 1, :] = part_ref[j, 4 * k + m : 4 * k + m + 1, :] - row
        return carry

    lax.fori_loop(0, step_blocks, body, 0)


def gradients_of(place, target, psf, skies, slopes, parts):
    count, _, side, _ = slopes.shape
    tiles = len(skies)
    step_blocks = 4
    return pl.pallas_call(
        functools.partial(gradient_kernel, tiles, step_blocks),
        grid=(count // step_blocks,),
        out_shape=jax.ShapeDtypeStruct((count, 8, side), F32),
        in_specs=[smem(), smem(), smem()]
        + [vmem()] * tiles
        + [
            pl.BlockSpec((step_blocks, 4, side, side), lambda i: (i, 0, 0, 0)),
            pl.BlockSpec((step_blocks, 8, side), lambda i: (i, 0, 0)),
        ],
        out_specs=pl.BlockSpec((step_blocks, 8, side), lambda i: (i, 0, 0)),
        scratch_shapes=[
            pltpu.VMEM((2, tiles * side + 16, side), F32),
            pltpu.VMEM((2, tiles * side, side), F32),
        ],
        compiler_params=pltpu.CompilerParams(vmem_limit_bytes=VMEM_BYTES),
        cost_estimate=pl.CostEstimate(flops=int(1e9), bytes_accessed=int(20e6), transcendentals=0),
        name="gradients",
    )(place, target, psf, *skies, slopes, parts)


def to_owners(pieces, tiles, halves):
    got = [pieces[0]]
    for index in range(1, tiles * halves):
        de, dz = divmod(index, tiles)
        perm = [(e * tiles + z, (e + de) % halves * tiles + (z + dz) % tiles) for e in range(halves) for z in range(tiles)]
        got.append(lax.ppermute(pieces[index], ("exp", "tx"), perm))
    return got


def sides_of(first, last, halves, columns):
    found = []
    for cells, turn in ((last, 1), (first, -1)):
        for flip in range(halves):
            perm = [
                (e * columns + y, (e + flip) % halves * columns + y + turn)
                for e in range(halves)
                for y in range(columns)
                if 0 <= y + turn < columns
            ]
            found.append(lax.ppermute(cells, ("exp", "ty"), perm))
    return found


def local(exposures, block_tile, affine, col_mask, block_weight, psf):
    blocks = exposures[0]
    count, side = blocks.shape[0], blocks.shape[1]
    tiles, halves, columns = lax.axis_size("tx"), lax.axis_size("exp"), lax.axis_size("ty")
    coef = jnp.asarray(series())
    place = jnp.stack([lax.axis_index("exp"), lax.axis_index("tx")]).astype(jnp.int32)
    target = block_tile.reshape(1, count)
    terms = affine.reshape(count, 8)
    masks = col_mask[0]
    small = halves == 2 and tiles <= 4
    pieces = tile_sums(place, target, terms, block_weight, coef, masks, blocks, tiles, halves if small else 1)
    if small:
        got = to_owners(pieces, tiles, halves)
        slopes, parts = slopes_of(terms, coef, masks, blocks)
        piece, first, last = coadd_of(got)
        other = lax.ppermute(piece, "exp", [(0, 1), (1, 0)])
        edges = sides_of(first, last, halves, columns)
        sky, coadd_tile = join(place, piece, other, edges)
        skies = [sky] + [
            lax.ppermute(sky, "tx", [(z, (z + dz) % tiles) for z in range(tiles)]) for dz in range(1, tiles)
        ]
    else:
        zero = jnp.zeros((), jnp.int32)
        me = lax.axis_index("tx")
        order = (jnp.arange(tiles, dtype=jnp.int32) - me) % tiles
        summed = lax.psum_scatter(jnp.take(jnp.stack(pieces), order, axis=0).astype(F32), "tx", scatter_dimension=0, tiled=True)
        summed = lax.psum(summed[0], "exp")
        one = summed[0] / (1.0 + summed[2])
        coadd_tile = (summed[1] + one) / (1.0 + summed[3])
        both = jnp.stack([one, coadd_tile])
        flipped = jnp.swapaxes(both, 1, 2).astype(BF16)
        left = lax.ppermute(flipped[:, side - 8 :], "ty", [(y, y + 1) for y in range(columns - 1)])
        right = lax.ppermute(flipped[:, :8], "ty", [(y + 1, y) for y in range(columns - 1)])
        sky = jnp.concatenate([both.astype(BF16), left, right], axis=1)
        gathered = lax.all_gather(sky, "tx", axis=0)
        slopes, parts = slopes_of(terms, coef, masks, blocks)
        skies = [lax.dynamic_index_in_dim(gathered, (me + tiles - turn) % tiles, 0, False) for turn in range(tiles)]
    rows = gradients_of(place, target, psf, skies, slopes, parts)
    gradients = (jnp.sum(rows, axis=2) / side).reshape(1, count, 2, 4)
    return gradients, coadd_tile


def solution(mesh):
    placed = (
        P("ty", ("exp", "tx"), None, None),
        P("ty", ("exp", "tx"), None),
        P("ty", ("exp", "tx"), None, None),
        P("ty", ("exp", "tx"), None),
        P("ty", ("exp", "tx")),
        P(),
    )
    return jax.shard_map(
        local,
        mesh=mesh,
        in_specs=placed,
        out_specs=(P("ty", ("exp", "tx"), None, None), P("tx", "ty")),
        check_vma=False,
    )
```

time: 592 us -> 135 us (0.23); the launches traced: 581 us -> 133 us
  matrix products: 201 us -> 0 us
  waiting for transfers between devices: 189 us -> 4.93 us
  Pallas kernels: 0 us -> 84.9 us
  other arithmetic: 62.7 us -> 0.82 us
  local copies, waits for them, and re-layouts: 45.5 us -> 11.1 us
  blocking collectives: 28.3 us -> 0 us
  between operations: 14.9 us -> 0.85 us
  starting transfers between devices: 40.2 us -> 30.3 us
    dot_general x14 -> x0, matrix products: 201 us -> none  [the longest x2 79.9 us: warp_block(): slope_y = jnp.dot(row_slope, col_pass, preferred_element_type=jnp.float32)]
    all_to_all x4 -> x0, waiting for transfers between devices: 165 us -> none  [the longest x2 165 us: local(): lax.all_to_all(block_slots, 'tx', split_axis=0, concat_axis=0, tiled=True)]
    pallas_call x0 -> x5, Pallas kernels: none -> 84.9 us  [the longest x1 38.8 us: slopes_of(): pl.pallas_call(functools.partial(slopes_kernel, step_blocks), grid=(count...]
    scatter x4 -> x0, local copies, waits for them, and re-layouts: 33.2 us -> none  [the longest x2 18.5 us: local(): block_slots = jnp.zeros((tile_rows * slot_cap, block_side, block_side), j...]
    reduce_sum x5 -> x1, other arithmetic: 30.4 us -> 0.14 us  [local(): gradients = (jnp.sum(rows, axis=2) / side).reshape(1, count, 2, 4)]
    all_gather x2 -> x0, blocking collectives: 28.3 us -> none  [local(): column_tiles = lax.all_gather(model_tile[None], 'tx', axis=0, tiled=True)]
    psum x1 -> x0, waiting for transfers between devices: 22.4 us -> none  [local(): numerator, denominator = lax.psum((numerator, denominator), 'exp')]
    all_to_all x4 -> x0, starting transfers between devices: 21.8 us -> none  [the longest x2 11.8 us: local(): lax.all_to_all(profile_slots, 'tx', split_axis=0, concat_axis=0, tiled=True)]
  transfers between devices with their start and end apart: 13 -> 15, of which waited for: 4 -> 5; matrix products, arithmetic and copies ran while one was open for 32% -> 0% of each run, Pallas kernels for 0% -> 29%
where the time goes in v1:
time: 135 us; the launch traced here: 133 us
  Pallas kernels  84.9 us (63%)
  starting transfers between devices  30.3 us (22%)
  local copies, waits for them, and re-layouts  11.1 us (8%)
  waiting for transfers between devices  4.93 us (4%)
    pallas_call x1, Pallas kernels, slopes_of(): pl.pallas_call(functools.partial(slopes_kernel, step_blocks), grid=(count...  38.8 us
    pallas_call x1, Pallas kernels, tile_sums(): pl.pallas_call(functools.partial(sums_kernel, tiles, halves, step_blocks)...  28.8 us
    ppermute x7, starting transfers between devices, to_owners(): got.append(lax.ppermute(pieces[index], ('exp', 'tx'), perm))  15.4 us
    pallas_call x1, Pallas kernels, gradients_of(): pl.pallas_call(functools.partial(gradient_kernel, tiles, step_blocks), gr...  13.8 us
    unnamed x52, local copies, waits for them, and re-layouts  10.2 us
    ppermute x4, starting transfers between devices, sides_of(): found.append(lax.ppermute(cells, ('exp', 'ty'), perm))  8.62 us
    ppermute x3, starting transfers between devices, local(): lax.ppermute(sky, 'tx', [(z, (z + dz) % tiles) for z in range(tiles)])  5.45 us
    ppermute x4, waiting for transfers between devices, sides_of(): found.append(lax.ppermute(cells, ('exp', 'ty'), perm))  3.03 us
  transfers between devices with their start and end apart: 15, of which 5 were waited for; matrix products, arithmetic and copies ran while one was open for 0% of the time, Pallas kernels for 29%

profile of v1, /device:TPU:0, one launch (start us, length us, event | category | flops | bytes accessed | tf_op | source)
XLA Modules:
  0.0 132.9 jit_solution(6885782714040267721)
XLA Ops:
  0.6 0.8 copy.18.affine_ref
  1.4 0.1 pad_add_fusion.place_ref
  1.5 0.7 copy-done.5
  2.1 1.6 %copy-done.7 = bf16[1,64,128,128]{3,2,1,0:T(8,128)(2,1)S(1)} copy-done((bf16[1,64,128,128]{3,2,1,0:T(8,128)(2,1)S(1)}, bf16[1,64,128,128]{3,2,1,0:T(8,128)(2,1)}, u32[]{:S(2)}) %copy-start.7) | copy-done | bytes 2097176
  3.7 0.8 copy-done.9
  4.5 0.7 copy-done.11
  5.1 0.9 copy-done.12
  6.0 28.8 %tile_sums.1 = (bf16[4,64,128]{2,1,0:T(8,128)(2,1)S(1)}, bf16[4,64,128]{2,1,0:T(8,128)(2,1)S(1)}, bf16[4,64,128]{2,1,0:T(8,128)(2,1)S(1)}, bf16[4,64,128]{2,1,0:...) custom-call(s32[2]{0:T(128)S(1)} %pad_add_fusion.place_ref, ...), custom_call_target="tpu_custom_call" | custom-call | flops 2000000000 | bytes 3000000 | tf_op jit(solution)/shard_map/tile_sums/pallas_call | solution.py:151
  34.8 0.0 copy-start.1
  34.8 0.6 copy-done.1
  35.5 3.0 %collective-permute-start = (bf16[4,64,128]{2,1,0:T(8,128)(2,1)S(1)}, bf16[4,64,128]{2,1,0:T(8,128)(2,1)S(1)}, u32[]{:S(2)}, u32[]{:S(2)}) collective-permute-start(bf16[4,64,128]{2,1,0:T(8,128)(2,1)S(1)} %get-tuple-element.18), channel_id=1, source_target_pairs={{0,4},{4,8},{8,12},{12,0},{16,20},{20,24},{24,28},{28,16},{1,5},{5... | collective-permute-start | bytes 196616 | tf_op jit(solution)/shard_map/ppermute | solution.py:393
  38.5 2.6 %collective-permute-start.1 = (bf16[4,64,128]{2,1,0:T(8,128)(2,1)S(1)}, bf16[4,64,128]{2,1,0:T(8,128)(2,1)S(1)}, u32[]{:S(2)}, u32[]{:S(2)}) collective-permute-start(bf16[4,64,128]{2,1,0:T(8,128)(2,1)S(1)} %get-tuple-element.19), channel_id=1, source_target_pairs={{0,8},{4,12},{8,0},{12,4},{16,24},{20,28},{24,16},{28,20},{1,9},{5... | collective-permute-start | bytes 196616 | tf_op jit(solution)/shard_map/ppermute | solution.py:393
  41.1 1.3 %collective-permute-start.2 = (bf16[4,64,128]{2,1,0:T(8,128)(2,1)S(1)}, bf16[4,64,128]{2,1,0:T(8,128)(2,1)S(1)}, u32[]{:S(2)}, u32[]{:S(2)}) collective-permute-start(bf16[4,64,128]{2,1,0:T(8,128)(2,1)S(1)} %get-tuple-element.20), channel_id=1, source_target_pairs={{0,12},{4,0},{8,4},{12,8},{16,28},{20,16},{24,20},{28,24},{1,13},{... | collective-permute-start | bytes 196616 | tf_op jit(solution)/shard_map/ppermute | solution.py:393
  42.4 1.5 %collective-permute-start.3 = (bf16[4,64,128]{2,1,0:T(8,128)(2,1)S(1)}, bf16[4,64,128]{2,1,0:T(8,128)(2,1)S(1)}, u32[]{:S(2)}, u32[]{:S(2)}) collective-permute-start(bf16[4,64,128]{2,1,0:T(8,128)(2,1)S(1)} %get-tuple-element.21), channel_id=1, source_target_pairs={{0,16},{4,20},{8,24},{12,28},{16,0},{20,4},{24,8},{28,12},{1,17},{... | collective-permute-start | bytes 196616 | tf_op jit(solution)/shard_map/ppermute | solution.py:393
  43.9 0.7 collective-permute-start.4
  44.6 0.0 collective-permute-done.refs_1_
  44.6 1.4 %collective-permute-start.5 = (bf16[4,64,128]{2,1,0:T(8,128)(2,1)S(1)}, bf16[4,64,128]{2,1,0:T(8,128)(2,1)S(1)}, u32[]{:S(2)}, u32[]{:S(2)}) collective-permute-start(bf16[4,64,128]{2,1,0:T(8,128)(2,1)S(1)} %get-tuple-element.23), channel_id=1, source_target_pairs={{0,24},{4,28},{8,16},{12,20},{16,8},{20,12},{24,0},{28,4},{1,25},{... | collective-permute-start | bytes 196616 | tf_op jit(solution)/shard_map/ppermute | solution.py:393
  46.0 0.0 collective-permute-done.1.refs_2_
  46.0 4.9 %collective-permute-start.6 = (bf16[4,64,128]{2,1,0:T(8,128)(2,1)S(1)}, bf16[4,64,128]{2,1,0:T(8,128)(2,1)S(1)}, u32[]{:S(2)}, u32[]{:S(2)}) collective-permute-start(bf16[4,64,128]{2,1,0:T(8,128)(2,1)S(1)} %get-tuple-element.24), channel_id=1, source_target_pairs={{0,28},{4,16},{8,20},{12,24},{16,12},{20,0},{24,4},{28,8},{1,29},{... | collective-permute-start | bytes 196616 | tf_op jit(solution)/shard_map/ppermute | solution.py:393
  50.9 0.1 collective-permute-done.4.refs_5_
  51.0 1.4 %collective-permute-done.5.refs_6_ = bf16[4,64,128]{2,1,0:T(8,128)(2,1)S(1)} collective-permute-done((bf16[4,64,128]{2,1,0:T(8,128)(2,1)S(1)}, bf16[4,64,128]{2,1,0:T(8,128)(2,1)S(1)}, u32[]{:S(2)}, u32[]{:S(2)}) %collective-permute-start.5) | collective-permute-done | bytes 65568 | tf_op jit(solution)/shard_map/ppermute | solution.py:393
  52.4 0.4 collective-permute-done.6.refs_7_
  52.8 0.2 copy-done.20
  53.0 0.4 copy-done.21
  53.4 1.8 %coadd.1 = (f32[2,64,128]{2,1,0:T(8,128)}, bf16[16,64]{1,0:T(8,128)(2,1)}, bf16[16,64]{1,0:T(8,128)(2,1)}) custom-call(bf16[4,64,128]{2,1,0:T(8,128)(2,1)} %copy-done.1, bf16[4,64,128]{2,1,0:T(8,128)(2,1)} %copy-done.15, bf16[4,64,128]{2,1,0:T(8,128)(2,1)} %copy-done.16, bf16[4,64,128]{2,1,0:T(8,128)(2,1)} %copy-done.17, bf16[4,64,128]{2,1,0:T(8,128)(2,1)} %copy-done.18, ...), custom_call_target="tpu_custom_call" | custom-call | tf_op jit(solution)/shard_map/coadd/pallas_call | solution.py:268
  55.2 0.9 collective-permute-start.7
  56.1 1.3 collective-permute-start.9
  57.4 4.8 %collective-permute-start.8 = (bf16[16,64]{1,0:T(8,128)(2,1)}, bf16[16,64]{1,0:T(8,128)(2,1)S(1)}, u32[]{:S(2)}, u32[]{:S(2)}) collective-permute-start(bf16[16,64]{1,0:T(8,128)(2,1)} %get-tuple-element.26), channel_id=1, source_target_pairs={{0,1},{1,2},{2,3},{16,17},{17,18},{18,19},{4,5},{5,6},{6,7},{20,21... | collective-permute-start | bytes 6152 | tf_op jit(solution)/shard_map/ppermute | solution.py:407
  62.1 1.3 collective-permute-start.11
  63.4 1.3 collective-permute-start.10
  64.8 0.0 collective-permute-done.8.left_own
  64.8 2.5 %collective-permute-done.11.right_other = bf16[16,64]{1,0:T(8,128)(2,1)S(1)} collective-permute-done((bf16[16,64]{1,0:T(8,128)(2,1)}, bf16[16,64]{1,0:T(8,128)(2,1)S(1)}, u32[]{:S(2)}, u32[]{:S(2)}) %collective-permute-start.11) | collective-permute-done | bytes 2080 | tf_op jit(solution)/shard_map/ppermute | solution.py:407
  67.3 0.5 collective-permute-done.10.right_own
  67.8 0.0 copy-done.24
  67.9 0.5 copy-done.25
  68.4 0.6 copy-done.14
  69.0 1.6 %join.1 = (bf16[2,144,128]{2,1,0:T(8,128)(2,1)}, f32[128,128]{1,0:T(8,128)}) custom-call(s32[2]{0:T(128)} %copy-done.2, f32[2,64,128]{2,1,0:T(8,128)} %get-tuple-element.25.own_ref, f32[2,64,128]{2,1,0:T(8,128)} %copy-done.14, bf16[16,64]{1,0:T(8,128)(2,1)} %copy-done.23, bf16[16,64]{1,0:T(8,128)(2,1)} %copy-done.22, bf16[16,64]{1,0:T(8,128)(2,1)} %copy-done.25, ...), custom_call_target="tpu_custom_call" | custom-call | tf_op jit(solution)/shard_map/join/pallas_call | solution.py:298
  70.6 4.8 %collective-permute-start.14 = (bf16[2,144,128]{2,1,0:T(8,128)(2,1)}, bf16[2,144,128]{2,1,0:T(8,128)(2,1)S(1)}, u32[]{:S(2)}, u32[]{:S(2)}) collective-permute-start(bf16[2,144,128]{2,1,0:T(8,128)(2,1)} %get-tuple-element.28.rest_0_), channel_id=1, source_target_pairs={{0,12},{4,0},{8,4},{12,8},{1,13},{5,1},{9,5},{13,9},{2,14},{6,2},{... | collective-permute-start | bytes 221192 | tf_op jit(solution)/shard_map/ppermute | solution.py:430
  75.4 0.6 collective-permute-start.12
  76.1 1.6 %copy-done.8 = bf16[1,64,128,128]{3,2,1,0:T(8,128)(2,1)S(1)} copy-done((bf16[1,64,128,128]{3,2,1,0:T(8,128)(2,1)S(1)}, bf16[1,64,128,128]{3,2,1,0:T(8,128)(2,1)}, u32[]{:S(2)}) %copy-start.8) | copy-done | bytes 2097176
  77.7 0.8 copy-done.10
  78.4 0.9 copy-done.13
  79.3 38.8 %slopes.1 = (f32[64,4,128,128]{3,2,1,0:T(8,128)}, f32[64,8,128]{2,1,0:T(8,128)S(1)}) custom-call(s32[64,8]{1,0:T(8,128)S(1)} %copy.18.affine_ref, f32[22,8,128]{2,1,0:T(8,128)S(1)} %copy-done.13, s32[64,128]{1,0:T(8,128)S(1)} %bitcast.12, bf16[64,128,128]{2,1,0:T(8,128)(2,1)S(1)} %bitcast.10), custom_call_target="tpu_custom_call" | custom-call | flops 8000000000 | bytes 20000000 | tf_op jit(solution)/shard_map/slopes/pallas_call | solution.py:233
  118.2 0.0 collective-permute-done.13.rest_2_
  118.2 13.8 %gradients.1 = f32[64,8,128]{2,1,0:T(8,128)S(1)} custom-call(s32[2]{0:T(128)S(1)} %copy-done.3, s32[1,64]{1,0:T(1,128)S(1)} %bitcast.8, f32[2,2,9]{2,1,0:T(2,128)S(1)} %copy-done.4, bf16[2,144,128]{2,1,0:T(8,128)(2,1)S(1)} %copy-done, bf16[2,144,128]{2,1,0:T(8,128)(2,1)S(1)} %collective-permute-done.12.rest_1_, ...), custom_call_target="tpu_custom_call" | custom-call | flops 1000000000 | bytes 20000000 | tf_op jit(solution)/shard_map/gradients/pallas_call | solution.py:367
  132.1 0.1 reduce_sum.9
  132.2 0.1 copy.20
  132.3 0.6 broadcast_multiply_fusion
  (44 shorter events, 0.1 us)
Async XLA Ops:
  1.5 66.3 %copy-start.2 = (s32[2]{0:T(128)}, s32[2]{0:T(128)S(1)}, u32[]{:S(2)}) copy-start(s32[2]{0:T(128)S(1)} %pad_add_fusion.place_ref) | copy-start | bytes 28
  1.5 0.7 copy-start.5
  2.1 1.6 %copy-start.7 = (bf16[1,64,128,128]{3,2,1,0:T(8,128)(2,1)S(1)}, bf16[1,64,128,128]{3,2,1,0:T(8,128)(2,1)}, u32[]{:S(2)}) copy-start(bf16[1,64,128,128]{3,2,1,0:T(8,128)(2,1)} %param.7) | copy-start | bytes 6291460
  3.7 0.8 copy-start.9
  4.5 0.7 copy-start.11
  5.1 0.9 copy-start.12
  34.8 0.6 copy-start.1
  35.4 82.7 %copy-start.4 = (f32[2,2,9]{2,1,0:T(2,128)S(1)}, f32[2,2,9]{2,1,0:T(2,128)}, u32[]{:S(2)}) copy-start(f32[2,2,9]{2,1,0:T(2,128)} %psf_ref.1) | copy-start | bytes 436
  35.5 82.7 %copy-start.6 = (s32[1,64,1]{1,2,0:T(1,128)S(1)}, s32[1,64,1]{1,2,0:T(1,128)}, u32[]{:S(2)}) copy-start(s32[1,64,1]{1,2,0:T(1,128)} %param.8) | copy-start | bytes 772
  35.5 9.1 %collective-permute-start = (bf16[4,64,128]{2,1,0:T(8,128)(2,1)S(1)}, bf16[4,64,128]{2,1,0:T(8,128)(2,1)S(1)}, u32[]{:S(2)}, u32[]{:S(2)}) collective-permute-start(bf16[4,64,128]{2,1,0:T(8,128)(2,1)S(1)} %get-tuple-element.18), channel_id=1, source_target_pairs={{0,4},{4,8},{8,12},{12,0},{16,20},{20,24},{24,28},{28,16},{1,5},{5... | collective-permute-start | bytes 196616 | tf_op jit(solution)/shard_map/ppermute | solution.py:393
  38.5 7.5 %collective-permute-start.1 = (bf16[4,64,128]{2,1,0:T(8,128)(2,1)S(1)}, bf16[4,64,128]{2,1,0:T(8,128)(2,1)S(1)}, u32[]{:S(2)}, u32[]{:S(2)}) collective-permute-start(bf16[4,64,128]{2,1,0:T(8,128)(2,1)S(1)} %get-tuple-element.19), channel_id=1, source_target_pairs={{0,8},{4,12},{8,0},{12,4},{16,24},{20,28},{24,16},{28,20},{1,9},{5... | collective-permute-start | bytes 196616 | tf_op jit(solution)/shard_map/ppermute | solution.py:393
  41.1 9.8 %collective-permute-start.2 = (bf16[4,64,128]{2,1,0:T(8,128)(2,1)S(1)}, bf16[4,64,128]{2,1,0:T(8,128)(2,1)S(1)}, u32[]{:S(2)}, u32[]{:S(2)}) collective-permute-start(bf16[4,64,128]{2,1,0:T(8,128)(2,1)S(1)} %get-tuple-element.20), channel_id=1, source_target_pairs={{0,12},{4,0},{8,4},{12,8},{16,28},{20,16},{24,20},{28,24},{1,13},{... | collective-permute-start | bytes 196616 | tf_op jit(solution)/shard_map/ppermute | solution.py:393
  42.4 8.5 %collective-permute-start.3 = (bf16[4,64,128]{2,1,0:T(8,128)(2,1)S(1)}, bf16[4,64,128]{2,1,0:T(8,128)(2,1)S(1)}, u32[]{:S(2)}, u32[]{:S(2)}) collective-permute-start(bf16[4,64,128]{2,1,0:T(8,128)(2,1)S(1)} %get-tuple-element.21), channel_id=1, source_target_pairs={{0,16},{4,20},{8,24},{12,28},{16,0},{20,4},{24,8},{28,12},{1,17},{... | collective-permute-start | bytes 196616 | tf_op jit(solution)/shard_map/ppermute | solution.py:393
  43.9 7.1 %collective-permute-start.4 = (bf16[4,64,128]{2,1,0:T(8,128)(2,1)S(1)}, bf16[4,64,128]{2,1,0:T(8,128)(2,1)S(1)}, u32[]{:S(2)}, u32[]{:S(2)}) collective-permute-start(bf16[4,64,128]{2,1,0:T(8,128)(2,1)S(1)} %get-tuple-element.22), channel_id=1, source_target_pairs={{0,20},{4,24},{8,28},{12,16},{16,4},{20,8},{24,12},{28,0},{1,21},{... | collective-permute-start | bytes 196616 | tf_op jit(solution)/shard_map/ppermute | solution.py:393
  44.6 8.2 %copy-start.15 = (bf16[4,64,128]{2,1,0:T(8,128)(2,1)}, bf16[4,64,128]{2,1,0:T(8,128)(2,1)S(1)}, u32[]{:S(2)}) copy-start(bf16[4,64,128]{2,1,0:T(8,128)(2,1)S(1)} %collective-permute-done.refs_1_) | copy-start | bytes 196612
  44.6 7.8 %collective-permute-start.5 = (bf16[4,64,128]{2,1,0:T(8,128)(2,1)S(1)}, bf16[4,64,128]{2,1,0:T(8,128)(2,1)S(1)}, u32[]{:S(2)}, u32[]{:S(2)}) collective-permute-start(bf16[4,64,128]{2,1,0:T(8,128)(2,1)S(1)} %get-tuple-element.23), channel_id=1, source_target_pairs={{0,24},{4,28},{8,16},{12,20},{16,8},{20,12},{24,0},{28,4},{1,25},{... | collective-permute-start | bytes 196616 | tf_op jit(solution)/shard_map/ppermute | solution.py:393
  46.0 6.8 %copy-start.16 = (bf16[4,64,128]{2,1,0:T(8,128)(2,1)}, bf16[4,64,128]{2,1,0:T(8,128)(2,1)S(1)}, u32[]{:S(2)}) copy-start(bf16[4,64,128]{2,1,0:T(8,128)(2,1)S(1)} %collective-permute-done.1.refs_2_) | copy-start | bytes 196612
  46.0 6.8 %collective-permute-start.6 = (bf16[4,64,128]{2,1,0:T(8,128)(2,1)S(1)}, bf16[4,64,128]{2,1,0:T(8,128)(2,1)S(1)}, u32[]{:S(2)}, u32[]{:S(2)}) collective-permute-start(bf16[4,64,128]{2,1,0:T(8,128)(2,1)S(1)} %get-tuple-element.24), channel_id=1, source_target_pairs={{0,28},{4,16},{8,20},{12,24},{16,12},{20,0},{24,4},{28,8},{1,29},{... | collective-permute-start | bytes 196616 | tf_op jit(solution)/shard_map/ppermute | solution.py:393
  50.9 1.9 %copy-start.17 = (bf16[4,64,128]{2,1,0:T(8,128)(2,1)}, bf16[4,64,128]{2,1,0:T(8,128)(2,1)S(1)}, u32[]{:S(2)}) copy-start(bf16[4,64,128]{2,1,0:T(8,128)(2,1)S(1)} %collective-permute-done.2.refs_3_) | copy-start | bytes 196612
  50.9 1.9 %copy-start.18 = (bf16[4,64,128]{2,1,0:T(8,128)(2,1)}, bf16[4,64,128]{2,1,0:T(8,128)(2,1)S(1)}, u32[]{:S(2)}) copy-start(bf16[4,64,128]{2,1,0:T(8,128)(2,1)S(1)} %collective-permute-done.3.refs_4_) | copy-start | bytes 196612
  51.0 1.8 %copy-start.19 = (bf16[4,64,128]{2,1,0:T(8,128)(2,1)}, bf16[4,64,128]{2,1,0:T(8,128)(2,1)S(1)}, u32[]{:S(2)}) copy-start(bf16[4,64,128]{2,1,0:T(8,128)(2,1)S(1)} %collective-permute-done.4.refs_5_) | copy-start | bytes 196612
  52.4 0.6 copy-start.20
  52.8 0.6 copy-start.21
  55.2 12.6 %collective-permute-start.7 = (f32[2,64,128]{2,1,0:T(8,128)}, f32[2,64,128]{2,1,0:T(8,128)S(1)}, u32[]{:S(2)}, u32[]{:S(2)}) collective-permute-start(f32[2,64,128]{2,1,0:T(8,128)} %get-tuple-element.25.own_ref), channel_id=1, source_target_pairs={{0,16},{16,0},{1,17},{17,1},{2,18},{18,2},{3,19},{19,3},{4,20},{20... | collective-permute-start | bytes 196616 | tf_op jit(solution)/shard_map/ppermute | solution.py:426
  56.1 8.7 %collective-permute-start.9 = (bf16[16,64]{1,0:T(8,128)(2,1)}, bf16[16,64]{1,0:T(8,128)(2,1)S(1)}, u32[]{:S(2)}, u32[]{:S(2)}) collective-permute-start(bf16[16,64]{1,0:T(8,128)(2,1)} %get-tuple-element.26), channel_id=1, source_target_pairs={{0,17},{1,18},{2,19},{16,1},{17,2},{18,3},{4,21},{5,22},{6,23},{20... | collective-permute-start | bytes 6152 | tf_op jit(solution)/shard_map/ppermute | solution.py:407
  57.4 7.4 %collective-permute-start.8 = (bf16[16,64]{1,0:T(8,128)(2,1)}, bf16[16,64]{1,0:T(8,128)(2,1)S(1)}, u32[]{:S(2)}, u32[]{:S(2)}) collective-permute-start(bf16[16,64]{1,0:T(8,128)(2,1)} %get-tuple-element.26), channel_id=1, source_target_pairs={{0,1},{1,2},{2,3},{16,17},{17,18},{18,19},{4,5},{5,6},{6,7},{20,21... | collective-permute-start | bytes 6152 | tf_op jit(solution)/shard_map/ppermute | solution.py:407
  62.1 5.1 %collective-permute-start.11 = (bf16[16,64]{1,0:T(8,128)(2,1)}, bf16[16,64]{1,0:T(8,128)(2,1)S(1)}, u32[]{:S(2)}, u32[]{:S(2)}) collective-permute-start(bf16[16,64]{1,0:T(8,128)(2,1)} %get-tuple-element.27), channel_id=1, source_target_pairs={{1,16},{2,17},{3,18},{17,0},{18,1},{19,2},{5,20},{6,21},{7,22},{21... | collective-permute-start | bytes 6152 | tf_op jit(solution)/shard_map/ppermute | solution.py:407
  63.4 4.4 %collective-permute-start.10 = (bf16[16,64]{1,0:T(8,128)(2,1)}, bf16[16,64]{1,0:T(8,128)(2,1)S(1)}, u32[]{:S(2)}, u32[]{:S(2)}) collective-permute-start(bf16[16,64]{1,0:T(8,128)(2,1)} %get-tuple-element.27), channel_id=1, source_target_pairs={{1,0},{2,1},{3,2},{17,16},{18,17},{19,18},{5,4},{6,5},{7,6},{21,20... | collective-permute-start | bytes 6152 | tf_op jit(solution)/shard_map/ppermute | solution.py:407
  64.7 3.1 %copy-start.22 = (bf16[16,64]{1,0:T(8,128)(2,1)}, bf16[16,64]{1,0:T(8,128)(2,1)S(1)}, u32[]{:S(2)}) copy-start(bf16[16,64]{1,0:T(8,128)(2,1)S(1)} %collective-permute-done.9.left_other) | copy-start | bytes 6148
  64.8 3.1 %copy-start.23 = (bf16[16,64]{1,0:T(8,128)(2,1)}, bf16[16,64]{1,0:T(8,128)(2,1)S(1)}, u32[]{:S(2)}) copy-start(bf16[16,64]{1,0:T(8,128)(2,1)S(1)} %collective-permute-done.8.left_own) | copy-start | bytes 6148
  67.3 0.6 copy-start.24
  67.8 0.6 copy-start.25
  68.4 0.6 copy-start.14
  70.6 47.6 %copy-start = (bf16[2,144,128]{2,1,0:T(8,128)(2,1)S(1)}, bf16[2,144,128]{2,1,0:T(8,128)(2,1)}, u32[]{:S(2)}) copy-start(bf16[2,144,128]{2,1,0:T(8,128)(2,1)} %get-tuple-element.28.rest_0_) | copy-start | bytes 221188
  70.6 47.6 %copy-start.3 = (s32[2]{0:T(128)S(1)}, s32[2]{0:T(128)}, u32[]{:S(2)}) copy-start(s32[2]{0:T(128)} %copy-done.2) | copy-start | bytes 28
  70.6 47.5 %collective-permute-start.14 = (bf16[2,144,128]{2,1,0:T(8,128)(2,1)}, bf16[2,144,128]{2,1,0:T(8,128)(2,1)S(1)}, u32[]{:S(2)}, u32[]{:S(2)}) collective-permute-start(bf16[2,144,128]{2,1,0:T(8,128)(2,1)} %get-tuple-element.28.rest_0_), channel_id=1, source_target_pairs={{0,12},{4,0},{8,4},{12,8},{1,13},{5,1},{9,5},{13,9},{2,14},{6,2},{... | collective-permute-start | bytes 221192 | tf_op jit(solution)/shard_map/ppermute | solution.py:430
  75.4 42.7 %collective-permute-start.13 = (bf16[2,144,128]{2,1,0:T(8,128)(2,1)}, bf16[2,144,128]{2,1,0:T(8,128)(2,1)S(1)}, u32[]{:S(2)}, u32[]{:S(2)}) collective-permute-start(bf16[2,144,128]{2,1,0:T(8,128)(2,1)} %get-tuple-element.28.rest_0_), channel_id=1, source_target_pairs={{0,8},{4,12},{8,0},{12,4},{1,9},{5,13},{9,1},{13,5},{2,10},{6,14},... | collective-permute-start | bytes 221192 | tf_op jit(solution)/shard_map/ppermute | solution.py:430
  75.4 42.7 %collective-permute-start.12 = (bf16[2,144,128]{2,1,0:T(8,128)(2,1)}, bf16[2,144,128]{2,1,0:T(8,128)(2,1)S(1)}, u32[]{:S(2)}, u32[]{:S(2)}) collective-permute-start(bf16[2,144,128]{2,1,0:T(8,128)(2,1)} %get-tuple-element.28.rest_0_), channel_id=1, source_target_pairs={{0,4},{4,8},{8,12},{12,0},{1,5},{5,9},{9,13},{13,1},{2,6},{6,10},{... | collective-permute-start | bytes 221192 | tf_op jit(solution)/shard_map/ppermute | solution.py:430
  76.1 1.6 %copy-start.8 = (bf16[1,64,128,128]{3,2,1,0:T(8,128)(2,1)S(1)}, bf16[1,64,128,128]{3,2,1,0:T(8,128)(2,1)}, u32[]{:S(2)}) copy-start(bf16[1,64,128,128]{3,2,1,0:T(8,128)(2,1)} %param.7) | copy-start | bytes 6291460
  77.7 0.8 copy-start.10
  78.4 0.9 copy-start.13

commit v2 on v1

v2 whole, which is shorter than its diff:
```python
import functools

import jax
import jax.numpy as jnp
import numpy as np
from jax import lax
from jax.experimental import pallas as pl
from jax.experimental.pallas import tpu as pltpu
from jax.sharding import PartitionSpec as P

RAD = 4
TAPS = 2 * RAD + 1
DEGREE = 10
F32 = jnp.float32
BF16 = jnp.bfloat16
GROUP1 = 8
GROUP2 = 4
GROUP3 = 4
CHUNKS = 4
SLOPE = jnp.float32
CODE_TILE, CODE_EXP, CODE_ROW = 8, 9, 10
VMEM_BYTES = 56 * 1024 * 1024


def series():
    count = 64
    nodes = np.cos(np.pi * (np.arange(count) + 0.5) / count)
    table = np.zeros((2, DEGREE + 1, 8), np.float64)
    for row in range(1, 7):
        d = nodes * 0.5 + 0.5 - (row - 3)
        a, b = np.sinc(d), np.sinc(d / 3.0)
        da = (np.cos(np.pi * d) - a) / d
        db = (np.cos(np.pi * d / 3.0) - b) / d
        for which, values in enumerate((a * b, da * b + a * db)):
            fit = np.polynomial.chebyshev.Chebyshev.fit(nodes * 0.5, values, DEGREE, domain=[-0.5, 0.5])
            table[which, :, row] = fit.convert(kind=np.polynomial.Polynomial).coef
    return np.repeat(table.reshape(2 * (DEGREE + 1), 8, 1), 128, axis=2).astype(np.float32)


def taps_of(shift_code, stretch_code, coef_ref, slopes):
    side = 128
    centre = (side - 1) / 2.0
    lane = lax.broadcasted_iota(jnp.int32, (8, side), 1).astype(F32)
    shift = jnp.full((8, side), shift_code, jnp.int32).astype(F32) * (1.0 / 256.0)
    stretch = jnp.full((8, side), stretch_code, jnp.int32).astype(F32) * (1.0 / 51200.0)
    source = centre + (1.0 + stretch) * (lane - centre) + shift
    whole = jnp.floor(source)
    v = (source - whole) - 0.5
    found = []
    for which in range(2 if slopes else 1):
        base = which * (DEGREE + 1)
        total = coef_ref[base + DEGREE]
        for power in range(DEGREE - 1, -1, -1):
            total = total * v + coef_ref[base + power]
        found.append(total)
    return found, whole.astype(jnp.int32)


def pick(taps, index):
    numbers = lax.GatherDimensionNumbers(
        offset_dims=(),
        collapsed_slice_dims=(0,),
        start_index_map=(0,),
        operand_batching_dims=(1,),
        start_indices_batching_dims=(1,),
    )
    mode = lax.GatherScatterMode.PROMISE_IN_BOUNDS
    return lax.gather(taps, index[..., None], numbers, slice_sizes=(1, 1), mode=mode)


def spread(tap_list, whole):
    side = 128
    base = lax.broadcasted_iota(jnp.int32, (8, side), 0) + 3 - whole
    indices = [jnp.clip(base + 8 * v, 0, 7) for v in range(side // 8)]
    return [
        jnp.concatenate([pick(taps, index) for index in indices], axis=0).astype(BF16)
        for taps in tap_list
    ]


def dot(a, b):
    return jnp.dot(a, b, preferred_element_type=F32)


def dot_t(a, b):
    return lax.dot_general(a, b, (((0,), (0,)), ((), ())), preferred_element_type=F32)


def mask_rows(mask_row):
    side = mask_row.shape[1]
    first = lax.broadcasted_iota(jnp.int32, (16, side), 0) == 0
    return jnp.where(first, jnp.broadcast_to(mask_row, (16, side)), 0.0).astype(BF16)


def halves_of(first, second):
    side = first.shape[1]
    left = lax.broadcasted_iota(jnp.int32, first.shape, 1) < side // 2
    low = jnp.where(left, first, pltpu.roll(second, side // 2, 1))
    high = jnp.where(left, pltpu.roll(first, side // 2, 1), second)
    return low, high


def sums_kernel(tiles, packed, step_blocks, code_ref, weight_ref, coef_ref, mask_ref, block_ref, *rest):
    outs = rest[:-4]
    acc, rows_sc, cols_sc, den_sc = rest[-4:]
    step = pl.program_id(0)
    side = 128

    @pl.when(step == 0)
    def _():
        acc[...] = jnp.zeros_like(acc)
        rows_sc[...] = jnp.zeros_like(rows_sc)

    def body(group, carry):
        work = []
        for u in range(GROUP1):
            j = group * GROUP1 + u
            b = step * step_blocks + j
            mask_row = mask_ref[pl.ds(j, 1), :].astype(F32)
            masked = block_ref[j] * mask_row.astype(BF16)
            for k in range(2):
                (tap_y,), whole_y = taps_of(code_ref[b, 4 * k + 1], code_ref[b, 4 * k + 3], coef_ref, False)
                (tap_x,), whole_x = taps_of(code_ref[b, 4 * k], code_ref[b, 4 * k + 2], coef_ref, False)
                work.append([b, k, mask_row, masked, tap_y, whole_y, tap_x, whole_x])
        passes = []
        for b, k, mask_row, masked, tap_y, whole_y, tap_x, whole_x in work:
            (ly_t,) = spread([tap_y], whole_y)
            passes.append(dot_t(ly_t, masked).astype(BF16))
        warps = []
        for (b, k, mask_row, masked, tap_y, whole_y, tap_x, whole_x), row_pass in zip(work, passes):
            (lx_t,) = spread([tap_x], whole_x)
            warps.append(dot(jnp.concatenate([row_pass, mask_rows(mask_row)], axis=0), lx_t))
        for (b, k, mask_row, masked, tap_y, whole_y, tap_x, whole_x), both in zip(work, warps):
            tile = code_ref[b, CODE_TILE]
            weight = weight_ref[0, b]
            sent = (weight * both[:side]).astype(BF16).astype(F32)
            acc[k, tile] = acc[k, tile] + sent
            at = whole_y + lax.broadcasted_iota(jnp.int32, (8, side), 0) - 3
            used = jnp.where((at >= 0) & (at < side), tap_y.astype(BF16).astype(F32), 0.0)
            rows_sum = jnp.sum(used, axis=0, keepdims=True)
            rows_sc[k, tile, pl.ds(b, 1), :] = (weight * rows_sum).astype(BF16).astype(F32)
            cols_sc[k, pl.ds(b, 1), :] = both[side : side + 1].astype(BF16).astype(F32)
        return carry

    lax.fori_loop(0, step_blocks // GROUP1, body, 0)

    @pl.when(step == pl.num_programs(0) - 1)
    def _():
        for k in range(2):
            cols = cols_sc[k]
            cols = jnp.concatenate([jnp.maximum(cols, 0.0), jnp.maximum(-cols, 0.0)], axis=0).astype(BF16)

            def one(t, carry, k=k, cols=cols):
                rows = rows_sc[k, t]
                rows = jnp.concatenate([jnp.maximum(rows, 0.0), jnp.maximum(-rows, 0.0)], axis=0).astype(BF16)
                den_sc[k, t] = dot_t(rows, cols)
                return carry

            lax.fori_loop(0, tiles, one, 0)
        if packed:
            keep_ref, send_ref = outs
            low_end = code_ref[0, CODE_EXP] == 0
            for dz in range(tiles):
                tile = lax.rem(code_ref[0, CODE_ROW] + dz, tiles)
                for which, source in enumerate((acc, den_sc)):
                    low, high = halves_of(source[0, tile], source[1, tile])
                    keep_ref[dz, which] = jnp.where(low_end, low, high)
                    send_ref[dz, which] = jnp.where(low_end, high, low).astype(BF16)
        else:

            def whole(t, carry):
                for k in range(2):
                    outs[0][t, 0, k] = acc[k, t]
                    outs[0][t, 1, k] = den_sc[k, t]
                return carry

            lax.fori_loop(0, tiles, whole, 0)


def vmem():
    return pl.BlockSpec(memory_space=pltpu.VMEM)


def smem():
    return pl.BlockSpec(memory_space=pltpu.SMEM)


def tile_sums(codes, weights, coef, masks, blocks, tiles, packed):
    count, side = blocks.shape[0], blocks.shape[1]
    step_blocks = GROUP1
    if packed:
        shapes = [((tiles, 2, side, side), F32), ((tiles, 2, side, side), BF16)]
    else:
        shapes = [((tiles, 2, 2, side, side), F32)]
    return pl.pallas_call(
        functools.partial(sums_kernel, tiles, packed, step_blocks),
        grid=(count // step_blocks,),
        out_shape=[jax.ShapeDtypeStruct(*shape) for shape in shapes],
        in_specs=[
            smem(),
            smem(),
            pl.BlockSpec(coef.shape, lambda i: (0, 0, 0)),
            pl.BlockSpec((step_blocks, side), lambda i: (i, 0)),
            pl.BlockSpec((step_blocks, side, side), lambda i: (i, 0, 0)),
        ],
        out_specs=[pl.BlockSpec(shape, lambda i, rank=len(shape): (0,) * rank) for shape, _ in shapes],
        scratch_shapes=[
            pltpu.VMEM((2, tiles, side, side), F32),
            pltpu.VMEM((2, tiles, count, side), F32),
            pltpu.VMEM((2, count, side), F32),
            pltpu.VMEM((2, tiles, side, side), F32),
        ],
        compiler_params=pltpu.CompilerParams(vmem_limit_bytes=VMEM_BYTES),
        cost_estimate=pl.CostEstimate(flops=int(8e9), bytes_accessed=int(3e6), transcendentals=0),
        name="tile_sums",
    )(codes, weights, coef, masks, blocks)


def pair_kernel(keep_ref, got_ref, *outs):
    for dz, out in enumerate(outs):
        for which in range(2):
            total = keep_ref[dz, which] + got_ref[dz, which].astype(F32)
            out[which] = total.astype(out.dtype)


def pair(keep, got):
    tiles, _, side, _ = keep.shape
    return pl.pallas_call(
        pair_kernel,
        out_shape=[jax.ShapeDtypeStruct((2, side, side), BF16 if dz else F32) for dz in range(tiles)],
        name="pair",
    )(keep, got)


def moments(product_x, product_y):
    side = product_x.shape[0]
    centre = (side - 1) / 2.0
    sum_x = product_x[side - 8 : side]
    sum_y = product_y[side - 8 : side]
    later = sum_y
    for v in range(side // 8 - 2, -1, -1):
        sum_x = sum_x + product_x[8 * v : 8 * v + 8]
        sum_y = sum_y + product_y[8 * v : 8 * v + 8]
        if v:
            later = later + sum_y
    sub = lax.broadcasted_iota(jnp.int32, (8, side), 0).astype(F32) - centre
    lane = lax.broadcasted_iota(jnp.int32, (1, side), 1).astype(F32) - centre
    tilted_y = 8.0 * later + sub * sum_y
    first = jnp.sum(sum_x, axis=0, keepdims=True)
    second = jnp.sum(sum_y, axis=0, keepdims=True)
    fourth = jnp.sum(tilted_y, axis=0, keepdims=True)
    return [first, second, first * lane * (1.0 / side), fourth * (1.0 / side)]


def slopes_kernel(step_blocks, start, code_ref, coef_ref, mask_ref, block_ref, *rest):
    slope_ref, part_ref = rest[-2:]
    step = pl.program_id(0) + start
    side = 128

    def body(group, carry):
        ones = jnp.ones((side, side), BF16)
        work = []
        for u in range(GROUP2):
            j = group * GROUP2 + u
            b = step * step_blocks + j
            mask_row = mask_ref[pl.ds(j, 1), :].astype(F32)
            masked = block_ref[j] * mask_row.astype(BF16)
            taps = []
            for k in range(2):
                taps.append(taps_of(code_ref[b, 4 * k], code_ref[b, 4 * k + 2], coef_ref, True))
                taps.append(taps_of(code_ref[b, 4 * k + 1], code_ref[b, 4 * k + 3], coef_ref, True))
            work.append([j, masked, mask_rows(mask_row), taps])
        cols, rights, rows, downs = [], [], [], []
        for j, masked, extra, taps in work:
            x0, x1 = spread(*taps[0]), spread(*taps[2])
            cols.append(dot(jnp.concatenate([masked, extra], axis=0), jnp.concatenate([x0[0], x1[0]], axis=1)))
            rights.append([jnp.concatenate(x0, axis=1), jnp.concatenate(x1, axis=1)])
        for j, masked, extra, taps in work:
            with_ones = jnp.concatenate([masked, ones], axis=1)
            y0, y1 = spread(*taps[1]), spread(*taps[3])
            rows.append([dot_t(y0[0], with_ones), dot_t(y1[0], with_ones)])
            downs.append([y0[1], y1[1]])
        late = []
        for (j, masked, extra, taps), col_both, right, row, down in zip(work, cols, rights, rows, downs):
            for k in range(2):
                row_pass = row[k][:, :side].astype(BF16)
                col_pass = col_both[:side, k * side : (k + 1) * side].astype(BF16)
                late.append((j, k, dot(row_pass, right[k]), dot_t(down[k], col_pass), row[k][:, side:], col_both[side : side + 1, k * side : (k + 1) * side]))
        for j, k, both, slope_y, rows_sum, cols_sum in late:
            warped = both[:, :side]
            weight_map = jnp.maximum(rows_sum * cols_sum, 0.0)
            value_x = weight_map * both[:, side:]
            value_y = weight_map * slope_y
            slope_ref[j, 2 * k] = value_x.astype(SLOPE)
            slope_ref[j, 2 * k + 1] = value_y.astype(SLOPE)
            for m, row in enumerate(moments(warped * value_x, warped * value_y)):
                part_ref[j, 4 * k + m : 4 * k + m + 1, :] = row
        return carry

    lax.fori_loop(0, step_blocks // GROUP2, body, 0)


def slopes_of(codes, coef, masks, blocks, first, size, filled):
    count, side = blocks.shape[0], blocks.shape[1]
    step_blocks = 8
    start = first // step_blocks
    return pl.pallas_call(
        functools.partial(slopes_kernel, step_blocks, start),
        grid=(size // step_blocks,),
        out_shape=[
            jax.ShapeDtypeStruct((count, 4, side, side), SLOPE),
            jax.ShapeDtypeStruct((count, 8, side), F32),
        ],
        in_specs=[
            smem(),
            pl.BlockSpec(coef.shape, lambda i: (0, 0, 0)),
            pl.BlockSpec((step_blocks, side), lambda i: (i + start, 0)),
            pl.BlockSpec((step_blocks, side, side), lambda i: (i + start, 0, 0)),
        ]
        + [pl.BlockSpec(memory_space=pl.ANY)] * len(filled),
        out_specs=[
            pl.BlockSpec((step_blocks, 4, side, side), lambda i: (i + start, 0, 0, 0)),
            pl.BlockSpec((step_blocks, 8, side), lambda i: (i + start, 0, 0)),
        ],
        input_output_aliases={4 + n: n for n in range(len(filled))},
        compiler_params=pltpu.CompilerParams(vmem_limit_bytes=VMEM_BYTES),
        cost_estimate=pl.CostEstimate(flops=int(1.5e8) * size, bytes_accessed=int(3e5) * size, transcendentals=0),
        name="slopes",
    )(codes, coef, masks, blocks, *filled)


def coadd_kernel(code_ref, *refs):
    parts, (piece_ref, edge_ref) = refs[:-2], refs[-2:]
    num, den = parts[0][0], parts[0][1]
    for part in parts[1:]:
        num = num + part[0].astype(F32)
        den = den + part[1].astype(F32)
    side = num.shape[1]
    left = lax.broadcasted_iota(jnp.int32, num.shape, 1) < side // 2
    first = num / (1.0 + den)
    piece = (num + jnp.where(left, 0.0, pltpu.roll(first, side // 2, 1))) / (1.0 + den)
    piece_ref[...] = piece
    flipped = jnp.transpose(piece)
    half = side // 2
    outer = jnp.concatenate([flipped[0:8], flipped[half : half + 8]], axis=0)
    inner = jnp.concatenate([flipped[half - 8 : half], flipped[side - 8 : side]], axis=0)
    edge_ref[...] = jnp.where(code_ref[0, CODE_EXP] == 0, outer, inner).astype(BF16)


def coadd_of(codes, parts):
    side = parts[0].shape[2]
    return pl.pallas_call(
        coadd_kernel,
        out_shape=[jax.ShapeDtypeStruct((side, side), F32), jax.ShapeDtypeStruct((16, side), BF16)],
        in_specs=[smem()] + [vmem()] * len(parts),
        out_specs=[vmem(), vmem()],
        name="coadd",
    )(codes, *parts)


def join_kernel(code_ref, own_ref, other_ref, edge_ref, far_ref, sky_ref, tile_ref):
    here = code_ref[0, CODE_EXP] == 0
    side = own_ref.shape[1]
    own, other = own_ref[...], other_ref[...]
    tiles = halves_of(jnp.where(here, own, other), jnp.where(here, other, own))
    edge, far = edge_ref[...].astype(F32), far_ref[...].astype(F32)
    left, right = jnp.where(here, far, edge), jnp.where(here, edge, far)
    for k in range(2):
        sky_ref[k, 0:side, :] = tiles[k].astype(BF16)
        at = slice(8 * k, 8 * k + 8)
        sky_ref[k, side : side + 16, :] = jnp.concatenate([left[at], right[at]], axis=0).astype(BF16)
    tile_ref[...] = tiles[1]


def join(codes, own, other, edge, far):
    side = own.shape[1]
    return pl.pallas_call(
        join_kernel,
        out_shape=[jax.ShapeDtypeStruct((2, side + 16, side), BF16), jax.ShapeDtypeStruct((side, side), F32)],
        in_specs=[smem()] + [vmem()] * 4,
        out_specs=[vmem(), vmem()],
        name="join",
    )(codes, own, other, edge, far)


def band_of(values, diagonal):
    total = jnp.zeros(diagonal.shape, F32)
    for q, value in enumerate(values):
        total = jnp.where(diagonal == q, value, total)
    high = total.astype(BF16)
    return jnp.concatenate([high, (total - high.astype(F32)).astype(BF16)], axis=1)


def gradient_kernel(tiles, step_blocks, code_ref, psf_ref, *rest):
    skies = rest[:tiles]
    slope_ref, part_ref, out_ref, smooth, model = rest[tiles:]
    step = pl.program_id(0)
    side = 128

    @pl.when(step == 0)
    def _():
        along = lax.broadcasted_iota(jnp.int32, (side, side), 0)
        across = lax.broadcasted_iota(jnp.int32, (side, side), 1)
        edge = lax.broadcasted_iota(jnp.int32, (16, side), 0)
        edge = jnp.where(edge < 8, edge - 8, edge + side - 8)
        for k in range(2):
            taps = [psf_ref[k, 1, q] for q in range(TAPS)]
            inner = band_of(taps, along - across + RAD)
            outer = band_of(taps, edge - across[:16] + RAD)
            smooth[k, 0:8, :] = jnp.zeros((8, side), F32)
            smooth[k, 8 + tiles * side : 16 + tiles * side, :] = jnp.zeros((8, side), F32)
            for turn in range(tiles):
                tile = lax.rem(code_ref[0, CODE_ROW] + tiles - turn, tiles)
                both = dot(skies[turn][k, 0:side, :], inner) + dot_t(skies[turn][k, side : side + 16, :], outer)
                smooth[k, pl.ds(pl.multiple_of(8 + tile * side, 8), side), :] = both[:, :side] + both[:, side:]
            chunk = 64

            def rows(c, carry, k=k):
                start = pl.multiple_of(c * chunk, chunk)
                seen = smooth[k, pl.ds(start, chunk + 16), :]
                total = psf_ref[k, 0, 0] * seen[4 : 4 + chunk]
                for p in range(1, TAPS):
                    total = total + psf_ref[k, 0, p] * seen[4 + p : 4 + p + chunk]
                model[k, pl.ds(start, chunk), :] = total.astype(BF16).astype(F32)
                return carry

            lax.fori_loop(0, tiles * side // chunk, rows, 0)

    def body(group, carry):
        found = []
        for u in range(GROUP3):
            j = group * GROUP3 + u
            start = pl.multiple_of(code_ref[step * step_blocks + j, CODE_TILE] * side, side)
            for k in range(2):
                cutout = model[k, pl.ds(start, side), :]
                slope_x, slope_y = slope_ref[j, 2 * k].astype(F32), slope_ref[j, 2 * k + 1].astype(F32)
                found.append((j, k, moments(cutout * slope_x, cutout * slope_y)))
        for j, k, rows in found:
            for m, row in enumerate(rows):
                out_ref[j, 4 * k + m : 4 * k + m + 1, :] = part_ref[j, 4 * k + m : 4 * k + m + 1, :] - row
        return carry

    lax.fori_loop(0, step_blocks // GROUP3, body, 0)


def gradients_of(codes, psf, skies, slopes, parts):
    count, _, side, _ = slopes.shape
    tiles = len(skies)
    step_blocks = 8
    sky_shape = skies[0].shape
    return pl.pallas_call(
        functools.partial(gradient_kernel, tiles, step_blocks),
        grid=(count // step_blocks,),
        out_shape=jax.ShapeDtypeStruct((count, 8, side), F32),
        in_specs=[smem(), smem()]
        + [pl.BlockSpec(sky_shape, lambda i: (0, 0, 0))] * tiles
        + [
            pl.BlockSpec((step_blocks, 4, side, side), lambda i: (i, 0, 0, 0)),
            pl.BlockSpec((step_blocks, 8, side), lambda i: (i, 0, 0)),
        ],
        out_specs=pl.BlockSpec((step_blocks, 8, side), lambda i: (i, 0, 0)),
        scratch_shapes=[
            pltpu.VMEM((2, tiles * side + 16, side), F32),
            pltpu.VMEM((2, tiles * side, side), F32),
        ],
        compiler_params=pltpu.CompilerParams(vmem_limit_bytes=VMEM_BYTES),
        cost_estimate=pl.CostEstimate(flops=int(4e9), bytes_accessed=int(20e6), transcendentals=0),
        name="gradients",
    )(codes, psf, *skies, slopes, parts)


def swap(cells):
    return lax.ppermute(cells, "exp", [(0, 1), (1, 0)])


def turned(cells, dz, tiles):
    return lax.ppermute(cells, "tx", [(z, (z + dz) % tiles) for z in range(tiles)])


def to_sides(edge, columns):
    perm = [(y, y - 1) for y in range(1, columns)] + [(columns + y, columns + y + 1) for y in range(columns - 1)]
    return lax.ppermute(edge, ("exp", "ty"), perm)


def local(exposures, block_tile, affine, col_mask, block_weight, psf):
    blocks = exposures[0]
    count, side = blocks.shape[0], blocks.shape[1]
    tiles, halves, columns = lax.axis_size("tx"), lax.axis_size("exp"), lax.axis_size("ty")
    coef = jnp.asarray(series())
    place = [jnp.full((count, 1), lax.axis_index(axis), jnp.int32) for axis in ("exp", "tx")]
    codes = jnp.concatenate([affine.reshape(count, 8), block_tile[0]] + place, axis=1)
    masks = col_mask[0]
    small = halves == 2 and tiles <= 4
    sums = tile_sums(codes, block_weight, coef, masks, blocks, tiles, small)
    filled = ()
    for chunk in range(CHUNKS):
        size = count // CHUNKS
        filled = slopes_of(codes, coef, masks, blocks, chunk * size, size, filled)
    slopes, parts = filled
    if small:
        keep, send = sums
        totals = pair(keep, swap(send))
        got = [totals[0]] + [turned(totals[dz], dz, tiles) for dz in range(1, tiles)]
        piece, edge = coadd_of(codes, got)
        other = swap(piece)
        edge = to_sides(edge, columns)
        sky, coadd_tile = join(codes, piece, other, edge, swap(edge))
        skies = [sky] + [turned(sky, dz, tiles) for dz in range(1, tiles)]
    else:
        me = lax.axis_index("tx")
        summed = lax.psum_scatter(sums[0], "tx", scatter_dimension=0, tiled=True)
        (num, den) = lax.psum(summed[0], "exp")
        one = num[0] / (1.0 + den[0])
        coadd_tile = (num[1] + one) / (1.0 + den[1])
        both = jnp.stack([one, coadd_tile])
        flipped = jnp.swapaxes(both, 1, 2).astype(BF16)
        left = lax.ppermute(flipped[:, side - 8 :], "ty", [(y, y + 1) for y in range(columns - 1)])
        right = lax.ppermute(flipped[:, :8], "ty", [(y + 1, y) for y in range(columns - 1)])
        sky = jnp.concatenate([both.astype(BF16), left, right], axis=1)
        gathered = lax.all_gather(sky, "tx", axis=0)
        skies = [lax.dynamic_index_in_dim(gathered, (me + tiles - turn) % tiles, 0, False) for turn in range(tiles)]
    rows = gradients_of(codes, psf, skies, slopes, parts)
    gradients = (jnp.sum(rows, axis=2) / side).reshape(1, count, 2, 4)
    return gradients, coadd_tile


def solution(mesh):
    placed = (
        P("ty", ("exp", "tx"), None, None),
        P("ty", ("exp", "tx"), None),
        P("ty", ("exp", "tx"), None, None),
        P("ty", ("exp", "tx"), None),
        P("ty", ("exp", "tx")),
        P(),
    )
    return jax.shard_map(
        local,
        mesh=mesh,
        in_specs=placed,
        out_specs=(P("ty", ("exp", "tx"), None, None), P("tx", "ty")),
        check_vma=False,
    )
```

time: 135 us -> 86.1 us (0.64)
  Pallas kernels: 84.9 us -> 55.1 us
  starting transfers between devices: 30.3 us -> 15.9 us
  local copies, waits for them, and re-layouts: 11.1 us -> 4.08 us
  waiting for transfers between devices: 4.93 us -> 6.6 us
  other arithmetic: 0.82 us -> 2.47 us
    pallas_call x3 -> x7, Pallas kernels: 69.4 us -> 42.2 us  [the longest x4 24.8 us: slopes_of(): pl.pallas_call(functools.partial(slopes_kernel, step_blocks, start), grid...]
    ppermute x15 -> x10, starting transfers between devices: 30.3 us -> 15.9 us  [the longest x6 9.53 us: turned(): lax.ppermute(cells, 'tx', [(z, (z + dz) % tiles) for z in range(tiles)])]
    unnamed x52 -> x22, local copies, waits for them, and re-layouts: 10.2 us -> 3.17 us
    pallas_call x1, Pallas kernels: 13.8 us -> 10.8 us  [gradients_of(): pl.pallas_call(functools.partial(gradient_kernel, tiles, step_blocks), gr...]
    ppermute x15 -> x10, waiting for transfers between devices: 4.93 us -> 6.6 us  [the longest x3 6.58 us: swap(): return lax.ppermute(cells, 'exp', [(0, 1), (1, 0)])]
  transfers between devices with their start and end apart: 15 -> 10, of which waited for: 5 -> 1; matrix products, arithmetic and copies ran while one was open for 0% -> 0% of each run, Pallas kernels for 29% -> 29%
where the time goes in v2:
time: 86.1 us; the launch traced here: 84.9 us
  Pallas kernels  55.1 us (64%)
  starting transfers between devices  15.9 us (18%)
  waiting for transfers between devices  6.6 us (8%)
  local copies, waits for them, and re-layouts  4.08 us (5%)
  other arithmetic  2.47 us (3%)
    pallas_call x4, Pallas kernels, slopes_of(): pl.pallas_call(functools.partial(slopes_kernel, step_blocks, start), grid...  24.8 us
    pallas_call x1, Pallas kernels, tile_sums(): pl.pallas_call(functools.partial(sums_kernel, tiles, packed, step_blocks)...  13.5 us
    pallas_call x1, Pallas kernels, gradients_of(): pl.pallas_call(functools.partial(gradient_kernel, tiles, step_blocks), gr...  10.8 us
    ppermute x6, starting transfers between devices, turned(): lax.ppermute(cells, 'tx', [(z, (z + dz) % tiles) for z in range(tiles)])  9.53 us
    ppermute x3, waiting for transfers between devices, swap(): return lax.ppermute(cells, 'exp', [(0, 1), (1, 0)])  6.58 us
    ppermute x3, starting transfers between devices, swap(): return lax.ppermute(cells, 'exp', [(0, 1), (1, 0)])  4.97 us
    unnamed x22, local copies, waits for them, and re-layouts  3.17 us
    pallas_call x1, Pallas kernels, coadd_of(): pl.pallas_call(coadd_kernel, out_shape=[jax.ShapeDtypeStruct((side, side)...  2.11 us
  transfers between devices with their start and end apart: 10, of which 1 were waited for; matrix products, arithmetic and copies ran while one was open for 0% of the time, Pallas kernels for 29%

profile of v2, /device:TPU:0, one launch (start us, length us, event | category | flops | bytes accessed | tf_op | source)
XLA Modules:
  0.0 84.9 jit_solution(7414726500427744007)
XLA Ops:
  0.6 0.1 pad.2.clone
  0.7 0.1 pad.3.clone
  0.8 0.8 add_add_fusion
  1.6 0.7 copy.44.code_ref
  2.3 13.5 %tile_sums.1 = (f32[4,2,128,128]{3,2,1,0:T(8,128)}, bf16[4,2,128,128]{3,2,1,0:T(8,128)(2,1)}) custom-call(s32[64,11]{1,0:T(8,128)} %copy.44.code_ref, f32[1,64]{1,0:T(1,128)} %weight_ref.1, f32[22,8,128]{2,1,0:T(8,128)} %constant.18.clone.coef_ref, s32[64,128]{1,0:T(8,128)} %bitcast.12, bf16[64,128,128]{2,1,0:T(8,128)(2,1)} %bitcast.7), custom_call_target="tpu_custom_call" | custom-call | flops 8000000000 | bytes 3000000 | tf_op jit(solution)/shard_map/tile_sums/pallas_call | solution.py:195
  15.7 2.9 %collective-permute-start = (bf16[4,2,128,128]{3,2,1,0:T(8,128)(2,1)}, bf16[4,2,128,128]{3,2,1,0:T(8,128)(2,1)S(1)}, u32[]{:S(2)}, u32[]{:S(2)}) collective-permute-start(bf16[4,2,128,128]{3,2,1,0:T(8,128)(2,1)} %get-tuple-element.21), channel_id=1, source_target_pairs={{0,16},{16,0},{1,17},{17,1},{2,18},{18,2},{3,19},{19,3},{4,20},{20... | collective-permute-start | bytes 786440 | tf_op jit(solution)/shard_map/ppermute | solution.py:473
  18.6 6.6 %collective-permute-done.got_ref = bf16[4,2,128,128]{3,2,1,0:T(8,128)(2,1)S(1)} collective-permute-done((bf16[4,2,128,128]{3,2,1,0:T(8,128)(2,1)}, bf16[4,2,128,128]{3,2,1,0:T(8,128)(2,1)S(1)}, u32[]{:S(2)}, u32[]{:S(2)}) %collective-permute-start) | collective-permute-done | bytes 262176 | tf_op jit(solution)/shard_map/ppermute | solution.py:473
  25.2 0.7 copy-done
  25.9 1.8 %pair.1 = (f32[2,128,128]{2,1,0:T(8,128)}, bf16[2,128,128]{2,1,0:T(8,128)(2,1)}, bf16[2,128,128]{2,1,0:T(8,128)(2,1)}, bf16[2,128,128]{2,1,0:T(8,128)(2,1)}) custom-call(f32[4,2,128,128]{3,2,1,0:T(8,128)} %get-tuple-element.20.keep_ref, bf16[4,2,128,128]{3,2,1,0:T(8,128)(2,1)} %copy-done), custom_call_target="tpu_custom_call" | custom-call | tf_op jit(solution)/shard_map/pair/pallas_call | solution.py:228
  27.7 1.8 %collective-permute-start.1 = (bf16[2,128,128]{2,1,0:T(8,128)(2,1)}, bf16[2,128,128]{2,1,0:T(8,128)(2,1)S(1)}, u32[]{:S(2)}, u32[]{:S(2)}) collective-permute-start(bf16[2,128,128]{2,1,0:T(8,128)(2,1)} %get-tuple-element.23), channel_id=1, source_target_pairs={{0,4},{4,8},{8,12},{12,0},{1,5},{5,9},{9,13},{13,1},{2,6},{6,10},{... | collective-permute-start | bytes 196616 | tf_op jit(solution)/shard_map/ppermute | solution.py:477
  29.5 2.6 %collective-permute-start.2 = (bf16[2,128,128]{2,1,0:T(8,128)(2,1)}, bf16[2,128,128]{2,1,0:T(8,128)(2,1)S(1)}, u32[]{:S(2)}, u32[]{:S(2)}) collective-permute-start(bf16[2,128,128]{2,1,0:T(8,128)(2,1)} %get-tuple-element.24), channel_id=1, source_target_pairs={{0,8},{4,12},{8,0},{12,4},{1,9},{5,13},{9,1},{13,5},{2,10},{6,14},... | collective-permute-start | bytes 196616 | tf_op jit(solution)/shard_map/ppermute | solution.py:477
  32.1 1.3 %collective-permute-start.3 = (bf16[2,128,128]{2,1,0:T(8,128)(2,1)}, bf16[2,128,128]{2,1,0:T(8,128)(2,1)S(1)}, u32[]{:S(2)}, u32[]{:S(2)}) collective-permute-start(bf16[2,128,128]{2,1,0:T(8,128)(2,1)} %get-tuple-element.25), channel_id=1, source_target_pairs={{0,12},{4,0},{8,4},{12,8},{1,13},{5,1},{9,5},{13,9},{2,14},{6,2},{... | collective-permute-start | bytes 196616 | tf_op jit(solution)/shard_map/ppermute | solution.py:477
  33.4 6.2 %slopes.4 = (f32[64,4,128,128]{3,2,1,0:T(8,128)}, f32[64,8,128]{2,1,0:T(8,128)}) custom-call(s32[64,11]{1,0:T(8,128)} %copy.44.code_ref, f32[22,8,128]{2,1,0:T(8,128)} %constant.18.clone.coef_ref, s32[64,128]{1,0:T(8,128)} %bitcast.13, bf16[64,128,128]{2,1,0:T(8,128)(2,1)} %bitcast.8), custom_call_target="tpu_custom_call" | custom-call | flops 2400000000 | bytes 4800000 | tf_op jit(solution)/shard_map/slopes/pallas_call | solution.py:307
  39.6 0.0 collective-permute-done.1.refs_1_
  39.6 0.0 collective-permute-done.2.refs_2_
  39.6 0.0 copy-start.7
  39.6 0.0 collective-permute-done.3.refs_3_
  39.6 0.0 copy-start.8
  39.6 0.6 copy-done.6
  40.2 0.0 copy-done.7
  40.2 0.0 copy-done.8
  40.3 2.1 %coadd.1 = (f32[128,128]{1,0:T(8,128)}, bf16[16,128]{1,0:T(8,128)(2,1)}) custom-call(s32[64,11]{1,0:T(8,128)} %copy.44.code_ref, f32[2,128,128]{2,1,0:T(8,128)} %get-tuple-element.22.refs_0_, bf16[2,128,128]{2,1,0:T(8,128)(2,1)} %copy-done.6, bf16[2,128,128]{2,1,0:T(8,128)(2,1)} %copy-done.7, bf16[2,128,128]{2,1,0:T(8,128)(2,1)} %copy-done.8), custom_call_target="tpu_custom_call" | custom-call | tf_op jit(solution)/shard_map/coadd/pallas_call | solution.py:352
  42.4 1.4 %collective-permute-start.5 = (bf16[16,128]{1,0:T(8,128)(2,1)}, bf16[16,128]{1,0:T(8,128)(2,1)S(1)}, u32[]{:S(2)}, u32[]{:S(2)}) collective-permute-start(bf16[16,128]{1,0:T(8,128)(2,1)} %get-tuple-element.27), channel_id=1, source_target_pairs={{1,0},{2,1},{3,2},{16,17},{17,18},{18,19},{5,4},{6,5},{7,6},{20,21... | collective-permute-start | bytes 12296 | tf_op jit(solution)/shard_map/ppermute | solution.py:482
  43.8 6.3 %slopes.5 = (f32[64,4,128,128]{3,2,1,0:T(8,128)}, f32[64,8,128]{2,1,0:T(8,128)}) custom-call(s32[64,11]{1,0:T(8,128)} %copy.44.code_ref, f32[22,8,128]{2,1,0:T(8,128)} %constant.18.clone.coef_ref, s32[64,128]{1,0:T(8,128)} %bitcast.14, bf16[64,128,128]{2,1,0:T(8,128)(2,1)} %bitcast.9, ...), custom_call_target="tpu_custom_call", output_to_operand_aliasing={{0}: (4, {}), {1}: (5, {})} | custom-call | flops 2400000000 | bytes 4800000 | tf_op jit(solution)/shard_map/slopes/pallas_call | solution.py:307
  50.1 1.5 %collective-permute-start.4 = (f32[128,128]{1,0:T(8,128)S(1)}, f32[128,128]{1,0:T(8,128)S(1)}, u32[]{:S(2)}, u32[]{:S(2)}) collective-permute-start(f32[128,128]{1,0:T(8,128)S(1)} %copy-done.4), channel_id=1, source_target_pairs={{0,16},{16,0},{1,17},{17,1},{2,18},{18,2},{3,19},{19,3},{4,20},{20... | collective-permute-start | bytes 196616 | tf_op jit(solution)/shard_map/ppermute | solution.py:473
  51.6 0.0 collective-permute-done.5.edge_ref
  51.6 0.5 collective-permute-start.6
  52.2 6.2 %slopes.6 = (f32[64,4,128,128]{3,2,1,0:T(8,128)}, f32[64,8,128]{2,1,0:T(8,128)}) custom-call(s32[64,11]{1,0:T(8,128)} %copy.44.code_ref, f32[22,8,128]{2,1,0:T(8,128)} %constant.18.clone.coef_ref, s32[64,128]{1,0:T(8,128)} %bitcast.15, bf16[64,128,128]{2,1,0:T(8,128)(2,1)} %bitcast.10, ...), custom_call_target="tpu_custom_call", output_to_operand_aliasing={{0}: (4, {}), {1}: (5, {})} | custom-call | flops 2400000000 | bytes 4800000 | tf_op jit(solution)/shard_map/slopes/pallas_call | solution.py:307
  58.4 0.0 collective-permute-done.6.far_ref
  58.4 0.0 collective-permute-done.4.other_ref
  58.4 0.6 copy-done.10
  59.0 0.6 copy-done.5
  59.6 2.1 %join.1 = (bf16[2,144,128]{2,1,0:T(8,128)(2,1)}, f32[128,128]{1,0:T(8,128)}) custom-call(s32[64,11]{1,0:T(8,128)} %copy.44.code_ref, f32[128,128]{1,0:T(8,128)} %get-tuple-element.26.own_ref, f32[128,128]{1,0:T(8,128)} %copy-done.5, bf16[16,128]{1,0:T(8,128)(2,1)} %copy-done.9, bf16[16,128]{1,0:T(8,128)(2,1)} %copy-done.10), custom_call_target="tpu_custom_call" | custom-call | tf_op jit(solution)/shard_map/join/pallas_call | solution.py:377
  61.7 0.7 collective-permute-start.7
  62.4 0.3 collective-permute-start.8
  62.7 2.8 %collective-permute-start.9 = (bf16[2,144,128]{2,1,0:T(8,128)(2,1)}, bf16[2,144,128]{2,1,0:T(8,128)(2,1)S(1)}, u32[]{:S(2)}, u32[]{:S(2)}) collective-permute-start(bf16[2,144,128]{2,1,0:T(8,128)(2,1)} %get-tuple-element.28.rest_0_), channel_id=1, source_target_pairs={{0,12},{4,0},{8,4},{12,8},{1,13},{5,1},{9,5},{13,9},{2,14},{6,2},{... | collective-permute-start | bytes 221192 | tf_op jit(solution)/shard_map/ppermute | solution.py:477
  65.5 6.2 %slopes.7 = (f32[64,4,128,128]{3,2,1,0:T(8,128)}, f32[64,8,128]{2,1,0:T(8,128)}) custom-call(s32[64,11]{1,0:T(8,128)} %copy.44.code_ref, f32[22,8,128]{2,1,0:T(8,128)} %constant.18.clone.coef_ref, s32[64,128]{1,0:T(8,128)} %bitcast.16, bf16[64,128,128]{2,1,0:T(8,128)(2,1)} %bitcast.11, ...), custom_call_target="tpu_custom_call", output_to_operand_aliasing={{0}: (4, {}), {1}: (5, {})} | custom-call | flops 2400000000 | bytes 4800000 | tf_op jit(solution)/shard_map/slopes/pallas_call | solution.py:307
  71.7 0.0 collective-permute-done.7.rest_1_
  71.7 0.0 collective-permute-done.8.rest_2_
  71.7 0.0 collective-permute-done.9.rest_3_
  71.7 0.0 copy-start.3
  71.8 0.6 copy-done.1
  72.3 0.0 copy-done.2
  72.4 0.0 copy-done.3
  72.4 10.8 %gradients.1 = f32[64,8,128]{2,1,0:T(8,128)} custom-call(s32[64,11]{1,0:T(8,128)} %copy.44.code_ref, f32[2,2,9]{2,1,0:T(2,128)} %psf_ref.1, bf16[2,144,128]{2,1,0:T(8,128)(2,1)} %get-tuple-element.28.rest_0_, bf16[2,144,128]{2,1,0:T(8,128)(2,1)} %copy-done.1, bf16[2,144,128]{2,1,0:T(8,128)(2,1)} %copy-done.2, bf16[2,144,128]{2,1,0:T(8,128)(2,1)} %copy-done.3, ...), custom_call_target="tpu_custom_call" | custom-call | flops 4000000000 | bytes 20000000 | tf_op jit(solution)/shard_map/gradients/pallas_call | solution.py:451
  83.2 1.1 %reduce_sum.9 = f32[64,8]{1,0:T(8,128)S(1)} reduce(f32[64,8,128]{2,1,0:T(8,128)} %gradients.1, f32[]{:T(128)} %constant.16.clone.1), dimensions={2}, to_apply=%region_0.0 | reduce | flops 65024 | bytes 264196 | tf_op jit(solution)/shard_map/reduce_sum | solution.py:523
  84.3 0.1 copy.45
  84.3 0.6 broadcast_multiply_fusion
  (10 shorter events, 0.0 us)
Async XLA Ops:
  15.7 9.5 %collective-permute-start = (bf16[4,2,128,128]{3,2,1,0:T(8,128)(2,1)}, bf16[4,2,128,128]{3,2,1,0:T(8,128)(2,1)S(1)}, u32[]{:S(2)}, u32[]{:S(2)}) collective-permute-start(bf16[4,2,128,128]{3,2,1,0:T(8,128)(2,1)} %get-tuple-element.21), channel_id=1, source_target_pairs={{0,16},{16,0},{1,17},{17,1},{2,18},{18,2},{3,19},{19,3},{4,20},{20... | collective-permute-start | bytes 786440 | tf_op jit(solution)/shard_map/ppermute | solution.py:473
  25.2 0.7 copy-start
  27.7 11.9 %collective-permute-start.1 = (bf16[2,128,128]{2,1,0:T(8,128)(2,1)}, bf16[2,128,128]{2,1,0:T(8,128)(2,1)S(1)}, u32[]{:S(2)}, u32[]{:S(2)}) collective-permute-start(bf16[2,128,128]{2,1,0:T(8,128)(2,1)} %get-tuple-element.23), channel_id=1, source_target_pairs={{0,4},{4,8},{8,12},{12,0},{1,5},{5,9},{9,13},{13,1},{2,6},{6,10},{... | collective-permute-start | bytes 196616 | tf_op jit(solution)/shard_map/ppermute | solution.py:477
  29.5 10.1 %collective-permute-start.2 = (bf16[2,128,128]{2,1,0:T(8,128)(2,1)}, bf16[2,128,128]{2,1,0:T(8,128)(2,1)S(1)}, u32[]{:S(2)}, u32[]{:S(2)}) collective-permute-start(bf16[2,128,128]{2,1,0:T(8,128)(2,1)} %get-tuple-element.24), channel_id=1, source_target_pairs={{0,8},{4,12},{8,0},{12,4},{1,9},{5,13},{9,1},{13,5},{2,10},{6,14},... | collective-permute-start | bytes 196616 | tf_op jit(solution)/shard_map/ppermute | solution.py:477
  32.1 7.6 %collective-permute-start.3 = (bf16[2,128,128]{2,1,0:T(8,128)(2,1)}, bf16[2,128,128]{2,1,0:T(8,128)(2,1)S(1)}, u32[]{:S(2)}, u32[]{:S(2)}) collective-permute-start(bf16[2,128,128]{2,1,0:T(8,128)(2,1)} %get-tuple-element.25), channel_id=1, source_target_pairs={{0,12},{4,0},{8,4},{12,8},{1,13},{5,1},{9,5},{13,9},{2,14},{6,2},{... | collective-permute-start | bytes 196616 | tf_op jit(solution)/shard_map/ppermute | solution.py:477
  39.6 0.6 copy-start.6
  39.6 0.6 copy-start.7
  39.6 0.6 copy-start.8
  42.4 7.7 %copy-start.4 = (f32[128,128]{1,0:T(8,128)S(1)}, f32[128,128]{1,0:T(8,128)}, u32[]{:S(2)}) copy-start(f32[128,128]{1,0:T(8,128)} %get-tuple-element.26.own_ref) | copy-start | bytes 196612
  42.4 9.3 %collective-permute-start.5 = (bf16[16,128]{1,0:T(8,128)(2,1)}, bf16[16,128]{1,0:T(8,128)(2,1)S(1)}, u32[]{:S(2)}, u32[]{:S(2)}) collective-permute-start(bf16[16,128]{1,0:T(8,128)(2,1)} %get-tuple-element.27), channel_id=1, source_target_pairs={{1,0},{2,1},{3,2},{16,17},{17,18},{18,19},{5,4},{6,5},{7,6},{20,21... | collective-permute-start | bytes 12296 | tf_op jit(solution)/shard_map/ppermute | solution.py:482
  50.1 8.3 %collective-permute-start.4 = (f32[128,128]{1,0:T(8,128)S(1)}, f32[128,128]{1,0:T(8,128)S(1)}, u32[]{:S(2)}, u32[]{:S(2)}) collective-permute-start(f32[128,128]{1,0:T(8,128)S(1)} %copy-done.4), channel_id=1, source_target_pairs={{0,16},{16,0},{1,17},{17,1},{2,18},{18,2},{3,19},{19,3},{4,20},{20... | collective-permute-start | bytes 196616 | tf_op jit(solution)/shard_map/ppermute | solution.py:473
  51.6 6.8 %copy-start.9 = (bf16[16,128]{1,0:T(8,128)(2,1)}, bf16[16,128]{1,0:T(8,128)(2,1)S(1)}, u32[]{:S(2)}) copy-start(bf16[16,128]{1,0:T(8,128)(2,1)S(1)} %collective-permute-done.5.edge_ref) | copy-start | bytes 12292
  51.6 6.8 %collective-permute-start.6 = (bf16[16,128]{1,0:T(8,128)(2,1)S(1)}, bf16[16,128]{1,0:T(8,128)(2,1)S(1)}, u32[]{:S(2)}, u32[]{:S(2)}) collective-permute-start(bf16[16,128]{1,0:T(8,128)(2,1)S(1)} %collective-permute-done.5.edge_ref), channel_id=1, source_target_pairs={{0,16},{16,0},{1,17},{17,1},{2,18},{18,2},{3,19},{19,3},{4,20},{20... | collective-permute-start | bytes 12296 | tf_op jit(solution)/shard_map/ppermute | solution.py:473
  58.4 0.6 copy-start.10
  59.0 0.6 copy-start.5
  61.7 10.0 %collective-permute-start.7 = (bf16[2,144,128]{2,1,0:T(8,128)(2,1)}, bf16[2,144,128]{2,1,0:T(8,128)(2,1)S(1)}, u32[]{:S(2)}, u32[]{:S(2)}) collective-permute-start(bf16[2,144,128]{2,1,0:T(8,128)(2,1)} %get-tuple-element.28.rest_0_), channel_id=1, source_target_pairs={{0,4},{4,8},{8,12},{12,0},{1,5},{5,9},{9,13},{13,1},{2,6},{6,10},{... | collective-permute-start | bytes 221192 | tf_op jit(solution)/shard_map/ppermute | solution.py:477
  62.4 9.3 %collective-permute-start.8 = (bf16[2,144,128]{2,1,0:T(8,128)(2,1)}, bf16[2,144,128]{2,1,0:T(8,128)(2,1)S(1)}, u32[]{:S(2)}, u32[]{:S(2)}) collective-permute-start(bf16[2,144,128]{2,1,0:T(8,128)(2,1)} %get-tuple-element.28.rest_0_), channel_id=1, source_target_pairs={{0,8},{4,12},{8,0},{12,4},{1,9},{5,13},{9,1},{13,5},{2,10},{6,14},... | collective-permute-start | bytes 221192 | tf_op jit(solution)/shard_map/ppermute | solution.py:477
  62.7 9.0 %collective-permute-start.9 = (bf16[2,144,128]{2,1,0:T(8,128)(2,1)}, bf16[2,144,128]{2,1,0:T(8,128)(2,1)S(1)}, u32[]{:S(2)}, u32[]{:S(2)}) collective-permute-start(bf16[2,144,128]{2,1,0:T(8,128)(2,1)} %get-tuple-element.28.rest_0_), channel_id=1, source_target_pairs={{0,12},{4,0},{8,4},{12,8},{1,13},{5,1},{9,5},{13,9},{2,14},{6,2},{... | collective-permute-start | bytes 221192 | tf_op jit(solution)/shard_map/ppermute | solution.py:477
  71.7 0.6 copy-start.1
  71.7 0.6 copy-start.2
  71.7 0.7 copy-start.3

commit v3 on v2

--- a/solution.py
+++ b/solution.py
@@ -16,10 +16,11 @@
 GROUP1 = 8
 GROUP2 = 4
 GROUP3 = 4
-CHUNKS = 4
-SLOPE = jnp.float32
-CODE_TILE, CODE_EXP, CODE_ROW = 8, 9, 10
+CHUNKS = (24, 20, 20)
+SLOPE = jnp.bfloat16
 VMEM_BYTES = 56 * 1024 * 1024
+SMALL_BYTES = 20 * 1024 * 1024
+TINY_BYTES = 6 * 1024 * 1024
 
 
 def series():
@@ -100,7 +101,7 @@
     return low, high
 
 
-def sums_kernel(tiles, packed, step_blocks, code_ref, weight_ref, coef_ref, mask_ref, block_ref, *rest):
+def sums_kernel(tiles, packed, step_blocks, affine_ref, target_ref, weight_ref, coef_ref, mask_ref, block_ref, *rest):
     outs = rest[:-4]
     acc, rows_sc, cols_sc, den_sc = rest[-4:]
     step = pl.program_id(0)
@@ -119,8 +120,8 @@
             mask_row = mask_ref[pl.ds(j, 1), :].astype(F32)
             masked = block_ref[j] * mask_row.astype(BF16)
             for k in range(2):
-                (tap_y,), whole_y = taps_of(code_ref[b, 4 * k + 1], code_ref[b, 4 * k + 3], coef_ref, False)
-                (tap_x,), whole_x = taps_of(code_ref[b, 4 * k], code_ref[b, 4 * k + 2], coef_ref, False)
+                (tap_y,), whole_y = taps_of(affine_ref[0, k, 1, b], affine_ref[0, k, 3, b], coef_ref, False)
+                (tap_x,), whole_x = taps_of(affine_ref[0, k, 0, b], affine_ref[0, k, 2, b], coef_ref, False)
                 work.append([b, k, mask_row, masked, tap_y, whole_y, tap_x, whole_x])
         passes = []
         for b, k, mask_row, masked, tap_y, whole_y, tap_x, whole_x in work:
@@ -131,7 +132,7 @@
             (lx_t,) = spread([tap_x], whole_x)
             warps.append(dot(jnp.concatenate([row_pass, mask_rows(mask_row)], axis=0), lx_t))
         for (b, k, mask_row, masked, tap_y, whole_y, tap_x, whole_x), both in zip(work, warps):
-            tile = code_ref[b, CODE_TILE]
+            tile = target_ref[0, 0, b]
             weight = weight_ref[0, b]
             sent = (weight * both[:side]).astype(BF16).astype(F32)
             acc[k, tile] = acc[k, tile] + sent
@@ -156,12 +157,12 @@
                 den_sc[k, t] = dot_t(rows, cols)
                 return carry
 
-            lax.fori_loop(0, tiles, one, 0)
+            lax.fori_loop(0, tiles, one, 0, unroll=tiles if packed else 1)
         if packed:
             keep_ref, send_ref = outs
-            low_end = code_ref[0, CODE_EXP] == 0
+            low_end = lax.axis_index("exp") == 0
             for dz in range(tiles):
-                tile = lax.rem(code_ref[0, CODE_ROW] + dz, tiles)
+                tile = lax.rem(lax.axis_index("tx") + dz, tiles)
                 for which, source in enumerate((acc, den_sc)):
                     low, high = halves_of(source[0, tile], source[1, tile])
                     keep_ref[dz, which] = jnp.where(low_end, low, high)
@@ -181,11 +182,16 @@
     return pl.BlockSpec(memory_space=pltpu.VMEM)
 
 
+def scalars(array):
+    rank = array.ndim
+    return pl.BlockSpec(array.shape, lambda i: (0,) * rank, memory_space=pltpu.SMEM)
+
+
 def smem():
     return pl.BlockSpec(memory_space=pltpu.SMEM)
 
 
-def tile_sums(codes, weights, coef, masks, blocks, tiles, packed):
+def tile_sums(affine, target, weights, coef, masks, blocks, tiles, packed):
     count, side = blocks.shape[0], blocks.shape[1]
     step_blocks = GROUP1
     if packed:
@@ -197,8 +203,9 @@
         grid=(count // step_blocks,),
         out_shape=[jax.ShapeDtypeStruct(*shape) for shape in shapes],
         in_specs=[
-            smem(),
-            smem(),
+            scalars(affine),
+            scalars(target),
+            scalars(weights),
             pl.BlockSpec(coef.shape, lambda i: (0, 0, 0)),
             pl.BlockSpec((step_blocks, side), lambda i: (i, 0)),
             pl.BlockSpec((step_blocks, side, side), lambda i: (i, 0, 0)),
@@ -213,23 +220,27 @@
         compiler_params=pltpu.CompilerParams(vmem_limit_bytes=VMEM_BYTES),
         cost_estimate=pl.CostEstimate(flops=int(8e9), bytes_accessed=int(3e6), transcendentals=0),
         name="tile_sums",
-    )(codes, weights, coef, masks, blocks)
-
-
-def pair_kernel(keep_ref, got_ref, *outs):
+    )(affine, target, weights, coef, masks, blocks)
+
+
+def pair_kernel(keep_ref, got_ref, after_ref, *outs):
+    del after_ref
     for dz, out in enumerate(outs):
         for which in range(2):
             total = keep_ref[dz, which] + got_ref[dz, which].astype(F32)
             out[which] = total.astype(out.dtype)
 
 
-def pair(keep, got):
+def pair(keep, got, after):
     tiles, _, side, _ = keep.shape
     return pl.pallas_call(
         pair_kernel,
         out_shape=[jax.ShapeDtypeStruct((2, side, side), BF16 if dz else F32) for dz in range(tiles)],
+        in_specs=[vmem(), vmem(), smem()],
+        out_specs=[vmem()] * tiles,
+        compiler_params=pltpu.CompilerParams(vmem_limit_bytes=TINY_BYTES),
         name="pair",
-    )(keep, got)
+    )(keep, got, after)
 
 
 def moments(product_x, product_y):
@@ -252,8 +263,9 @@
     return [first, second, first * lane * (1.0 / side), fourth * (1.0 / side)]
 
 
-def slopes_kernel(step_blocks, start, code_ref, coef_ref, mask_ref, block_ref, *rest):
-    slope_ref, part_ref = rest[-2:]
+def slopes_kernel(step_blocks, start, affine_ref, coef_ref, mask_ref, block_ref, *rest):
+    slope_ref, part_ref, token_ref = rest[-3:]
+    token_ref[0] = 0
     step = pl.program_id(0) + start
     side = 128
 
@@ -263,12 +275,12 @@
         for u in range(GROUP2):
             j = group * GROUP2 + u
             b = step * step_blocks + j
-            mask_row = mask_ref[pl.ds(j, 1), :].astype(F32)
+            mask_row = mask_ref[pl.ds(b, 1), :].astype(F32)
             masked = block_ref[j] * mask_row.astype(BF16)
             taps = []
             for k in range(2):
-                taps.append(taps_of(code_ref[b, 4 * k], code_ref[b, 4 * k + 2], coef_ref, True))
-                taps.append(taps_of(code_ref[b, 4 * k + 1], code_ref[b, 4 * k + 3], coef_ref, True))
+                taps.append(taps_of(affine_ref[0, k, 0, b], affine_ref[0, k, 2, b], coef_ref, True))
+                taps.append(taps_of(affine_ref[0, k, 1, b], affine_ref[0, k, 3, b], coef_ref, True))
             work.append([j, masked, mask_rows(mask_row), taps])
         cols, rights, rows, downs = [], [], [], []
         for j, masked, extra, taps in work:
@@ -300,36 +312,37 @@
     lax.fori_loop(0, step_blocks // GROUP2, body, 0)
 
 
-def slopes_of(codes, coef, masks, blocks, first, size, filled):
-    count, side = blocks.shape[0], blocks.shape[1]
-    step_blocks = 8
+def slopes_of(affine, coef, masks, blocks, first, size):
+    side = blocks.shape[1]
+    step_blocks = GROUP2
     start = first // step_blocks
     return pl.pallas_call(
         functools.partial(slopes_kernel, step_blocks, start),
         grid=(size // step_blocks,),
         out_shape=[
-            jax.ShapeDtypeStruct((count, 4, side, side), SLOPE),
-            jax.ShapeDtypeStruct((count, 8, side), F32),
+            jax.ShapeDtypeStruct((size, 4, side, side), SLOPE),
+            jax.ShapeDtypeStruct((size, 8, side), F32),
+            jax.ShapeDtypeStruct((1,), jnp.int32),
         ],
         in_specs=[
+            scalars(affine),
+            pl.BlockSpec(coef.shape, lambda i: (0, 0, 0)),
+            pl.BlockSpec(masks.shape, lambda i: (0, 0)),
+            pl.BlockSpec((step_blocks, side, side), lambda i: (i + start, 0, 0)),
+        ],
+        out_specs=[
+            pl.BlockSpec((step_blocks, 4, side, side), lambda i: (i, 0, 0, 0)),
+            pl.BlockSpec((step_blocks, 8, side), lambda i: (i, 0, 0)),
             smem(),
-            pl.BlockSpec(coef.shape, lambda i: (0, 0, 0)),
-            pl.BlockSpec((step_blocks, side), lambda i: (i + start, 0)),
-            pl.BlockSpec((step_blocks, side, side), lambda i: (i + start, 0, 0)),
-        ]
-        + [pl.BlockSpec(memory_space=pl.ANY)] * len(filled),
-        out_specs=[
-            pl.BlockSpec((step_blocks, 4, side, side), lambda i: (i + start, 0, 0, 0)),
-            pl.BlockSpec((step_blocks, 8, side), lambda i: (i + start, 0, 0)),
         ],
-        input_output_aliases={4 + n: n for n in range(len(filled))},
-        compiler_params=pltpu.CompilerParams(vmem_limit_bytes=VMEM_BYTES),
+        compiler_params=pltpu.CompilerParams(vmem_limit_bytes=SMALL_BYTES),
         cost_estimate=pl.CostEstimate(flops=int(1.5e8) * size, bytes_accessed=int(3e5) * size, transcendentals=0),
         name="slopes",
-    )(codes, coef, masks, blocks, *filled)
-
-
-def coadd_kernel(code_ref, *refs):
+    )(affine, coef, masks, blocks)
+
+
+def coadd_kernel(after_ref, *refs):
+    del after_ref
     parts, (piece_ref, edge_ref) = refs[:-2], refs[-2:]
     num, den = parts[0][0], parts[0][1]
     for part in parts[1:]:
@@ -344,43 +357,19 @@
     half = side // 2
     outer = jnp.concatenate([flipped[0:8], flipped[half : half + 8]], axis=0)
     inner = jnp.concatenate([flipped[half - 8 : half], flipped[side - 8 : side]], axis=0)
-    edge_ref[...] = jnp.where(code_ref[0, CODE_EXP] == 0, outer, inner).astype(BF16)
-
-
-def coadd_of(codes, parts):
+    edge_ref[...] = jnp.where(lax.axis_index("exp") == 0, outer, inner).astype(BF16)
+
+
+def coadd_of(after, parts):
     side = parts[0].shape[2]
     return pl.pallas_call(
         coadd_kernel,
         out_shape=[jax.ShapeDtypeStruct((side, side), F32), jax.ShapeDtypeStruct((16, side), BF16)],
         in_specs=[smem()] + [vmem()] * len(parts),
         out_specs=[vmem(), vmem()],
+        compiler_params=pltpu.CompilerParams(vmem_limit_bytes=TINY_BYTES),
         name="coadd",
-    )(codes, *parts)
-
-
-def join_kernel(code_ref, own_ref, other_ref, edge_ref, far_ref, sky_ref, tile_ref):
-    here = code_ref[0, CODE_EXP] == 0
-    side = own_ref.shape[1]
-    own, other = own_ref[...], other_ref[...]
-    tiles = halves_of(jnp.where(here, own, other), jnp.where(here, other, own))
-    edge, far = edge_ref[...].astype(F32), far_ref[...].astype(F32)
-    left, right = jnp.where(here, far, edge), jnp.where(here, edge, far)
-    for k in range(2):
-        sky_ref[k, 0:side, :] = tiles[k].astype(BF16)
-        at = slice(8 * k, 8 * k + 8)
-        sky_ref[k, side : side + 16, :] = jnp.concatenate([left[at], right[at]], axis=0).astype(BF16)
-    tile_ref[...] = tiles[1]
-
-
-def join(codes, own, other, edge, far):
-    side = own.shape[1]
-    return pl.pallas_call(
-        join_kernel,
-        out_shape=[jax.ShapeDtypeStruct((2, side + 16, side), BF16), jax.ShapeDtypeStruct((side, side), F32)],
-        in_specs=[smem()] + [vmem()] * 4,
-        out_specs=[vmem(), vmem()],
-        name="join",
-    )(codes, own, other, edge, far)
+    )(after, *parts)
 
 
 def band_of(values, diagonal):
@@ -391,82 +380,128 @@
     return jnp.concatenate([high, (total - high.astype(F32)).astype(BF16)], axis=1)
 
 
-def gradient_kernel(tiles, step_blocks, code_ref, psf_ref, *rest):
+def smoothed(tile, edges, taps):
+    side = tile.shape[1]
+    along = lax.broadcasted_iota(jnp.int32, (side, side), 0)
+    across = lax.broadcasted_iota(jnp.int32, (side, side), 1)
+    edge = along[:16]
+    edge = jnp.where(edge < 8, edge - 8, edge + side - 8)
+    inner = band_of(taps, along - across + RAD)
+    outer = band_of(taps, edge - across[:16] + RAD)
+    high = tile.astype(BF16)
+    low = (tile - high.astype(F32)).astype(BF16)
+    both = dot(high, inner) + dot_t(edges, outer)
+    return both[:, :side] + both[:, side:] + dot(low, inner[:, :side])
+
+
+def join_kernel(psf_ref, own_ref, other_ref, edge_ref, far_ref, after_ref, sky_ref, tile_ref):
+    del after_ref
+    here = lax.axis_index("exp") == 0
+    own, other = own_ref[...], other_ref[...]
+    tiles = halves_of(jnp.where(here, own, other), jnp.where(here, other, own))
+    edge, far = edge_ref[...].astype(F32), far_ref[...].astype(F32)
+    left, right = jnp.where(here, far, edge), jnp.where(here, edge, far)
+    for k in range(2):
+        at = slice(8 * k, 8 * k + 8)
+        edges = jnp.concatenate([left[at], right[at]], axis=0).astype(BF16)
+        sky_ref[k] = smoothed(tiles[k], edges, [psf_ref[k, 1, q] for q in range(TAPS)]).astype(BF16)
+    tile_ref[...] = tiles[1]
+
+
+def join(psf, own, other, edge, far, after):
+    side = own.shape[1]
+    return pl.pallas_call(
+        join_kernel,
+        out_shape=[jax.ShapeDtypeStruct((2, side, side), BF16), jax.ShapeDtypeStruct((side, side), F32)],
+        in_specs=[smem()] + [vmem()] * 4 + [smem()],
+        out_specs=[vmem(), vmem()],
+        compiler_params=pltpu.CompilerParams(vmem_limit_bytes=TINY_BYTES),
+        name="join",
+    )(psf, own, other, edge, far, after)
+
+
+def whole_kernel(psf_ref, tile_ref, edge_ref, sky_ref):
+    for k in range(2):
+        sky_ref[k] = smoothed(tile_ref[k], edge_ref[k], [psf_ref[k, 1, q] for q in range(TAPS)]).astype(BF16)
+
+
+def whole_sky(psf, tiles, edges):
+    return pl.pallas_call(
+        whole_kernel,
+        out_shape=jax.ShapeDtypeStruct(tiles.shape, BF16),
+        in_specs=[smem(), vmem(), vmem()],
+        out_specs=vmem(),
+        compiler_params=pltpu.CompilerParams(vmem_limit_bytes=TINY_BYTES),
+        name="whole_sky",
+    )(psf, tiles, edges)
+
+
+def gradient_kernel(tiles, target_ref, psf_ref, *rest):
     skies = rest[:tiles]
-    slope_ref, part_ref, out_ref, smooth, model = rest[tiles:]
-    step = pl.program_id(0)
+    chunk_refs, (out_ref, smooth, model) = rest[tiles:-3], rest[-3:]
     side = 128
-
-    @pl.when(step == 0)
-    def _():
-        along = lax.broadcasted_iota(jnp.int32, (side, side), 0)
-        across = lax.broadcasted_iota(jnp.int32, (side, side), 1)
-        edge = lax.broadcasted_iota(jnp.int32, (16, side), 0)
-        edge = jnp.where(edge < 8, edge - 8, edge + side - 8)
-        for k in range(2):
-            taps = [psf_ref[k, 1, q] for q in range(TAPS)]
-            inner = band_of(taps, along - across + RAD)
-            outer = band_of(taps, edge - across[:16] + RAD)
-            smooth[k, 0:8, :] = jnp.zeros((8, side), F32)
-            smooth[k, 8 + tiles * side : 16 + tiles * side, :] = jnp.zeros((8, side), F32)
-            for turn in range(tiles):
-                tile = lax.rem(code_ref[0, CODE_ROW] + tiles - turn, tiles)
-                both = dot(skies[turn][k, 0:side, :], inner) + dot_t(skies[turn][k, side : side + 16, :], outer)
-                smooth[k, pl.ds(pl.multiple_of(8 + tile * side, 8), side), :] = both[:, :side] + both[:, side:]
-            chunk = 64
-
-            def rows(c, carry, k=k):
-                start = pl.multiple_of(c * chunk, chunk)
-                seen = smooth[k, pl.ds(start, chunk + 16), :]
-                total = psf_ref[k, 0, 0] * seen[4 : 4 + chunk]
-                for p in range(1, TAPS):
-                    total = total + psf_ref[k, 0, p] * seen[4 + p : 4 + p + chunk]
-                model[k, pl.ds(start, chunk), :] = total.astype(BF16).astype(F32)
-                return carry
-
-            lax.fori_loop(0, tiles * side // chunk, rows, 0)
-
-    def body(group, carry):
-        found = []
-        for u in range(GROUP3):
-            j = group * GROUP3 + u
-            start = pl.multiple_of(code_ref[step * step_blocks + j, CODE_TILE] * side, side)
-            for k in range(2):
-                cutout = model[k, pl.ds(start, side), :]
-                slope_x, slope_y = slope_ref[j, 2 * k].astype(F32), slope_ref[j, 2 * k + 1].astype(F32)
-                found.append((j, k, moments(cutout * slope_x, cutout * slope_y)))
-        for j, k, rows in found:
-            for m, row in enumerate(rows):
-                out_ref[j, 4 * k + m : 4 * k + m + 1, :] = part_ref[j, 4 * k + m : 4 * k + m + 1, :] - row
-        return carry
-
-    lax.fori_loop(0, step_blocks // GROUP3, body, 0)
-
-
-def gradients_of(codes, psf, skies, slopes, parts):
-    count, _, side, _ = slopes.shape
-    tiles = len(skies)
-    step_blocks = 8
-    sky_shape = skies[0].shape
-    return pl.pallas_call(
-        functools.partial(gradient_kernel, tiles, step_blocks),
-        grid=(count // step_blocks,),
-        out_shape=jax.ShapeDtypeStruct((count, 8, side), F32),
-        in_specs=[smem(), smem()]
-        + [pl.BlockSpec(sky_shape, lambda i: (0, 0, 0))] * tiles
-        + [
-            pl.BlockSpec((step_blocks, 4, side, side), lambda i: (i, 0, 0, 0)),
-            pl.BlockSpec((step_blocks, 8, side), lambda i: (i, 0, 0)),
-        ],
-        out_specs=pl.BlockSpec((step_blocks, 8, side), lambda i: (i, 0, 0)),
+    for k in range(2):
+        smooth[k, 0:8, :] = jnp.zeros((8, side), F32)
+        smooth[k, 8 + tiles * side : 16 + tiles * side, :] = jnp.zeros((8, side), F32)
+        for turn in range(tiles):
+            tile = lax.rem(lax.axis_index("tx") + tiles - turn, tiles)
+            smooth[k, pl.ds(pl.multiple_of(8 + tile * side, 8), side), :] = skies[turn][k].astype(F32)
+        chunk = 64
+
+        def rows(c, carry, k=k):
+            start = pl.multiple_of(c * chunk, chunk)
+            seen = smooth[k, pl.ds(start, chunk + 16), :]
+            total = psf_ref[k, 0, 0] * seen[4 : 4 + chunk]
+            for p in range(1, TAPS):
+                total = total + psf_ref[k, 0, p] * seen[4 + p : 4 + p + chunk]
+            model[k, pl.ds(start, chunk), :] = total.astype(BF16).astype(F32)
+            return carry
+
+        lax.fori_loop(0, tiles * side // chunk, rows, 0, unroll=2)
+
+    lane = lax.broadcasted_iota(jnp.int32, out_ref.shape[1:], 2)
+    gathered = jnp.zeros(out_ref.shape[1:], F32)
+    first = 0
+    for slope_ref, part_ref in zip(chunk_refs[::2], chunk_refs[1::2]):
+
+        def body(group, gathered, first=first, slope_ref=slope_ref, part_ref=part_ref):
+            found = []
+            for u in range(GROUP3):
+                j = group * GROUP3 + u
+                start = pl.multiple_of(target_ref[0, 0, first + j] * side, side)
+                rows = []
+                for k in range(2):
+                    cutout = model[k, pl.ds(start, side), :]
+                    slope_x, slope_y = slope_ref[j, 2 * k].astype(F32), slope_ref[j, 2 * k + 1].astype(F32)
+                    rows += moments(cutout * slope_x, cutout * slope_y)
+                found.append((j, rows))
+            for j, rows in found:
+                total = jnp.sum(part_ref[j] - jnp.concatenate(rows, axis=0), axis=1, keepdims=True) * (1.0 / side)
+                gathered = jnp.where(lane == first + j, total.reshape(2, 4, 1), gathered)
+            return gathered
+
+        gathered = lax.fori_loop(0, slope_ref.shape[0] // GROUP3, body, gathered)
+        first += slope_ref.shape[0]
+    out_ref[0] = gathered
+
+
+def gradients_of(target, psf, skies, chunks):
+    side = skies[0].shape[1]
+    tiles, count = len(skies), target.shape[2]
+    arrays = [array for pair_of in chunks for array in pair_of]
+    return pl.pallas_call(
+        functools.partial(gradient_kernel, tiles),
+        out_shape=jax.ShapeDtypeStruct((1, 2, 4, count), F32),
+        in_specs=[smem(), smem()] + [vmem()] * (tiles + len(arrays)),
+        out_specs=vmem(),
         scratch_shapes=[
             pltpu.VMEM((2, tiles * side + 16, side), F32),
             pltpu.VMEM((2, tiles * side, side), F32),
         ],
-        compiler_params=pltpu.CompilerParams(vmem_limit_bytes=VMEM_BYTES),
+        compiler_params=pltpu.CompilerParams(vmem_limit_bytes=SMALL_BYTES),
         cost_estimate=pl.CostEstimate(flops=int(4e9), bytes_accessed=int(20e6), transcendentals=0),
         name="gradients",
-    )(codes, psf, *skies, slopes, parts)
+    )(target, psf, *skies, *arrays)
 
 
 def swap(cells):
@@ -487,24 +522,26 @@
     count, side = blocks.shape[0], blocks.shape[1]
     tiles, halves, columns = lax.axis_size("tx"), lax.axis_size("exp"), lax.axis_size("ty")
     coef = jnp.asarray(series())
-    place = [jnp.full((count, 1), lax.axis_index(axis), jnp.int32) for axis in ("exp", "tx")]
-    codes = jnp.concatenate([affine.reshape(count, 8), block_tile[0]] + place, axis=1)
+    affine = affine.transpose(0, 2, 3, 1)
+    block_tile = block_tile.transpose(0, 2, 1)
     masks = col_mask[0]
     small = halves == 2 and tiles <= 4
-    sums = tile_sums(codes, block_weight, coef, masks, blocks, tiles, small)
-    filled = ()
-    for chunk in range(CHUNKS):
-        size = count // CHUNKS
-        filled = slopes_of(codes, coef, masks, blocks, chunk * size, size, filled)
-    slopes, parts = filled
+    sums = tile_sums(affine, block_tile, block_weight, coef, masks, blocks, tiles, small)
+    chunks, tokens, first = [], [], 0
+    scale = count // sum(CHUNKS)
+    for size in CHUNKS:
+        *found, token = slopes_of(affine, coef, masks, blocks, first, size * scale)
+        chunks.append(found)
+        tokens.append(token)
+        first += size * scale
     if small:
         keep, send = sums
-        totals = pair(keep, swap(send))
+        totals = pair(keep, swap(send), tokens[0])
         got = [totals[0]] + [turned(totals[dz], dz, tiles) for dz in range(1, tiles)]
-        piece, edge = coadd_of(codes, got)
+        piece, edge = coadd_of(tokens[1], got)
         other = swap(piece)
         edge = to_sides(edge, columns)
-        sky, coadd_tile = join(codes, piece, other, edge, swap(edge))
+        sky, coadd_tile = join(psf, piece, other, edge, swap(edge), tokens[1])
         skies = [sky] + [turned(sky, dz, tiles) for dz in range(1, tiles)]
     else:
         me = lax.axis_index("tx")
@@ -516,12 +553,11 @@
         flipped = jnp.swapaxes(both, 1, 2).astype(BF16)
         left = lax.ppermute(flipped[:, side - 8 :], "ty", [(y, y + 1) for y in range(columns - 1)])
         right = lax.ppermute(flipped[:, :8], "ty", [(y + 1, y) for y in range(columns - 1)])
-        sky = jnp.concatenate([both.astype(BF16), left, right], axis=1)
+        sky = whole_sky(psf, both, jnp.concatenate([left, right], axis=1))
         gathered = lax.all_gather(sky, "tx", axis=0)
         skies = [lax.dynamic_index_in_dim(gathered, (me + tiles - turn) % tiles, 0, False) for turn in range(tiles)]
-    rows = gradients_of(codes, psf, skies, slopes, parts)
-    gradients = (jnp.sum(rows, axis=2) / side).reshape(1, count, 2, 4)
-    return gradients, coadd_tile
+    gradients = gradients_of(block_tile, psf, skies, chunks)
+    return gradients.transpose(0, 3, 1, 2), coadd_tile
 
 
 def solution(mesh):

time: 86.1 us -> 60 us (0.70); the launches traced: 84.9 us -> 59.8 us
  Pallas kernels: 55.1 us -> 37.4 us
  local copies, waits for them, and re-layouts: 4.08 us -> 0.03 us
  other arithmetic: 2.47 us -> 0 us
    pallas_call x4 -> x3, Pallas kernels: 24.8 us -> 16.2 us  [slopes_of(): pl.pallas_call(functools.partial(slopes_kernel, step_blocks, start), grid...]
    pallas_call x2, Pallas kernels: 12.9 us -> 7.68 us  [the longest x1 5.63 us: gradients_of(): pl.pallas_call(functools.partial(gradient_kernel, tiles), out_shape=jax.S...]
    unnamed x22 -> x14, local copies, waits for them, and re-layouts: 3.17 us -> 0.03 us
    ppermute x3, waiting for transfers between devices: 6.58 us -> 4.12 us  [swap(): return lax.ppermute(cells, 'exp', [(0, 1), (1, 0)])]
    ppermute x1, waiting for transfers between devices: 0.01 us -> 1.76 us  [to_sides(): return lax.ppermute(edge, ('exp', 'ty'), perm)]
    pallas_call x1, Pallas kernels: 13.5 us -> 12 us  [tile_sums(): pl.pallas_call(functools.partial(sums_kernel, tiles, packed, step_blocks)...]
    pallas_call x1, Pallas kernels: 2.11 us -> 0.81 us  [coadd_of(): pl.pallas_call(coadd_kernel, out_shape=[jax.ShapeDtypeStruct((side, side)...]
    pallas_call x1, Pallas kernels: 1.84 us -> 0.69 us  [pair(): pl.pallas_call(pair_kernel, out_shape=[jax.ShapeDtypeStruct((2, side, sid...]
  transfers between devices with their start and end apart: 10 -> 10, of which waited for: 1 -> 4; matrix products, arithmetic and copies ran while one was open for 0% -> 0% of each run, Pallas kernels for 29% -> 27%
where the time goes in v3:
time: 60 us; the launch traced here: 59.8 us
  Pallas kernels  37.4 us (62%)
  starting transfers between devices  15.4 us (26%)
  waiting for transfers between devices  6.21 us (10%)
  between operations  0.76 us (1%)
    pallas_call x3, Pallas kernels, slopes_of(): pl.pallas_call(functools.partial(slopes_kernel, step_blocks, start), grid...  16.2 us
    pallas_call x1, Pallas kernels, tile_sums(): pl.pallas_call(functools.partial(sums_kernel, tiles, packed, step_blocks)...  12 us
    ppermute x6, starting transfers between devices, turned(): lax.ppermute(cells, 'tx', [(z, (z + dz) % tiles) for z in range(tiles)])  9.66 us
    pallas_call x1, Pallas kernels, gradients_of(): pl.pallas_call(functools.partial(gradient_kernel, tiles), out_shape=jax.S...  5.63 us
    ppermute x3, starting transfers between devices, swap(): return lax.ppermute(cells, 'exp', [(0, 1), (1, 0)])  4.49 us
    ppermute x3, waiting for transfers between devices, swap(): return lax.ppermute(cells, 'exp', [(0, 1), (1, 0)])  4.12 us
    pallas_call x1, Pallas kernels, join(): pl.pallas_call(join_kernel, out_shape=[jax.ShapeDtypeStruct((2, side, sid...  2.05 us
    ppermute x1, waiting for transfers between devices, to_sides(): return lax.ppermute(edge, ('exp', 'ty'), perm)  1.76 us
  transfers between devices with their start and end apart: 10, of which 4 were waited for; matrix products, arithmetic and copies ran while one was open for 0% of the time, Pallas kernels for 27%

profile of v3, /device:TPU:0, one launch (start us, length us, event | category | flops | bytes accessed | tf_op | source)
XLA Modules:
  0.0 59.8 jit_solution(14816774309997489152)
XLA Ops:
  0.6 0.0 copy-start.2
  0.6 0.0 copy-start.3
  0.7 0.0 copy-start.4
  0.7 0.0 copy-start.6
  0.7 12.0 %tile_sums.1 = (f32[4,2,128,128]{3,2,1,0:T(8,128)}, bf16[4,2,128,128]{3,2,1,0:T(8,128)(2,1)}) custom-call(s32[1,2,4,64]{3,2,1,0:T(4,128)} %bitcast.13, s32[1,1,64]{2,1,0:T(1,128)} %bitcast.17, f32[1,64]{1,0:T(1,128)} %weight_ref.1, f32[22,8,128]{2,1,0:T(8,128)} %constant.2.clone.coef_ref, s32[64,128]{1,0:T(8,128)} %bitcast.9, bf16[64,128,128]{2,1,0:T(8,128)(2,1)} %bitcast.5), custom_call_target="tpu_custom_call" | custom-call | flops 8000000000 | bytes 3000000 | tf_op jit(solution)/shard_map/tile_sums/pallas_call | solution.py:201
  12.7 0.0 copy-start
  12.7 2.9 %collective-permute-start = (bf16[4,2,128,128]{3,2,1,0:T(8,128)(2,1)}, bf16[4,2,128,128]{3,2,1,0:T(8,128)(2,1)S(1)}, u32[]{:S(2)}, u32[]{:S(2)}) collective-permute-start(bf16[4,2,128,128]{3,2,1,0:T(8,128)(2,1)} %get-tuple-element.22), channel_id=1, source_target_pairs={{0,16},{16,0},{1,17},{17,1},{2,18},{18,2},{3,19},{19,3},{4,20},{20... | collective-permute-start | bytes 786440 | tf_op jit(solution)/shard_map/ppermute | solution.py:508
  15.6 0.0 copy-done.2
  15.6 0.0 copy-done.3
  15.6 0.0 copy-done.4
  15.6 0.0 copy-done.6
  15.7 6.0 %slopes.4 = (bf16[24,4,128,128]{3,2,1,0:T(8,128)(2,1)S(1)}, f32[24,8,128]{2,1,0:T(8,128)S(1)}, s32[1]{0:T(128)}) custom-call(s32[1,2,4,64]{3,2,1,0:T(4,128)S(1)} %bitcast.14, f32[22,8,128]{2,1,0:T(8,128)S(1)} %copy-done.6, s32[64,128]{1,0:T(8,128)S(1)} %bitcast.10, bf16[64,128,128]{2,1,0:T(8,128)(2,1)S(1)} %bitcast.6), custom_call_target="tpu_custom_call" | custom-call | flops 3600000000 | bytes 7200000 | tf_op jit(solution)/shard_map/slopes/pallas_call | solution.py:319
  21.6 0.5 collective-permute-done.got_ref
  22.2 0.0 copy-done
  22.2 0.7 %pair.1 = (f32[2,128,128]{2,1,0:T(8,128)S(1)}, bf16[2,128,128]{2,1,0:T(8,128)(2,1)S(1)}, bf16[2,128,128]{2,1,0:T(8,128)(2,1)S(1)}, bf16[2,128,128]{2,1,0:T(8,128)(2,1)S(1)}) custom-call(f32[4,2,128,128]{3,2,1,0:T(8,128)S(1)} %copy-done, bf16[4,2,128,128]{3,2,1,0:T(8,128)(2,1)S(1)} %collective-permute-done.got_ref, s32[1]{0:T(128)} %get-tuple-element.23.after_ref), custom_call_target="tpu_custom_call" | custom-call | tf_op jit(solution)/shard_map/pair/pallas_call | solution.py:236
  22.9 1.9 %collective-permute-start.1 = (bf16[2,128,128]{2,1,0:T(8,128)(2,1)S(1)}, bf16[2,128,128]{2,1,0:T(8,128)(2,1)S(1)}, u32[]{:S(2)}, u32[]{:S(2)}) collective-permute-start(bf16[2,128,128]{2,1,0:T(8,128)(2,1)S(1)} %get-tuple-element.25), channel_id=1, source_target_pairs={{0,4},{4,8},{8,12},{12,0},{1,5},{5,9},{9,13},{13,1},{2,6},{6,10},{... | collective-permute-start | bytes 196616 | tf_op jit(solution)/shard_map/ppermute | solution.py:512
  24.7 2.6 %collective-permute-start.2 = (bf16[2,128,128]{2,1,0:T(8,128)(2,1)S(1)}, bf16[2,128,128]{2,1,0:T(8,128)(2,1)S(1)}, u32[]{:S(2)}, u32[]{:S(2)}) collective-permute-start(bf16[2,128,128]{2,1,0:T(8,128)(2,1)S(1)} %get-tuple-element.26), channel_id=1, source_target_pairs={{0,8},{4,12},{8,0},{12,4},{1,9},{5,13},{9,1},{13,5},{2,10},{6,14},... | collective-permute-start | bytes 196616 | tf_op jit(solution)/shard_map/ppermute | solution.py:512
  27.3 0.0 copy-start.1
  27.3 1.4 %collective-permute-start.3 = (bf16[2,128,128]{2,1,0:T(8,128)(2,1)S(1)}, bf16[2,128,128]{2,1,0:T(8,128)(2,1)S(1)}, u32[]{:S(2)}, u32[]{:S(2)}) collective-permute-start(bf16[2,128,128]{2,1,0:T(8,128)(2,1)S(1)} %get-tuple-element.27), channel_id=1, source_target_pairs={{0,12},{4,0},{8,4},{12,8},{1,13},{5,1},{9,5},{13,9},{2,14},{6,2},{... | collective-permute-start | bytes 196616 | tf_op jit(solution)/shard_map/ppermute | solution.py:512
  28.7 5.1 %slopes.3 = (bf16[20,4,128,128]{3,2,1,0:T(8,128)(2,1)S(1)}, f32[20,8,128]{2,1,0:T(8,128)S(1)}, s32[1]{0:T(128)}) custom-call(s32[1,2,4,64]{3,2,1,0:T(4,128)S(1)} %bitcast.15, f32[22,8,128]{2,1,0:T(8,128)S(1)} %copy-done.6, s32[64,128]{1,0:T(8,128)S(1)} %bitcast.11, bf16[64,128,128]{2,1,0:T(8,128)(2,1)S(1)} %bitcast.7), custom_call_target="tpu_custom_call" | custom-call | flops 3000000000 | bytes 6000000 | tf_op jit(solution)/shard_map/slopes/pallas_call | solution.py:319
  33.8 0.0 collective-permute-done.1.refs_1_
  33.8 0.0 collective-permute-done.2.refs_2_
  33.8 0.0 collective-permute-done.3.refs_3_
  33.8 0.8 %coadd.1 = (f32[128,128]{1,0:T(8,128)S(1)}, bf16[16,128]{1,0:T(8,128)(2,1)S(1)}) custom-call(s32[1]{0:T(128)} %get-tuple-element.20.after_ref, f32[2,128,128]{2,1,0:T(8,128)S(1)} %get-tuple-element.24.refs_0_, bf16[2,128,128]{2,1,0:T(8,128)(2,1)S(1)} %collective-permute-done.1.refs_1_, bf16[2,128,128]{2,1,0:T(8,128)(2,1)S(1)} %collective-permute-done.2.refs_2_, ...), custom_call_target="tpu_custom_call" | custom-call | tf_op jit(solution)/shard_map/coadd/pallas_call | solution.py:365
  34.7 1.5 %collective-permute-start.4 = (f32[128,128]{1,0:T(8,128)S(1)}, f32[128,128]{1,0:T(8,128)S(1)}, u32[]{:S(2)}, u32[]{:S(2)}) collective-permute-start(f32[128,128]{1,0:T(8,128)S(1)} %get-tuple-element.28.own_ref), channel_id=1, source_target_pairs={{0,16},{16,0},{1,17},{17,1},{2,18},{18,2},{3,19},{19,3},{4,20},{20... | collective-permute-start | bytes 196616 | tf_op jit(solution)/shard_map/ppermute | solution.py:508
  36.2 1.3 %collective-permute-start.5 = (bf16[16,128]{1,0:T(8,128)(2,1)S(1)}, bf16[16,128]{1,0:T(8,128)(2,1)S(1)}, u32[]{:S(2)}, u32[]{:S(2)}) collective-permute-start(bf16[16,128]{1,0:T(8,128)(2,1)S(1)} %get-tuple-element.29), channel_id=1, source_target_pairs={{1,0},{2,1},{3,2},{16,17},{17,18},{18,19},{5,4},{6,5},{7,6},{20,21... | collective-permute-start | bytes 12296 | tf_op jit(solution)/shard_map/ppermute | solution.py:517
  37.5 1.8 %collective-permute-done.5.edge_ref = bf16[16,128]{1,0:T(8,128)(2,1)S(1)} collective-permute-done((bf16[16,128]{1,0:T(8,128)(2,1)S(1)}, bf16[16,128]{1,0:T(8,128)(2,1)S(1)}, u32[]{:S(2)}, u32[]{:S(2)}) %collective-permute-start.5) | collective-permute-done | bytes 4128 | tf_op jit(solution)/shard_map/ppermute | solution.py:517
  39.2 0.0 collective-permute-start.6
  39.2 3.6 %collective-permute-done.6.far_ref = bf16[16,128]{1,0:T(8,128)(2,1)S(1)} collective-permute-done((bf16[16,128]{1,0:T(8,128)(2,1)S(1)}, bf16[16,128]{1,0:T(8,128)(2,1)S(1)}, u32[]{:S(2)}, u32[]{:S(2)}) %collective-permute-start.6) | collective-permute-done | bytes 4128 | tf_op jit(solution)/shard_map/ppermute | solution.py:508
  42.9 0.0 collective-permute-done.4.other_ref
  42.9 0.0 copy-done.1
  42.9 2.1 %join.1 = (bf16[2,128,128]{2,1,0:T(8,128)(2,1)S(1)}, f32[128,128]{1,0:T(8,128)}) custom-call(f32[2,2,9]{2,1,0:T(2,128)S(1)} %copy-done.1, f32[128,128]{1,0:T(8,128)S(1)} %get-tuple-element.28.own_ref, f32[128,128]{1,0:T(8,128)S(1)} %collective-permute-done.4.other_ref, bf16[16,128]{1,0:T(8,128)(2,1)S(1)} %collective-permute-done.5.edge_ref, ...), custom_call_target="tpu_custom_call" | custom-call | tf_op jit(solution)/shard_map/join/pallas_call | solution.py:413
  44.9 0.0 copy-start.5
  44.9 0.7 %collective-permute-start.7 = (bf16[2,128,128]{2,1,0:T(8,128)(2,1)S(1)}, bf16[2,128,128]{2,1,0:T(8,128)(2,1)S(1)}, u32[]{:S(2)}, u32[]{:S(2)}) collective-permute-start(bf16[2,128,128]{2,1,0:T(8,128)(2,1)S(1)} %get-tuple-element.30.rest_0_), channel_id=1, source_target_pairs={{0,4},{4,8},{8,12},{12,0},{1,5},{5,9},{9,13},{13,1},{2,6},{6,10},{... | collective-permute-start | bytes 196616 | tf_op jit(solution)/shard_map/ppermute | solution.py:512
  45.6 0.8 %collective-permute-start.8 = (bf16[2,128,128]{2,1,0:T(8,128)(2,1)S(1)}, bf16[2,128,128]{2,1,0:T(8,128)(2,1)S(1)}, u32[]{:S(2)}, u32[]{:S(2)}) collective-permute-start(bf16[2,128,128]{2,1,0:T(8,128)(2,1)S(1)} %get-tuple-element.30.rest_0_), channel_id=1, source_target_pairs={{0,8},{4,12},{8,0},{12,4},{1,9},{5,13},{9,1},{13,5},{2,10},{6,14},... | collective-permute-start | bytes 196616 | tf_op jit(solution)/shard_map/ppermute | solution.py:512
  46.4 2.3 %collective-permute-start.9 = (bf16[2,128,128]{2,1,0:T(8,128)(2,1)S(1)}, bf16[2,128,128]{2,1,0:T(8,128)(2,1)S(1)}, u32[]{:S(2)}, u32[]{:S(2)}) collective-permute-start(bf16[2,128,128]{2,1,0:T(8,128)(2,1)S(1)} %get-tuple-element.30.rest_0_), channel_id=1, source_target_pairs={{0,12},{4,0},{8,4},{12,8},{1,13},{5,1},{9,5},{13,9},{2,14},{6,2},{... | collective-permute-start | bytes 196616 | tf_op jit(solution)/shard_map/ppermute | solution.py:512
  48.7 5.1 %slopes.5 = (bf16[20,4,128,128]{3,2,1,0:T(8,128)(2,1)S(1)}, f32[20,8,128]{2,1,0:T(8,128)S(1)}, s32[1]{0:T(128)}) custom-call(s32[1,2,4,64]{3,2,1,0:T(4,128)S(1)} %bitcast.16, f32[22,8,128]{2,1,0:T(8,128)S(1)} %copy-done.6, s32[64,128]{1,0:T(8,128)S(1)} %bitcast.12, bf16[64,128,128]{2,1,0:T(8,128)(2,1)S(1)} %bitcast.8), custom_call_target="tpu_custom_call" | custom-call | flops 3000000000 | bytes 6000000 | tf_op jit(solution)/shard_map/slopes/pallas_call | solution.py:319
  53.9 0.0 collective-permute-done.7.rest_1_
  53.9 0.3 collective-permute-done.8.rest_2_
  54.2 0.0 collective-permute-done.9.rest_3_
  54.2 0.0 copy-done.5
  54.2 5.6 %gradients.1 = f32[1,2,4,64]{3,2,1,0:T(4,128)} custom-call(s32[1,1,64]{2,1,0:T(1,128)S(1)} %bitcast.18, f32[2,2,9]{2,1,0:T(2,128)S(1)} %copy-done.1, bf16[2,128,128]{2,1,0:T(8,128)(2,1)S(1)} %get-tuple-element.30.rest_0_, bf16[2,128,128]{2,1,0:T(8,128)(2,1)S(1)} %collective-permute-done.7.rest_1_, bf16[2,128,128]{2,1,0:T(8,128)(2,1)S(1)} %collective-permute-done.8.rest_2_, ...), custom_call_target="tpu_custom_call" | custom-call | flops 4000000000 | bytes 20000000 | tf_op jit(solution)/shard_map/gradients/pallas_call | solution.py:492
Async XLA Ops:
  0.6 15.0 %copy-start.2 = (bf16[1,64,128,128]{3,2,1,0:T(8,128)(2,1)S(1)}, bf16[1,64,128,128]{3,2,1,0:T(8,128)(2,1)}, u32[]{:S(2)}) copy-start(bf16[1,64,128,128]{3,2,1,0:T(8,128)(2,1)} %param.7) | copy-start | bytes 6291460
  0.6 15.0 %copy-start.3 = (s32[1,64,128]{2,1,0:T(8,128)S(1)}, s32[1,64,128]{2,1,0:T(8,128)}, u32[]{:S(2)}) copy-start(s32[1,64,128]{2,1,0:T(8,128)} %param.10) | copy-start | bytes 98308
  0.7 15.0 %copy-start.4 = (s32[1,64,2,4]{1,3,2,0:T(4,128)S(1)}, s32[1,64,2,4]{1,3,2,0:T(4,128)}, u32[]{:S(2)}) copy-start(s32[1,64,2,4]{1,3,2,0:T(4,128)} %param.9) | copy-start | bytes 6148
  0.7 15.0 %copy-start.6 = (f32[22,8,128]{2,1,0:T(8,128)S(1)}, f32[22,8,128]{2,1,0:T(8,128)}, u32[]{:S(2)}) copy-start(f32[22,8,128]{2,1,0:T(8,128)} %constant.2.clone.coef_ref) | copy-start | bytes 270340
  12.7 9.5 %copy-start = (f32[4,2,128,128]{3,2,1,0:T(8,128)S(1)}, f32[4,2,128,128]{3,2,1,0:T(8,128)}, u32[]{:S(2)}) copy-start(f32[4,2,128,128]{3,2,1,0:T(8,128)} %get-tuple-element.21.keep_ref) | copy-start | bytes 1572868
  12.7 9.5 %collective-permute-start = (bf16[4,2,128,128]{3,2,1,0:T(8,128)(2,1)}, bf16[4,2,128,128]{3,2,1,0:T(8,128)(2,1)S(1)}, u32[]{:S(2)}, u32[]{:S(2)}) collective-permute-start(bf16[4,2,128,128]{3,2,1,0:T(8,128)(2,1)} %get-tuple-element.22), channel_id=1, source_target_pairs={{0,16},{16,0},{1,17},{17,1},{2,18},{18,2},{3,19},{19,3},{4,20},{20... | collective-permute-start | bytes 786440 | tf_op jit(solution)/shard_map/ppermute | solution.py:508
  22.9 11.0 %collective-permute-start.1 = (bf16[2,128,128]{2,1,0:T(8,128)(2,1)S(1)}, bf16[2,128,128]{2,1,0:T(8,128)(2,1)S(1)}, u32[]{:S(2)}, u32[]{:S(2)}) collective-permute-start(bf16[2,128,128]{2,1,0:T(8,128)(2,1)S(1)} %get-tuple-element.25), channel_id=1, source_target_pairs={{0,4},{4,8},{8,12},{12,0},{1,5},{5,9},{9,13},{13,1},{2,6},{6,10},{... | collective-permute-start | bytes 196616 | tf_op jit(solution)/shard_map/ppermute | solution.py:512
  24.7 9.1 %collective-permute-start.2 = (bf16[2,128,128]{2,1,0:T(8,128)(2,1)S(1)}, bf16[2,128,128]{2,1,0:T(8,128)(2,1)S(1)}, u32[]{:S(2)}, u32[]{:S(2)}) collective-permute-start(bf16[2,128,128]{2,1,0:T(8,128)(2,1)S(1)} %get-tuple-element.26), channel_id=1, source_target_pairs={{0,8},{4,12},{8,0},{12,4},{1,9},{5,13},{9,1},{13,5},{2,10},{6,14},... | collective-permute-start | bytes 196616 | tf_op jit(solution)/shard_map/ppermute | solution.py:512
  27.3 15.5 %copy-start.1 = (f32[2,2,9]{2,1,0:T(2,128)S(1)}, f32[2,2,9]{2,1,0:T(2,128)}, u32[]{:S(2)}) copy-start(f32[2,2,9]{2,1,0:T(2,128)} %psf_ref.3) | copy-start | bytes 436
  27.3 6.5 %collective-permute-start.3 = (bf16[2,128,128]{2,1,0:T(8,128)(2,1)S(1)}, bf16[2,128,128]{2,1,0:T(8,128)(2,1)S(1)}, u32[]{:S(2)}, u32[]{:S(2)}) collective-permute-start(bf16[2,128,128]{2,1,0:T(8,128)(2,1)S(1)} %get-tuple-element.27), channel_id=1, source_target_pairs={{0,12},{4,0},{8,4},{12,8},{1,13},{5,1},{9,5},{13,9},{2,14},{6,2},{... | collective-permute-start | bytes 196616 | tf_op jit(solution)/shard_map/ppermute | solution.py:512
  34.7 8.2 %collective-permute-start.4 = (f32[128,128]{1,0:T(8,128)S(1)}, f32[128,128]{1,0:T(8,128)S(1)}, u32[]{:S(2)}, u32[]{:S(2)}) collective-permute-start(f32[128,128]{1,0:T(8,128)S(1)} %get-tuple-element.28.own_ref), channel_id=1, source_target_pairs={{0,16},{16,0},{1,17},{17,1},{2,18},{18,2},{3,19},{19,3},{4,20},{20... | collective-permute-start | bytes 196616 | tf_op jit(solution)/shard_map/ppermute | solution.py:508
  36.2 3.0 %collective-permute-start.5 = (bf16[16,128]{1,0:T(8,128)(2,1)S(1)}, bf16[16,128]{1,0:T(8,128)(2,1)S(1)}, u32[]{:S(2)}, u32[]{:S(2)}) collective-permute-start(bf16[16,128]{1,0:T(8,128)(2,1)S(1)} %get-tuple-element.29), channel_id=1, source_target_pairs={{1,0},{2,1},{3,2},{16,17},{17,18},{18,19},{5,4},{6,5},{7,6},{20,21... | collective-permute-start | bytes 12296 | tf_op jit(solution)/shard_map/ppermute | solution.py:517
  39.2 3.6 %collective-permute-start.6 = (bf16[16,128]{1,0:T(8,128)(2,1)S(1)}, bf16[16,128]{1,0:T(8,128)(2,1)S(1)}, u32[]{:S(2)}, u32[]{:S(2)}) collective-permute-start(bf16[16,128]{1,0:T(8,128)(2,1)S(1)} %collective-permute-done.5.edge_ref), channel_id=1, source_target_pairs={{0,16},{16,0},{1,17},{17,1},{2,18},{18,2},{3,19},{19,3},{4,20},{20... | collective-permute-start | bytes 12296 | tf_op jit(solution)/shard_map/ppermute | solution.py:508
  44.9 9.3 %copy-start.5 = (s32[1,64,1]{1,2,0:T(1,128)S(1)}, s32[1,64,1]{1,2,0:T(1,128)}, u32[]{:S(2)}) copy-start(s32[1,64,1]{1,2,0:T(1,128)} %param.8) | copy-start | bytes 772
  44.9 8.9 %collective-permute-start.7 = (bf16[2,128,128]{2,1,0:T(8,128)(2,1)S(1)}, bf16[2,128,128]{2,1,0:T(8,128)(2,1)S(1)}, u32[]{:S(2)}, u32[]{:S(2)}) collective-permute-start(bf16[2,128,128]{2,1,0:T(8,128)(2,1)S(1)} %get-tuple-element.30.rest_0_), channel_id=1, source_target_pairs={{0,4},{4,8},{8,12},{12,0},{1,5},{5,9},{9,13},{13,1},{2,6},{6,10},{... | collective-permute-start | bytes 196616 | tf_op jit(solution)/shard_map/ppermute | solution.py:512
  45.6 8.6 %collective-permute-start.8 = (bf16[2,128,128]{2,1,0:T(8,128)(2,1)S(1)}, bf16[2,128,128]{2,1,0:T(8,128)(2,1)S(1)}, u32[]{:S(2)}, u32[]{:S(2)}) collective-permute-start(bf16[2,128,128]{2,1,0:T(8,128)(2,1)S(1)} %get-tuple-element.30.rest_0_), channel_id=1, source_target_pairs={{0,8},{4,12},{8,0},{12,4},{1,9},{5,13},{9,1},{13,5},{2,10},{6,14},... | collective-permute-start | bytes 196616 | tf_op jit(solution)/shard_map/ppermute | solution.py:512
  46.4 7.8 %collective-permute-start.9 = (bf16[2,128,128]{2,1,0:T(8,128)(2,1)S(1)}, bf16[2,128,128]{2,1,0:T(8,128)(2,1)S(1)}, u32[]{:S(2)}, u32[]{:S(2)}) collective-permute-start(bf16[2,128,128]{2,1,0:T(8,128)(2,1)S(1)} %get-tuple-element.30.rest_0_), channel_id=1, source_target_pairs={{0,12},{4,0},{8,4},{12,8},{1,13},{5,1},{9,5},{13,9},{2,14},{6,2},{... | collective-permute-start | bytes 196616 | tf_op jit(solution)/shard_map/ppermute | solution.py:512

commit v4 on v3

--- a/solution.py
+++ b/solution.py
@@ -15,8 +15,8 @@
 BF16 = jnp.bfloat16
 GROUP1 = 8
 GROUP2 = 4
-GROUP3 = 4
-CHUNKS = (24, 20, 20)
+GROUP3 = 8
+CHUNKS = (24, 16, 24)
 SLOPE = jnp.bfloat16
 VMEM_BYTES = 56 * 1024 * 1024
 SMALL_BYTES = 20 * 1024 * 1024
@@ -380,60 +380,82 @@
     return jnp.concatenate([high, (total - high.astype(F32)).astype(BF16)], axis=1)
 
 
-def smoothed(tile, edges, taps):
-    side = tile.shape[1]
+def bands_kernel(psf_ref, after_ref, inner_ref, outer_ref, token_ref):
+    token_ref[0] = after_ref[0]
+    side = inner_ref.shape[1]
     along = lax.broadcasted_iota(jnp.int32, (side, side), 0)
     across = lax.broadcasted_iota(jnp.int32, (side, side), 1)
     edge = along[:16]
     edge = jnp.where(edge < 8, edge - 8, edge + side - 8)
-    inner = band_of(taps, along - across + RAD)
-    outer = band_of(taps, edge - across[:16] + RAD)
+    for k in range(2):
+        taps = [psf_ref[k, 1, q] for q in range(TAPS)]
+        inner_ref[k] = band_of(taps, along - across + RAD)
+        outer_ref[k] = band_of(taps, edge - across[:16] + RAD)
+
+
+def bands_of(psf, after, side=128):
+    return pl.pallas_call(
+        bands_kernel,
+        out_shape=[jax.ShapeDtypeStruct((2, rows, 2 * side), BF16) for rows in (side, 16)]
+        + [jax.ShapeDtypeStruct((1,), jnp.int32)],
+        in_specs=[smem(), smem()],
+        out_specs=[vmem(), vmem(), smem()],
+        compiler_params=pltpu.CompilerParams(vmem_limit_bytes=TINY_BYTES),
+        name="bands",
+    )(psf, after)
+
+
+def smoothed(tile, edges, inner, outer):
+    side = tile.shape[1]
     high = tile.astype(BF16)
     low = (tile - high.astype(F32)).astype(BF16)
     both = dot(high, inner) + dot_t(edges, outer)
     return both[:, :side] + both[:, side:] + dot(low, inner[:, :side])
 
 
-def join_kernel(psf_ref, own_ref, other_ref, edge_ref, far_ref, after_ref, sky_ref, tile_ref):
+def join_kernel(inner_ref, outer_ref, own_ref, other_ref, edge_ref, far_ref, after_ref, sky_ref, tile_ref):
     del after_ref
     here = lax.axis_index("exp") == 0
     own, other = own_ref[...], other_ref[...]
     tiles = halves_of(jnp.where(here, own, other), jnp.where(here, other, own))
     edge, far = edge_ref[...].astype(F32), far_ref[...].astype(F32)
     left, right = jnp.where(here, far, edge), jnp.where(here, edge, far)
+    column = lax.axis_index("ty")
+    left = jnp.where(column > 0, left, 0.0)
+    right = jnp.where(column < lax.axis_size("ty") - 1, right, 0.0)
     for k in range(2):
         at = slice(8 * k, 8 * k + 8)
         edges = jnp.concatenate([left[at], right[at]], axis=0).astype(BF16)
-        sky_ref[k] = smoothed(tiles[k], edges, [psf_ref[k, 1, q] for q in range(TAPS)]).astype(BF16)
+        sky_ref[k] = smoothed(tiles[k], edges, inner_ref[k], outer_ref[k]).astype(BF16)
     tile_ref[...] = tiles[1]
 
 
-def join(psf, own, other, edge, far, after):
+def join(bands, own, other, edge, far, after):
     side = own.shape[1]
     return pl.pallas_call(
         join_kernel,
         out_shape=[jax.ShapeDtypeStruct((2, side, side), BF16), jax.ShapeDtypeStruct((side, side), F32)],
-        in_specs=[smem()] + [vmem()] * 4 + [smem()],
+        in_specs=[vmem()] * 6 + [smem()],
         out_specs=[vmem(), vmem()],
         compiler_params=pltpu.CompilerParams(vmem_limit_bytes=TINY_BYTES),
         name="join",
-    )(psf, own, other, edge, far, after)
-
-
-def whole_kernel(psf_ref, tile_ref, edge_ref, sky_ref):
+    )(*bands, own, other, edge, far, after)
+
+
+def whole_kernel(inner_ref, outer_ref, tile_ref, edge_ref, sky_ref):
     for k in range(2):
-        sky_ref[k] = smoothed(tile_ref[k], edge_ref[k], [psf_ref[k, 1, q] for q in range(TAPS)]).astype(BF16)
-
-
-def whole_sky(psf, tiles, edges):
+        sky_ref[k] = smoothed(tile_ref[k], edge_ref[k], inner_ref[k], outer_ref[k]).astype(BF16)
+
+
+def whole_sky(bands, tiles, edges):
     return pl.pallas_call(
         whole_kernel,
         out_shape=jax.ShapeDtypeStruct(tiles.shape, BF16),
-        in_specs=[smem(), vmem(), vmem()],
+        in_specs=[vmem()] * 4,
         out_specs=vmem(),
         compiler_params=pltpu.CompilerParams(vmem_limit_bytes=TINY_BYTES),
         name="whole_sky",
-    )(psf, tiles, edges)
+    )(*bands, tiles, edges)
 
 
 def gradient_kernel(tiles, target_ref, psf_ref, *rest):
@@ -512,8 +534,9 @@
     return lax.ppermute(cells, "tx", [(z, (z + dz) % tiles) for z in range(tiles)])
 
 
-def to_sides(edge, columns):
-    perm = [(y, y - 1) for y in range(1, columns)] + [(columns + y, columns + y + 1) for y in range(columns - 1)]
+def to_sides(edge, columns, flip):
+    perm = [(y, flip * columns + (y - 1) % columns) for y in range(columns)]
+    perm += [(columns + y, (1 - flip) * columns + (y + 1) % columns) for y in range(columns)]
     return lax.ppermute(edge, ("exp", "ty"), perm)
 
 
@@ -536,12 +559,13 @@
         first += size * scale
     if small:
         keep, send = sums
-        totals = pair(keep, swap(send), tokens[0])
+        *bands, token = bands_of(psf, tokens[0])
+        totals = pair(keep, swap(send), token)
         got = [totals[0]] + [turned(totals[dz], dz, tiles) for dz in range(1, tiles)]
         piece, edge = coadd_of(tokens[1], got)
         other = swap(piece)
-        edge = to_sides(edge, columns)
-        sky, coadd_tile = join(psf, piece, other, edge, swap(edge), tokens[1])
+        near, far = to_sides(edge, columns, 0), to_sides(edge, columns, 1)
+        sky, coadd_tile = join(bands, piece, other, near, far, tokens[-2])
         skies = [sky] + [turned(sky, dz, tiles) for dz in range(1, tiles)]
     else:
         me = lax.axis_index("tx")
@@ -553,7 +577,7 @@
         flipped = jnp.swapaxes(both, 1, 2).astype(BF16)
         left = lax.ppermute(flipped[:, side - 8 :], "ty", [(y, y + 1) for y in range(columns - 1)])
         right = lax.ppermute(flipped[:, :8], "ty", [(y + 1, y) for y in range(columns - 1)])
-        sky = whole_sky(psf, both, jnp.concatenate([left, right], axis=1))
+        sky = whole_sky(bands_of(psf, tokens[0])[:2], both, jnp.concatenate([left, right], axis=1))
         gathered = lax.all_gather(sky, "tx", axis=0)
         skies = [lax.dynamic_index_in_dim(gathered, (me + tiles - turn) % tiles, 0, False) for turn in range(tiles)]
     gradients = gradients_of(block_tile, psf, skies, chunks)

time: 60 us -> 55.5 us (0.925)
  waiting for transfers between devices: 6.21 us -> 2.38 us
  starting transfers between devices: 15.4 us -> 14.3 us
    ppermute x3 -> x2, waiting for transfers between devices: 4.12 us -> 0.01 us  [swap(): return lax.ppermute(cells, 'exp', [(0, 1), (1, 0)])]
    pallas_call x0 -> x1, Pallas kernels: none -> 1.73 us  [bands_of(): pl.pallas_call(bands_kernel, out_shape=[jax.ShapeDtypeStruct((2, rows, 2...]
    ppermute x6, starting transfers between devices: 9.66 us -> 7.97 us  [turned(): lax.ppermute(cells, 'tx', [(z, (z + dz) % tiles) for z in range(tiles)])]
    ppermute x1 -> x2, starting transfers between devices: 1.28 us -> 2.73 us  [to_sides(): return lax.ppermute(edge, ('exp', 'ty'), perm)]
    ppermute x3 -> x2, starting transfers between devices: 4.49 us -> 3.61 us  [swap(): return lax.ppermute(cells, 'exp', [(0, 1), (1, 0)])]
    ppermute x6, waiting for transfers between devices: 0.33 us -> 1.05 us  [turned(): lax.ppermute(cells, 'tx', [(z, (z + dz) % tiles) for z in range(tiles)])]
    pallas_call x1, Pallas kernels: 5.63 us -> 4.92 us  [gradients_of(): pl.pallas_call(functools.partial(gradient_kernel, tiles), out_shape=jax.S...]
    pallas_call x1, Pallas kernels: 2.05 us -> 1.44 us  [join(): pl.pallas_call(join_kernel, out_shape=[jax.ShapeDtypeStruct((2, side, sid...]
  transfers between devices with their start and end apart: 10 -> 10, of which waited for: 4 -> 3; matrix products, arithmetic and copies ran while one was open for 0% -> 0% of each run, Pallas kernels for 27% -> 32%
where the time goes in v4:
time: 55.5 us; the launch traced here: 55.3 us
  Pallas kernels  37.8 us (68%)
  starting transfers between devices  14.3 us (26%)
  waiting for transfers between devices  2.38 us (4%)
  between operations  0.78 us (1%)
    pallas_call x3, Pallas kernels, slopes_of(): pl.pallas_call(functools.partial(slopes_kernel, step_blocks, start), grid...  16.2 us
    pallas_call x1, Pallas kernels, tile_sums(): pl.pallas_call(functools.partial(sums_kernel, tiles, packed, step_blocks)...  12 us
    ppermute x6, starting transfers between devices, turned(): lax.ppermute(cells, 'tx', [(z, (z + dz) % tiles) for z in range(tiles)])  7.97 us
    pallas_call x1, Pallas kernels, gradients_of(): pl.pallas_call(functools.partial(gradient_kernel, tiles), out_shape=jax.S...  4.92 us
    ppermute x2, starting transfers between devices, swap(): return lax.ppermute(cells, 'exp', [(0, 1), (1, 0)])  3.61 us
    ppermute x2, starting transfers between devices, to_sides(): return lax.ppermute(edge, ('exp', 'ty'), perm)  2.73 us
    pallas_call x1, Pallas kernels, bands_of(): pl.pallas_call(bands_kernel, out_shape=[jax.ShapeDtypeStruct((2, rows, 2...  1.73 us
    pallas_call x1, Pallas kernels, join(): pl.pallas_call(join_kernel, out_shape=[jax.ShapeDtypeStruct((2, side, sid...  1.44 us
  transfers between devices with their start and end apart: 10, of which 3 were waited for; matrix products, arithmetic and copies ran while one was open for 0% of the time, Pallas kernels for 32%

profile of v4, /device:TPU:0, one launch (start us, length us, event | category | flops | bytes accessed | tf_op | source)
XLA Modules:
  0.0 55.3 jit_solution(9417182607946889287)
XLA Ops:
  0.6 0.0 copy-start.2
  0.6 0.0 copy-start.3
  0.7 0.0 copy-start.4
  0.7 0.0 copy-start.6
  0.7 12.0 %tile_sums.1 = (f32[4,2,128,128]{3,2,1,0:T(8,128)}, bf16[4,2,128,128]{3,2,1,0:T(8,128)(2,1)}) custom-call(s32[1,2,4,64]{3,2,1,0:T(4,128)} %bitcast.13, s32[1,1,64]{2,1,0:T(1,128)} %bitcast.17, f32[1,64]{1,0:T(1,128)} %weight_ref.1, f32[22,8,128]{2,1,0:T(8,128)} %constant.2.clone.coef_ref, s32[64,128]{1,0:T(8,128)} %bitcast.9, bf16[64,128,128]{2,1,0:T(8,128)(2,1)} %bitcast.5), custom_call_target="tpu_custom_call" | custom-call | flops 8000000000 | bytes 3000000 | tf_op jit(solution)/shard_map/tile_sums/pallas_call | solution.py:201
  12.7 0.0 copy-start.1
  12.7 0.0 copy-start
  12.7 3.0 %collective-permute-start = (bf16[4,2,128,128]{3,2,1,0:T(8,128)(2,1)}, bf16[4,2,128,128]{3,2,1,0:T(8,128)(2,1)S(1)}, u32[]{:S(2)}, u32[]{:S(2)}) collective-permute-start(bf16[4,2,128,128]{3,2,1,0:T(8,128)(2,1)} %get-tuple-element.28), channel_id=1, source_target_pairs={{0,16},{16,0},{1,17},{17,1},{2,18},{18,2},{3,19},{19,3},{4,20},{20... | collective-permute-start | bytes 786440 | tf_op jit(solution)/shard_map/ppermute | solution.py:530
  15.7 0.0 copy-done.2
  15.7 0.0 copy-done.3
  15.7 0.0 copy-done.4
  15.7 0.0 copy-done.6
  15.7 6.0 %slopes.3 = (bf16[24,4,128,128]{3,2,1,0:T(8,128)(2,1)S(1)}, f32[24,8,128]{2,1,0:T(8,128)S(1)}, s32[1]{0:T(128)}) custom-call(s32[1,2,4,64]{3,2,1,0:T(4,128)S(1)} %bitcast.14, f32[22,8,128]{2,1,0:T(8,128)S(1)} %copy-done.6, s32[64,128]{1,0:T(8,128)S(1)} %bitcast.10, bf16[64,128,128]{2,1,0:T(8,128)(2,1)S(1)} %bitcast.6), custom_call_target="tpu_custom_call" | custom-call | flops 3600000000 | bytes 7200000 | tf_op jit(solution)/shard_map/slopes/pallas_call | solution.py:319
  21.7 0.0 copy-done.1
  21.8 1.7 %bands.1 = (bf16[2,128,256]{2,1,0:T(8,128)(2,1)S(1)}, bf16[2,16,256]{2,1,0:T(8,128)(2,1)S(1)}, s32[1]{0:T(128)}) custom-call(f32[2,2,9]{2,1,0:T(2,128)S(1)} %copy-done.1, s32[1]{0:T(128)} %get-tuple-element.23.after_ref), custom_call_target="tpu_custom_call" | custom-call | tf_op jit(solution)/shard_map/bands/pallas_call | solution.py:397
  23.5 0.0 collective-permute-done.got_ref
  23.5 0.0 copy-done
  23.5 0.7 %pair.1 = (f32[2,128,128]{2,1,0:T(8,128)S(1)}, bf16[2,128,128]{2,1,0:T(8,128)(2,1)S(1)}, bf16[2,128,128]{2,1,0:T(8,128)(2,1)S(1)}, bf16[2,128,128]{2,1,0:T(8,128)(2,1)S(1)}) custom-call(f32[4,2,128,128]{3,2,1,0:T(8,128)S(1)} %copy-done, bf16[4,2,128,128]{3,2,1,0:T(8,128)(2,1)S(1)} %collective-permute-done.got_ref, s32[1]{0:T(128)} %get-tuple-element.29.after_ref), custom_call_target="tpu_custom_call" | custom-call | tf_op jit(solution)/shard_map/pair/pallas_call | solution.py:236
  24.2 1.6 %collective-permute-start.1 = (bf16[2,128,128]{2,1,0:T(8,128)(2,1)S(1)}, bf16[2,128,128]{2,1,0:T(8,128)(2,1)S(1)}, u32[]{:S(2)}, u32[]{:S(2)}) collective-permute-start(bf16[2,128,128]{2,1,0:T(8,128)(2,1)S(1)} %get-tuple-element.31), channel_id=1, source_target_pairs={{0,4},{4,8},{8,12},{12,0},{1,5},{5,9},{9,13},{13,1},{2,6},{6,10},{... | collective-permute-start | bytes 196616 | tf_op jit(solution)/shard_map/ppermute | solution.py:534
  25.9 2.6 %collective-permute-start.2 = (bf16[2,128,128]{2,1,0:T(8,128)(2,1)S(1)}, bf16[2,128,128]{2,1,0:T(8,128)(2,1)S(1)}, u32[]{:S(2)}, u32[]{:S(2)}) collective-permute-start(bf16[2,128,128]{2,1,0:T(8,128)(2,1)S(1)} %get-tuple-element.32), channel_id=1, source_target_pairs={{0,8},{4,12},{8,0},{12,4},{1,9},{5,13},{9,1},{13,5},{2,10},{6,14},... | collective-permute-start | bytes 196616 | tf_op jit(solution)/shard_map/ppermute | solution.py:534
  28.4 1.3 %collective-permute-start.3 = (bf16[2,128,128]{2,1,0:T(8,128)(2,1)S(1)}, bf16[2,128,128]{2,1,0:T(8,128)(2,1)S(1)}, u32[]{:S(2)}, u32[]{:S(2)}) collective-permute-start(bf16[2,128,128]{2,1,0:T(8,128)(2,1)S(1)} %get-tuple-element.33), channel_id=1, source_target_pairs={{0,12},{4,0},{8,4},{12,8},{1,13},{5,1},{9,5},{13,9},{2,14},{6,2},{... | collective-permute-start | bytes 196616 | tf_op jit(solution)/shard_map/ppermute | solution.py:534
  29.8 4.2 %slopes.4 = (bf16[16,4,128,128]{3,2,1,0:T(8,128)(2,1)S(1)}, f32[16,8,128]{2,1,0:T(8,128)S(1)}, s32[1]{0:T(128)}) custom-call(s32[1,2,4,64]{3,2,1,0:T(4,128)S(1)} %bitcast.15, f32[22,8,128]{2,1,0:T(8,128)S(1)} %copy-done.6, s32[64,128]{1,0:T(8,128)S(1)} %bitcast.11, bf16[64,128,128]{2,1,0:T(8,128)(2,1)S(1)} %bitcast.7), custom_call_target="tpu_custom_call" | custom-call | flops 2400000000 | bytes 4800000 | tf_op jit(solution)/shard_map/slopes/pallas_call | solution.py:319
  34.0 0.0 collective-permute-done.1.refs_1_
  34.0 0.0 collective-permute-done.2.refs_2_
  34.0 0.0 collective-permute-done.3.refs_3_
  34.0 0.8 %coadd.1 = (f32[128,128]{1,0:T(8,128)S(1)}, bf16[16,128]{1,0:T(8,128)(2,1)S(1)}) custom-call(s32[1]{0:T(128)} %get-tuple-element.26.after_ref, f32[2,128,128]{2,1,0:T(8,128)S(1)} %get-tuple-element.30.refs_0_, bf16[2,128,128]{2,1,0:T(8,128)(2,1)S(1)} %collective-permute-done.1.refs_1_, bf16[2,128,128]{2,1,0:T(8,128)(2,1)S(1)} %collective-permute-done.2.refs_2_, ...), custom_call_target="tpu_custom_call" | custom-call | tf_op jit(solution)/shard_map/coadd/pallas_call | solution.py:365
  34.8 0.6 %collective-permute-start.4 = (f32[128,128]{1,0:T(8,128)S(1)}, f32[128,128]{1,0:T(8,128)S(1)}, u32[]{:S(2)}, u32[]{:S(2)}) collective-permute-start(f32[128,128]{1,0:T(8,128)S(1)} %get-tuple-element.34.own_ref), channel_id=1, source_target_pairs={{0,16},{16,0},{1,17},{17,1},{2,18},{18,2},{3,19},{19,3},{4,20},{20... | collective-permute-start | bytes 196616 | tf_op jit(solution)/shard_map/ppermute | solution.py:530
  35.5 0.4 collective-permute-start.6
  35.9 2.3 %collective-permute-start.5 = (bf16[16,128]{1,0:T(8,128)(2,1)S(1)}, bf16[16,128]{1,0:T(8,128)(2,1)S(1)}, u32[]{:S(2)}, u32[]{:S(2)}) collective-permute-start(bf16[16,128]{1,0:T(8,128)(2,1)S(1)} %get-tuple-element.35), channel_id=1, source_target_pairs={{0,3},{1,0},{2,1},{3,2},{16,17},{17,18},{18,19},{19,16},{4,7},{5,4... | collective-permute-start | bytes 12296 | tf_op jit(solution)/shard_map/ppermute | solution.py:540
  38.2 1.2 %collective-permute-done.6.far_ref = bf16[16,128]{1,0:T(8,128)(2,1)S(1)} collective-permute-done((bf16[16,128]{1,0:T(8,128)(2,1)S(1)}, bf16[16,128]{1,0:T(8,128)(2,1)S(1)}, u32[]{:S(2)}, u32[]{:S(2)}) %collective-permute-start.6) | collective-permute-done | bytes 4128 | tf_op jit(solution)/shard_map/ppermute | solution.py:540
  39.4 0.1 collective-permute-done.5.edge_ref
  39.5 0.0 collective-permute-done.4.other_ref
  39.5 1.4 %join.1 = (bf16[2,128,128]{2,1,0:T(8,128)(2,1)S(1)}, f32[128,128]{1,0:T(8,128)}) custom-call(bf16[2,128,256]{2,1,0:T(8,128)(2,1)S(1)} %get-tuple-element.24.inner_ref, bf16[2,16,256]{2,1,0:T(8,128)(2,1)S(1)} %get-tuple-element.25.outer_ref, f32[128,128]{1,0:T(8,128)S(1)} %get-tuple-element.34.own_ref, f32[128,128]{1,0:T(8,128)S(1)} %collective-permute-done.4.other_ref, ...), custom_call_target="tpu_custom_call" | custom-call | tf_op jit(solution)/shard_map/join/pallas_call | solution.py:435
  41.0 0.0 copy-start.5
  41.0 1.8 %collective-permute-start.9 = (bf16[2,128,128]{2,1,0:T(8,128)(2,1)S(1)}, bf16[2,128,128]{2,1,0:T(8,128)(2,1)S(1)}, u32[]{:S(2)}, u32[]{:S(2)}) collective-permute-start(bf16[2,128,128]{2,1,0:T(8,128)(2,1)S(1)} %get-tuple-element.36.rest_0_), channel_id=1, source_target_pairs={{0,12},{4,0},{8,4},{12,8},{1,13},{5,1},{9,5},{13,9},{2,14},{6,2},{... | collective-permute-start | bytes 196616 | tf_op jit(solution)/shard_map/ppermute | solution.py:534
  42.8 0.3 collective-permute-start.8
  43.1 0.3 collective-permute-start.7
  43.4 6.0 %slopes.5 = (bf16[24,4,128,128]{3,2,1,0:T(8,128)(2,1)S(1)}, f32[24,8,128]{2,1,0:T(8,128)S(1)}, s32[1]{0:T(128)}) custom-call(s32[1,2,4,64]{3,2,1,0:T(4,128)S(1)} %bitcast.16, f32[22,8,128]{2,1,0:T(8,128)S(1)} %copy-done.6, s32[64,128]{1,0:T(8,128)S(1)} %bitcast.12, bf16[64,128,128]{2,1,0:T(8,128)(2,1)S(1)} %bitcast.8), custom_call_target="tpu_custom_call" | custom-call | flops 3600000000 | bytes 7200000 | tf_op jit(solution)/shard_map/slopes/pallas_call | solution.py:319
  49.4 0.0 collective-permute-done.9.rest_3_
  49.4 1.0 %collective-permute-done.8.rest_2_ = bf16[2,128,128]{2,1,0:T(8,128)(2,1)S(1)} collective-permute-done((bf16[2,128,128]{2,1,0:T(8,128)(2,1)S(1)}, bf16[2,128,128]{2,1,0:T(8,128)(2,1)S(1)}, u32[]{:S(2)}, u32[]{:S(2)}) %collective-permute-start.8) | collective-permute-done | bytes 65568 | tf_op jit(solution)/shard_map/ppermute | solution.py:534
  50.4 0.0 collective-permute-done.7.rest_1_
  50.4 0.0 copy-done.5
  50.4 4.9 %gradients.1 = f32[1,2,4,64]{3,2,1,0:T(4,128)} custom-call(s32[1,1,64]{2,1,0:T(1,128)S(1)} %bitcast.18, f32[2,2,9]{2,1,0:T(2,128)S(1)} %copy-done.1, bf16[2,128,128]{2,1,0:T(8,128)(2,1)S(1)} %get-tuple-element.36.rest_0_, bf16[2,128,128]{2,1,0:T(8,128)(2,1)S(1)} %collective-permute-done.7.rest_1_, bf16[2,128,128]{2,1,0:T(8,128)(2,1)S(1)} %collective-permute-done.8.rest_2_, ...), custom_call_target="tpu_custom_call" | custom-call | flops 4000000000 | bytes 20000000 | tf_op jit(solution)/shard_map/gradients/pallas_call | solution.py:514
Async XLA Ops:
  0.6 15.1 %copy-start.2 = (bf16[1,64,128,128]{3,2,1,0:T(8,128)(2,1)S(1)}, bf16[1,64,128,128]{3,2,1,0:T(8,128)(2,1)}, u32[]{:S(2)}) copy-start(bf16[1,64,128,128]{3,2,1,0:T(8,128)(2,1)} %param.7) | copy-start | bytes 6291460
  0.6 15.1 %copy-start.3 = (s32[1,64,128]{2,1,0:T(8,128)S(1)}, s32[1,64,128]{2,1,0:T(8,128)}, u32[]{:S(2)}) copy-start(s32[1,64,128]{2,1,0:T(8,128)} %param.10) | copy-start | bytes 98308
  0.7 15.1 %copy-start.4 = (s32[1,64,2,4]{1,3,2,0:T(4,128)S(1)}, s32[1,64,2,4]{1,3,2,0:T(4,128)}, u32[]{:S(2)}) copy-start(s32[1,64,2,4]{1,3,2,0:T(4,128)} %param.9) | copy-start | bytes 6148
  0.7 15.1 %copy-start.6 = (f32[22,8,128]{2,1,0:T(8,128)S(1)}, f32[22,8,128]{2,1,0:T(8,128)}, u32[]{:S(2)}) copy-start(f32[22,8,128]{2,1,0:T(8,128)} %constant.2.clone.coef_ref) | copy-start | bytes 270340
  12.7 9.1 %copy-start.1 = (f32[2,2,9]{2,1,0:T(2,128)S(1)}, f32[2,2,9]{2,1,0:T(2,128)}, u32[]{:S(2)}) copy-start(f32[2,2,9]{2,1,0:T(2,128)} %psf_ref.3) | copy-start | bytes 436
  12.7 10.8 %copy-start = (f32[4,2,128,128]{3,2,1,0:T(8,128)S(1)}, f32[4,2,128,128]{3,2,1,0:T(8,128)}, u32[]{:S(2)}) copy-start(f32[4,2,128,128]{3,2,1,0:T(8,128)} %get-tuple-element.27.keep_ref) | copy-start | bytes 1572868
  12.7 10.8 %collective-permute-start = (bf16[4,2,128,128]{3,2,1,0:T(8,128)(2,1)}, bf16[4,2,128,128]{3,2,1,0:T(8,128)(2,1)S(1)}, u32[]{:S(2)}, u32[]{:S(2)}) collective-permute-start(bf16[4,2,128,128]{3,2,1,0:T(8,128)(2,1)} %get-tuple-element.28), channel_id=1, source_target_pairs={{0,16},{16,0},{1,17},{17,1},{2,18},{18,2},{3,19},{19,3},{4,20},{20... | collective-permute-start | bytes 786440 | tf_op jit(solution)/shard_map/ppermute | solution.py:530
  24.2 9.8 %collective-permute-start.1 = (bf16[2,128,128]{2,1,0:T(8,128)(2,1)S(1)}, bf16[2,128,128]{2,1,0:T(8,128)(2,1)S(1)}, u32[]{:S(2)}, u32[]{:S(2)}) collective-permute-start(bf16[2,128,128]{2,1,0:T(8,128)(2,1)S(1)} %get-tuple-element.31), channel_id=1, source_target_pairs={{0,4},{4,8},{8,12},{12,0},{1,5},{5,9},{9,13},{13,1},{2,6},{6,10},{... | collective-permute-start | bytes 196616 | tf_op jit(solution)/shard_map/ppermute | solution.py:534
  25.9 8.2 %collective-permute-start.2 = (bf16[2,128,128]{2,1,0:T(8,128)(2,1)S(1)}, bf16[2,128,128]{2,1,0:T(8,128)(2,1)S(1)}, u32[]{:S(2)}, u32[]{:S(2)}) collective-permute-start(bf16[2,128,128]{2,1,0:T(8,128)(2,1)S(1)} %get-tuple-element.32), channel_id=1, source_target_pairs={{0,8},{4,12},{8,0},{12,4},{1,9},{5,13},{9,1},{13,5},{2,10},{6,14},... | collective-permute-start | bytes 196616 | tf_op jit(solution)/shard_map/ppermute | solution.py:534
  28.4 5.6 %collective-permute-start.3 = (bf16[2,128,128]{2,1,0:T(8,128)(2,1)S(1)}, bf16[2,128,128]{2,1,0:T(8,128)(2,1)S(1)}, u32[]{:S(2)}, u32[]{:S(2)}) collective-permute-start(bf16[2,128,128]{2,1,0:T(8,128)(2,1)S(1)} %get-tuple-element.33), channel_id=1, source_target_pairs={{0,12},{4,0},{8,4},{12,8},{1,13},{5,1},{9,5},{13,9},{2,14},{6,2},{... | collective-permute-start | bytes 196616 | tf_op jit(solution)/shard_map/ppermute | solution.py:534
  34.8 4.7 %collective-permute-start.4 = (f32[128,128]{1,0:T(8,128)S(1)}, f32[128,128]{1,0:T(8,128)S(1)}, u32[]{:S(2)}, u32[]{:S(2)}) collective-permute-start(f32[128,128]{1,0:T(8,128)S(1)} %get-tuple-element.34.own_ref), channel_id=1, source_target_pairs={{0,16},{16,0},{1,17},{17,1},{2,18},{18,2},{3,19},{19,3},{4,20},{20... | collective-permute-start | bytes 196616 | tf_op jit(solution)/shard_map/ppermute | solution.py:530
  35.5 3.9 %collective-permute-start.6 = (bf16[16,128]{1,0:T(8,128)(2,1)S(1)}, bf16[16,128]{1,0:T(8,128)(2,1)S(1)}, u32[]{:S(2)}, u32[]{:S(2)}) collective-permute-start(bf16[16,128]{1,0:T(8,128)(2,1)S(1)} %get-tuple-element.35), channel_id=1, source_target_pairs={{0,19},{1,16},{2,17},{3,18},{16,1},{17,2},{18,3},{19,0},{4,23},{5,... | collective-permute-start | bytes 12296 | tf_op jit(solution)/shard_map/ppermute | solution.py:540
  35.9 3.6 %collective-permute-start.5 = (bf16[16,128]{1,0:T(8,128)(2,1)S(1)}, bf16[16,128]{1,0:T(8,128)(2,1)S(1)}, u32[]{:S(2)}, u32[]{:S(2)}) collective-permute-start(bf16[16,128]{1,0:T(8,128)(2,1)S(1)} %get-tuple-element.35), channel_id=1, source_target_pairs={{0,3},{1,0},{2,1},{3,2},{16,17},{17,18},{18,19},{19,16},{4,7},{5,4... | collective-permute-start | bytes 12296 | tf_op jit(solution)/shard_map/ppermute | solution.py:540
  41.0 9.5 %copy-start.5 = (s32[1,64,1]{1,2,0:T(1,128)S(1)}, s32[1,64,1]{1,2,0:T(1,128)}, u32[]{:S(2)}) copy-start(s32[1,64,1]{1,2,0:T(1,128)} %param.8) | copy-start | bytes 772
  41.0 8.4 %collective-permute-start.9 = (bf16[2,128,128]{2,1,0:T(8,128)(2,1)S(1)}, bf16[2,128,128]{2,1,0:T(8,128)(2,1)S(1)}, u32[]{:S(2)}, u32[]{:S(2)}) collective-permute-start(bf16[2,128,128]{2,1,0:T(8,128)(2,1)S(1)} %get-tuple-element.36.rest_0_), channel_id=1, source_target_pairs={{0,12},{4,0},{8,4},{12,8},{1,13},{5,1},{9,5},{13,9},{2,14},{6,2},{... | collective-permute-start | bytes 196616 | tf_op jit(solution)/shard_map/ppermute | solution.py:534
  42.8 7.6 %collective-permute-start.8 = (bf16[2,128,128]{2,1,0:T(8,128)(2,1)S(1)}, bf16[2,128,128]{2,1,0:T(8,128)(2,1)S(1)}, u32[]{:S(2)}, u32[]{:S(2)}) collective-permute-start(bf16[2,128,128]{2,1,0:T(8,128)(2,1)S(1)} %get-tuple-element.36.rest_0_), channel_id=1, source_target_pairs={{0,8},{4,12},{8,0},{12,4},{1,9},{5,13},{9,1},{13,5},{2,10},{6,14},... | collective-permute-start | bytes 196616 | tf_op jit(solution)/shard_map/ppermute | solution.py:534
  43.1 7.3 %collective-permute-start.7 = (bf16[2,128,128]{2,1,0:T(8,128)(2,1)S(1)}, bf16[2,128,128]{2,1,0:T(8,128)(2,1)S(1)}, u32[]{:S(2)}, u32[]{:S(2)}) collective-permute-start(bf16[2,128,128]{2,1,0:T(8,128)(2,1)S(1)} %get-tuple-element.36.rest_0_), channel_id=1, source_target_pairs={{0,4},{4,8},{8,12},{12,0},{1,5},{5,9},{9,13},{13,1},{2,6},{6,10},{... | collective-permute-start | bytes 196616 | tf_op jit(solution)/shard_map/ppermute | solution.py:534

commit v5 on v4

--- a/solution.py
+++ b/solution.py
@@ -14,7 +14,8 @@
 F32 = jnp.float32
 BF16 = jnp.bfloat16
 GROUP1 = 8
-GROUP2 = 4
+STEP2 = 8
+LAG2 = (0, 4, 8, 12)
 GROUP3 = 8
 CHUNKS = (24, 16, 24)
 SLOPE = jnp.bfloat16
@@ -69,14 +70,24 @@
     return lax.gather(taps, index[..., None], numbers, slice_sizes=(1, 1), mode=mode)
 
 
-def spread(tap_list, whole):
-    side = 128
-    base = lax.broadcasted_iota(jnp.int32, (8, side), 0) + 3 - whole
-    indices = [jnp.clip(base + 8 * v, 0, 7) for v in range(side // 8)]
-    return [
-        jnp.concatenate([pick(taps, index) for index in indices], axis=0).astype(BF16)
-        for taps in tap_list
-    ]
+def windows():
+    sub, lane = np.arange(8)[:, None], np.arange(128)[None, :]
+    rows = [8 * (3 * ((lane + 8 - 8 * r) // 24) + r) + sub + 3 for r in range(3)]
+    start = np.arange(128)[:, None] // 8 * 8 - 8
+    near = (lane >= start) & (lane < start + 24)
+    return np.stack(rows).astype(np.int32), near.astype(np.float32)
+
+
+def spread(tap_list, whole, rows_ref, near_ref):
+    indices = [jnp.clip(rows_ref[r] - whole, 0, 7) for r in range(3)]
+    bands = []
+    for taps in tap_list:
+        classes = [pick(taps, index) for index in indices]
+        pairs = [
+            jnp.concatenate([classes[2 * w % 3], classes[(2 * w + 1) % 3]], axis=0).astype(BF16) for w in range(3)
+        ]
+        bands.append(jnp.concatenate([pairs[w % 3] for w in range(8)], axis=0) * near_ref[...])
+    return bands
 
 
 def dot(a, b):
@@ -85,6 +96,23 @@
 
 def dot_t(a, b):
     return lax.dot_general(a, b, (((0,), (0,)), ((), ())), preferred_element_type=F32)
+
+
+def staged(count, lags, enter, first, second, leave):
+    held = [dict() for _ in range(3)]
+    for turn in range(count + max(lags)):
+        for stage in range(4):
+            j = turn - lags[stage]
+            if not 0 <= j < count:
+                continue
+            if stage == 0:
+                held[0][j] = enter(j)
+            elif stage == 1:
+                held[1][j] = first(*held[0].pop(j))
+            elif stage == 2:
+                held[2][j] = second(*held[1].pop(j))
+            else:
+                leave(j, held[2].pop(j))
 
 
 def mask_rows(mask_row):
@@ -101,7 +129,7 @@
     return low, high
 
 
-def sums_kernel(tiles, packed, step_blocks, affine_ref, target_ref, weight_ref, coef_ref, mask_ref, block_ref, *rest):
+def sums_kernel(tiles, packed, step_blocks, affine_ref, target_ref, weight_ref, coef_ref, rows_ref, near_ref, mask_ref, block_ref, *rest):
     outs = rest[:-4]
     acc, rows_sc, cols_sc, den_sc = rest[-4:]
     step = pl.program_id(0)
@@ -125,11 +153,11 @@
                 work.append([b, k, mask_row, masked, tap_y, whole_y, tap_x, whole_x])
         passes = []
         for b, k, mask_row, masked, tap_y, whole_y, tap_x, whole_x in work:
-            (ly_t,) = spread([tap_y], whole_y)
+            (ly_t,) = spread([tap_y], whole_y, rows_ref, near_ref)
             passes.append(dot_t(ly_t, masked).astype(BF16))
         warps = []
         for (b, k, mask_row, masked, tap_y, whole_y, tap_x, whole_x), row_pass in zip(work, passes):
-            (lx_t,) = spread([tap_x], whole_x)
+            (lx_t,) = spread([tap_x], whole_x, rows_ref, near_ref)
             warps.append(dot(jnp.concatenate([row_pass, mask_rows(mask_row)], axis=0), lx_t))
         for (b, k, mask_row, masked, tap_y, whole_y, tap_x, whole_x), both in zip(work, warps):
             tile = target_ref[0, 0, b]
@@ -206,7 +234,7 @@
             scalars(affine),
             scalars(target),
             scalars(weights),
-            pl.BlockSpec(coef.shape, lambda i: (0, 0, 0)),
+            *[pl.BlockSpec(c.shape, lambda i, rank=c.ndim: (0,) * rank) for c in coef],
             pl.BlockSpec((step_blocks, side), lambda i: (i, 0)),
             pl.BlockSpec((step_blocks, side, side), lambda i: (i, 0, 0)),
         ],
@@ -220,7 +248,7 @@
         compiler_params=pltpu.CompilerParams(vmem_limit_bytes=VMEM_BYTES),
         cost_estimate=pl.CostEstimate(flops=int(8e9), bytes_accessed=int(3e6), transcendentals=0),
         name="tile_sums",
-    )(affine, target, weights, coef, masks, blocks)
+    )(affine, target, weights, *coef, masks, blocks)
 
 
 def pair_kernel(keep_ref, got_ref, after_ref, *outs):
@@ -263,58 +291,58 @@
     return [first, second, first * lane * (1.0 / side), fourth * (1.0 / side)]
 
 
-def slopes_kernel(step_blocks, start, affine_ref, coef_ref, mask_ref, block_ref, *rest):
+def slopes_kernel(step_blocks, start, affine_ref, coef_ref, rows_ref, near_ref, mask_ref, block_ref, *rest):
     slope_ref, part_ref, token_ref = rest[-3:]
     token_ref[0] = 0
     step = pl.program_id(0) + start
     side = 128
 
-    def body(group, carry):
-        ones = jnp.ones((side, side), BF16)
-        work = []
-        for u in range(GROUP2):
-            j = group * GROUP2 + u
-            b = step * step_blocks + j
-            mask_row = mask_ref[pl.ds(b, 1), :].astype(F32)
-            masked = block_ref[j] * mask_row.astype(BF16)
-            taps = []
-            for k in range(2):
-                taps.append(taps_of(affine_ref[0, k, 0, b], affine_ref[0, k, 2, b], coef_ref, True))
-                taps.append(taps_of(affine_ref[0, k, 1, b], affine_ref[0, k, 3, b], coef_ref, True))
-            work.append([j, masked, mask_rows(mask_row), taps])
-        cols, rights, rows, downs = [], [], [], []
-        for j, masked, extra, taps in work:
-            x0, x1 = spread(*taps[0]), spread(*taps[2])
-            cols.append(dot(jnp.concatenate([masked, extra], axis=0), jnp.concatenate([x0[0], x1[0]], axis=1)))
-            rights.append([jnp.concatenate(x0, axis=1), jnp.concatenate(x1, axis=1)])
-        for j, masked, extra, taps in work:
-            with_ones = jnp.concatenate([masked, ones], axis=1)
-            y0, y1 = spread(*taps[1]), spread(*taps[3])
-            rows.append([dot_t(y0[0], with_ones), dot_t(y1[0], with_ones)])
-            downs.append([y0[1], y1[1]])
-        late = []
-        for (j, masked, extra, taps), col_both, right, row, down in zip(work, cols, rights, rows, downs):
-            for k in range(2):
-                row_pass = row[k][:, :side].astype(BF16)
-                col_pass = col_both[:side, k * side : (k + 1) * side].astype(BF16)
-                late.append((j, k, dot(row_pass, right[k]), dot_t(down[k], col_pass), row[k][:, side:], col_both[side : side + 1, k * side : (k + 1) * side]))
-        for j, k, both, slope_y, rows_sum, cols_sum in late:
-            warped = both[:, :side]
+    ones = jnp.ones((side, side), BF16)
+
+    def enter(j):
+        b = step * step_blocks + j
+        mask_row = mask_ref[pl.ds(b, 1), :].astype(F32)
+        masked = block_ref[j] * mask_row.astype(BF16)
+        taps = []
+        for k in range(2):
+            taps.append(taps_of(affine_ref[0, k, 0, b], affine_ref[0, k, 2, b], coef_ref, True))
+            taps.append(taps_of(affine_ref[0, k, 1, b], affine_ref[0, k, 3, b], coef_ref, True))
+        return masked, mask_rows(mask_row), taps
+
+    def first(masked, extra, taps):
+        x0, x1 = spread(*taps[0], rows_ref, near_ref), spread(*taps[2], rows_ref, near_ref)
+        col_both = dot(jnp.concatenate([masked, extra], axis=0), jnp.concatenate([x0[0], x1[0]], axis=1))
+        y0, y1 = spread(*taps[1], rows_ref, near_ref), spread(*taps[3], rows_ref, near_ref)
+        with_ones = jnp.concatenate([masked, ones], axis=1)
+        rights = [jnp.concatenate(x0, axis=1), jnp.concatenate(x1, axis=1)]
+        return col_both, [dot_t(y0[0], with_ones), dot_t(y1[0], with_ones)], rights, [y0[1], y1[1]]
+
+    def second(col_both, rows, rights, downs):
+        found = []
+        for k in range(2):
+            row_pass = rows[k][:, :side].astype(BF16)
+            col_pass = col_both[:side, k * side : (k + 1) * side].astype(BF16)
+            cols_sum = col_both[side : side + 1, k * side : (k + 1) * side]
+            found.append((dot(row_pass, rights[k]), dot_t(downs[k], col_pass), rows[k][:, side:], cols_sum))
+        return found
+
+    def leave(j, found):
+        for k, (both, slope_y, rows_sum, cols_sum) in enumerate(found):
             weight_map = jnp.maximum(rows_sum * cols_sum, 0.0)
             value_x = weight_map * both[:, side:]
             value_y = weight_map * slope_y
             slope_ref[j, 2 * k] = value_x.astype(SLOPE)
             slope_ref[j, 2 * k + 1] = value_y.astype(SLOPE)
+            warped = both[:, :side]
             for m, row in enumerate(moments(warped * value_x, warped * value_y)):
                 part_ref[j, 4 * k + m : 4 * k + m + 1, :] = row
-        return carry
-
-    lax.fori_loop(0, step_blocks // GROUP2, body, 0)
+
+    staged(step_blocks, LAG2, enter, first, second, leave)
 
 
 def slopes_of(affine, coef, masks, blocks, first, size):
     side = blocks.shape[1]
-    step_blocks = GROUP2
+    step_blocks = STEP2
     start = first // step_blocks
     return pl.pallas_call(
         functools.partial(slopes_kernel, step_blocks, start),
@@ -326,7 +354,7 @@
         ],
         in_specs=[
             scalars(affine),
-            pl.BlockSpec(coef.shape, lambda i: (0, 0, 0)),
+            *[pl.BlockSpec(c.shape, lambda i, rank=c.ndim: (0,) * rank) for c in coef],
             pl.BlockSpec(masks.shape, lambda i: (0, 0)),
             pl.BlockSpec((step_blocks, side, side), lambda i: (i + start, 0, 0)),
         ],
@@ -338,7 +366,7 @@
         compiler_params=pltpu.CompilerParams(vmem_limit_bytes=SMALL_BYTES),
         cost_estimate=pl.CostEstimate(flops=int(1.5e8) * size, bytes_accessed=int(3e5) * size, transcendentals=0),
         name="slopes",
-    )(affine, coef, masks, blocks)
+    )(affine, *coef, masks, blocks)
 
 
 def coadd_kernel(after_ref, *refs):
@@ -544,7 +572,8 @@
     blocks = exposures[0]
     count, side = blocks.shape[0], blocks.shape[1]
     tiles, halves, columns = lax.axis_size("tx"), lax.axis_size("exp"), lax.axis_size("ty")
-    coef = jnp.asarray(series())
+    rows, near = windows()
+    coef = (jnp.asarray(series()), jnp.asarray(rows), jnp.asarray(near, BF16))
     affine = affine.transpose(0, 2, 3, 1)
     block_tile = block_tile.transpose(0, 2, 1)
     masks = col_mask[0]

time: 55.5 us -> 52.2 us (0.941)
  Pallas kernels: 37.8 us -> 31.1 us
  waiting for transfers between devices: 2.38 us -> 4.35 us
  starting transfers between devices: 14.3 us -> 15.6 us
    pallas_call x3, Pallas kernels: 16.2 us -> 11.7 us  [slopes_of(): pl.pallas_call(functools.partial(slopes_kernel, step_blocks, start), grid...]
    pallas_call x1, Pallas kernels: 12 us -> 9.76 us  [tile_sums(): pl.pallas_call(functools.partial(sums_kernel, tiles, packed, step_blocks)...]
    ppermute x6, starting transfers between devices: 7.97 us -> 9.18 us  [turned(): lax.ppermute(cells, 'tx', [(z, (z + dz) % tiles) for z in range(tiles)])]
    ppermute x2, starting transfers between devices: 3.61 us -> 4.67 us  [swap(): return lax.ppermute(cells, 'exp', [(0, 1), (1, 0)])]
    ppermute x2, starting transfers between devices: 2.73 us -> 1.77 us  [to_sides(): return lax.ppermute(edge, ('exp', 'ty'), perm)]
    ppermute x2, waiting for transfers between devices: 1.33 us -> 2.16 us  [to_sides(): return lax.ppermute(edge, ('exp', 'ty'), perm)]
    ppermute x6, waiting for transfers between devices: 1.05 us -> 1.82 us  [turned(): lax.ppermute(cells, 'tx', [(z, (z + dz) % tiles) for z in range(tiles)])]
  transfers between devices with their start and end apart: 10 -> 10, of which waited for: 3 -> 4; matrix products, arithmetic and copies ran while one was open for 0% -> 0% of each run, Pallas kernels for 32% -> 26%
where the time goes in v5:
time: 52.2 us; the launch traced here: 51.9 us
  Pallas kernels  31.1 us (60%)
  starting transfers between devices  15.6 us (30%)
  waiting for transfers between devices  4.35 us (8%)
  between operations  0.79 us (2%)
    pallas_call x3, Pallas kernels, slopes_of(): pl.pallas_call(functools.partial(slopes_kernel, step_blocks, start), grid...  11.7 us
    pallas_call x1, Pallas kernels, tile_sums(): pl.pallas_call(functools.partial(sums_kernel, tiles, packed, step_blocks)...  9.76 us
    ppermute x6, starting transfers between devices, turned(): lax.ppermute(cells, 'tx', [(z, (z + dz) % tiles) for z in range(tiles)])  9.18 us
    pallas_call x1, Pallas kernels, gradients_of(): pl.pallas_call(functools.partial(gradient_kernel, tiles), out_shape=jax.S...  4.92 us
    ppermute x2, starting transfers between devices, swap(): return lax.ppermute(cells, 'exp', [(0, 1), (1, 0)])  4.67 us
    ppermute x2, waiting for transfers between devices, to_sides(): return lax.ppermute(edge, ('exp', 'ty'), perm)  2.16 us
    ppermute x6, waiting for transfers between devices, turned(): lax.ppermute(cells, 'tx', [(z, (z + dz) % tiles) for z in range(tiles)])  1.82 us
    ppermute x2, starting transfers between devices, to_sides(): return lax.ppermute(edge, ('exp', 'ty'), perm)  1.77 us
  transfers between devices with their start and end apart: 10, of which 4 were waited for; matrix products, arithmetic and copies ran while one was open for 0% of the time, Pallas kernels for 26%

profile of v5, /device:TPU:0, one launch (start us, length us, event | category | flops | bytes accessed | tf_op | source)
XLA Modules:
  0.0 51.9 jit_solution(16984873626081621207)
XLA Ops:
  0.6 0.0 copy-start.2
  0.6 0.0 copy-start.3
  0.7 0.0 copy-start.4
  0.7 0.0 copy-start.6
  0.7 0.0 copy-start.7
  0.7 0.0 copy-start.8
  0.7 9.8 %tile_sums.1 = (f32[4,2,128,128]{3,2,1,0:T(8,128)}, bf16[4,2,128,128]{3,2,1,0:T(8,128)(2,1)}) custom-call(s32[1,2,4,64]{3,2,1,0:T(4,128)} %bitcast.13, s32[1,1,64]{2,1,0:T(1,128)} %bitcast.17, f32[1,64]{1,0:T(1,128)} %weight_ref.1, f32[22,8,128]{2,1,0:T(8,128)} %constant.6.clone.coef_ref, s32[3,8,128]{2,1,0:T(8,128)} %constant.7.clone.rows_ref, ...), custom_call_target="tpu_custom_call" | custom-call | flops 8000000000 | bytes 3000000 | tf_op jit(solution)/shard_map/tile_sums/pallas_call | solution.py:229
  10.5 0.0 copy-start.1
  10.5 0.0 copy-start
  10.5 3.0 %collective-permute-start = (bf16[4,2,128,128]{3,2,1,0:T(8,128)(2,1)}, bf16[4,2,128,128]{3,2,1,0:T(8,128)(2,1)S(1)}, u32[]{:S(2)}, u32[]{:S(2)}) collective-permute-start(bf16[4,2,128,128]{3,2,1,0:T(8,128)(2,1)} %get-tuple-element.28), channel_id=1, source_target_pairs={{0,16},{16,0},{1,17},{17,1},{2,18},{18,2},{3,19},{19,3},{4,20},{20... | collective-permute-start | bytes 786440 | tf_op jit(solution)/shard_map/ppermute | solution.py:558
  13.5 0.0 copy-done.2
  13.5 0.0 copy-done.3
  13.5 0.0 copy-done.4
  13.5 0.0 copy-done.6
  13.5 0.0 copy-done.7
  13.5 0.0 copy-done.8
  13.5 4.4 %slopes.3 = (bf16[24,4,128,128]{3,2,1,0:T(8,128)(2,1)S(1)}, f32[24,8,128]{2,1,0:T(8,128)S(1)}, s32[1]{0:T(128)}) custom-call(s32[1,2,4,64]{3,2,1,0:T(4,128)S(1)} %bitcast.14, f32[22,8,128]{2,1,0:T(8,128)S(1)} %copy-done.6, s32[3,8,128]{2,1,0:T(8,128)S(1)} %copy-done.8, bf16[128,128]{1,0:T(8,128)(2,1)S(1)} %copy-done.7, s32[64,128]{1,0:T(8,128)S(1)} %bitcast.10, ...), custom_call_target="tpu_custom_call" | custom-call | flops 3600000000 | bytes 7200000 | tf_op jit(solution)/shard_map/slopes/pallas_call | solution.py:347
  17.9 0.0 copy-done.1
  17.9 1.7 %bands.1 = (bf16[2,128,256]{2,1,0:T(8,128)(2,1)S(1)}, bf16[2,16,256]{2,1,0:T(8,128)(2,1)S(1)}, s32[1]{0:T(128)}) custom-call(f32[2,2,9]{2,1,0:T(2,128)S(1)} %copy-done.1, s32[1]{0:T(128)} %get-tuple-element.23.after_ref), custom_call_target="tpu_custom_call" | custom-call | tf_op jit(solution)/shard_map/bands/pallas_call | solution.py:425
  19.6 0.4 collective-permute-done.got_ref
  20.0 0.0 copy-done
  20.0 0.7 %pair.1 = (f32[2,128,128]{2,1,0:T(8,128)S(1)}, bf16[2,128,128]{2,1,0:T(8,128)(2,1)S(1)}, bf16[2,128,128]{2,1,0:T(8,128)(2,1)S(1)}, bf16[2,128,128]{2,1,0:T(8,128)(2,1)S(1)}) custom-call(f32[4,2,128,128]{3,2,1,0:T(8,128)S(1)} %copy-done, bf16[4,2,128,128]{3,2,1,0:T(8,128)(2,1)S(1)} %collective-permute-done.got_ref, s32[1]{0:T(128)} %get-tuple-element.29.after_ref), custom_call_target="tpu_custom_call" | custom-call | tf_op jit(solution)/shard_map/pair/pallas_call | solution.py:264
  20.7 1.9 %collective-permute-start.1 = (bf16[2,128,128]{2,1,0:T(8,128)(2,1)S(1)}, bf16[2,128,128]{2,1,0:T(8,128)(2,1)S(1)}, u32[]{:S(2)}, u32[]{:S(2)}) collective-permute-start(bf16[2,128,128]{2,1,0:T(8,128)(2,1)S(1)} %get-tuple-element.31), channel_id=1, source_target_pairs={{0,4},{4,8},{8,12},{12,0},{1,5},{5,9},{9,13},{13,1},{2,6},{6,10},{... | collective-permute-start | bytes 196616 | tf_op jit(solution)/shard_map/ppermute | solution.py:562
  22.6 2.6 %collective-permute-start.2 = (bf16[2,128,128]{2,1,0:T(8,128)(2,1)S(1)}, bf16[2,128,128]{2,1,0:T(8,128)(2,1)S(1)}, u32[]{:S(2)}, u32[]{:S(2)}) collective-permute-start(bf16[2,128,128]{2,1,0:T(8,128)(2,1)S(1)} %get-tuple-element.32), channel_id=1, source_target_pairs={{0,8},{4,12},{8,0},{12,4},{1,9},{5,13},{9,1},{13,5},{2,10},{6,14},... | collective-permute-start | bytes 196616 | tf_op jit(solution)/shard_map/ppermute | solution.py:562
  25.2 1.4 %collective-permute-start.3 = (bf16[2,128,128]{2,1,0:T(8,128)(2,1)S(1)}, bf16[2,128,128]{2,1,0:T(8,128)(2,1)S(1)}, u32[]{:S(2)}, u32[]{:S(2)}) collective-permute-start(bf16[2,128,128]{2,1,0:T(8,128)(2,1)S(1)} %get-tuple-element.33), channel_id=1, source_target_pairs={{0,12},{4,0},{8,4},{12,8},{1,13},{5,1},{9,5},{13,9},{2,14},{6,2},{... | collective-permute-start | bytes 196616 | tf_op jit(solution)/shard_map/ppermute | solution.py:562
  26.5 3.1 %slopes.4 = (bf16[16,4,128,128]{3,2,1,0:T(8,128)(2,1)S(1)}, f32[16,8,128]{2,1,0:T(8,128)S(1)}, s32[1]{0:T(128)}) custom-call(s32[1,2,4,64]{3,2,1,0:T(4,128)S(1)} %bitcast.15, f32[22,8,128]{2,1,0:T(8,128)S(1)} %copy-done.6, s32[3,8,128]{2,1,0:T(8,128)S(1)} %copy-done.8, bf16[128,128]{1,0:T(8,128)(2,1)S(1)} %copy-done.7, s32[64,128]{1,0:T(8,128)S(1)} %bitcast.11, ...), custom_call_target="tpu_custom_call" | custom-call | flops 2400000000 | bytes 4800000 | tf_op jit(solution)/shard_map/slopes/pallas_call | solution.py:347
  29.6 0.0 collective-permute-done.1.refs_1_
  29.6 0.0 collective-permute-done.2.refs_2_
  29.6 0.1 collective-permute-done.3.refs_3_
  29.7 0.8 %coadd.1 = (f32[128,128]{1,0:T(8,128)S(1)}, bf16[16,128]{1,0:T(8,128)(2,1)S(1)}) custom-call(s32[1]{0:T(128)} %get-tuple-element.26.after_ref, f32[2,128,128]{2,1,0:T(8,128)S(1)} %get-tuple-element.30.refs_0_, bf16[2,128,128]{2,1,0:T(8,128)(2,1)S(1)} %collective-permute-done.1.refs_1_, bf16[2,128,128]{2,1,0:T(8,128)(2,1)S(1)} %collective-permute-done.2.refs_2_, ...), custom_call_target="tpu_custom_call" | custom-call | tf_op jit(solution)/shard_map/coadd/pallas_call | solution.py:393
  30.5 1.7 %collective-permute-start.4 = (f32[128,128]{1,0:T(8,128)S(1)}, f32[128,128]{1,0:T(8,128)S(1)}, u32[]{:S(2)}, u32[]{:S(2)}) collective-permute-start(f32[128,128]{1,0:T(8,128)S(1)} %get-tuple-element.34.own_ref), channel_id=1, source_target_pairs={{0,16},{16,0},{1,17},{17,1},{2,18},{18,2},{3,19},{19,3},{4,20},{20... | collective-permute-start | bytes 196616 | tf_op jit(solution)/shard_map/ppermute | solution.py:558
  32.2 0.0 collective-permute-start.6
  32.2 1.8 %collective-permute-start.5 = (bf16[16,128]{1,0:T(8,128)(2,1)S(1)}, bf16[16,128]{1,0:T(8,128)(2,1)S(1)}, u32[]{:S(2)}, u32[]{:S(2)}) collective-permute-start(bf16[16,128]{1,0:T(8,128)(2,1)S(1)} %get-tuple-element.35), channel_id=1, source_target_pairs={{0,3},{1,0},{2,1},{3,2},{16,17},{17,18},{18,19},{19,16},{4,7},{5,4... | collective-permute-start | bytes 12296 | tf_op jit(solution)/shard_map/ppermute | solution.py:568
  33.9 2.2 %collective-permute-done.6.far_ref = bf16[16,128]{1,0:T(8,128)(2,1)S(1)} collective-permute-done((bf16[16,128]{1,0:T(8,128)(2,1)S(1)}, bf16[16,128]{1,0:T(8,128)(2,1)S(1)}, u32[]{:S(2)}, u32[]{:S(2)}) %collective-permute-start.6) | collective-permute-done | bytes 4128 | tf_op jit(solution)/shard_map/ppermute | solution.py:568
  36.1 0.0 collective-permute-done.5.edge_ref
  36.1 0.0 collective-permute-done.4.other_ref
  36.1 1.4 %join.1 = (bf16[2,128,128]{2,1,0:T(8,128)(2,1)S(1)}, f32[128,128]{1,0:T(8,128)}) custom-call(bf16[2,128,256]{2,1,0:T(8,128)(2,1)S(1)} %get-tuple-element.24.inner_ref, bf16[2,16,256]{2,1,0:T(8,128)(2,1)S(1)} %get-tuple-element.25.outer_ref, f32[128,128]{1,0:T(8,128)S(1)} %get-tuple-element.34.own_ref, f32[128,128]{1,0:T(8,128)S(1)} %collective-permute-done.4.other_ref, ...), custom_call_target="tpu_custom_call" | custom-call | tf_op jit(solution)/shard_map/join/pallas_call | solution.py:463
  37.5 0.0 copy-start.5
  37.5 2.8 %collective-permute-start.9 = (bf16[2,128,128]{2,1,0:T(8,128)(2,1)S(1)}, bf16[2,128,128]{2,1,0:T(8,128)(2,1)S(1)}, u32[]{:S(2)}, u32[]{:S(2)}) collective-permute-start(bf16[2,128,128]{2,1,0:T(8,128)(2,1)S(1)} %get-tuple-element.36.rest_0_), channel_id=1, source_target_pairs={{0,12},{4,0},{8,4},{12,8},{1,13},{5,1},{9,5},{13,9},{2,14},{6,2},{... | collective-permute-start | bytes 196616 | tf_op jit(solution)/shard_map/ppermute | solution.py:562
  40.3 0.0 collective-permute-start.8
  40.3 0.6 %collective-permute-start.7 = (bf16[2,128,128]{2,1,0:T(8,128)(2,1)S(1)}, bf16[2,128,128]{2,1,0:T(8,128)(2,1)S(1)}, u32[]{:S(2)}, u32[]{:S(2)}) collective-permute-start(bf16[2,128,128]{2,1,0:T(8,128)(2,1)S(1)} %get-tuple-element.36.rest_0_), channel_id=1, source_target_pairs={{0,4},{4,8},{8,12},{12,0},{1,5},{5,9},{9,13},{13,1},{2,6},{6,10},{... | collective-permute-start | bytes 196616 | tf_op jit(solution)/shard_map/ppermute | solution.py:562
  40.9 4.3 %slopes.5 = (bf16[24,4,128,128]{3,2,1,0:T(8,128)(2,1)S(1)}, f32[24,8,128]{2,1,0:T(8,128)S(1)}, s32[1]{0:T(128)}) custom-call(s32[1,2,4,64]{3,2,1,0:T(4,128)S(1)} %bitcast.16, f32[22,8,128]{2,1,0:T(8,128)S(1)} %copy-done.6, s32[3,8,128]{2,1,0:T(8,128)S(1)} %copy-done.8, bf16[128,128]{1,0:T(8,128)(2,1)S(1)} %copy-done.7, s32[64,128]{1,0:T(8,128)S(1)} %bitcast.12, ...), custom_call_target="tpu_custom_call" | custom-call | flops 3600000000 | bytes 7200000 | tf_op jit(solution)/shard_map/slopes/pallas_call | solution.py:347
  45.2 0.0 collective-permute-done.9.rest_3_
  45.2 1.7 %collective-permute-done.8.rest_2_ = bf16[2,128,128]{2,1,0:T(8,128)(2,1)S(1)} collective-permute-done((bf16[2,128,128]{2,1,0:T(8,128)(2,1)S(1)}, bf16[2,128,128]{2,1,0:T(8,128)(2,1)S(1)}, u32[]{:S(2)}, u32[]{:S(2)}) %collective-permute-start.8) | collective-permute-done | bytes 65568 | tf_op jit(solution)/shard_map/ppermute | solution.py:562
  47.0 0.0 collective-permute-done.7.rest_1_
  47.0 0.0 copy-done.5
  47.0 4.9 %gradients.1 = f32[1,2,4,64]{3,2,1,0:T(4,128)} custom-call(s32[1,1,64]{2,1,0:T(1,128)S(1)} %bitcast.18, f32[2,2,9]{2,1,0:T(2,128)S(1)} %copy-done.1, bf16[2,128,128]{2,1,0:T(8,128)(2,1)S(1)} %get-tuple-element.36.rest_0_, bf16[2,128,128]{2,1,0:T(8,128)(2,1)S(1)} %collective-permute-done.7.rest_1_, bf16[2,128,128]{2,1,0:T(8,128)(2,1)S(1)} %collective-permute-done.8.rest_2_, ...), custom_call_target="tpu_custom_call" | custom-call | flops 4000000000 | bytes 20000000 | tf_op jit(solution)/shard_map/gradients/pallas_call | solution.py:542
Async XLA Ops:
  0.6 12.8 %copy-start.2 = (bf16[1,64,128,128]{3,2,1,0:T(8,128)(2,1)S(1)}, bf16[1,64,128,128]{3,2,1,0:T(8,128)(2,1)}, u32[]{:S(2)}) copy-start(bf16[1,64,128,128]{3,2,1,0:T(8,128)(2,1)} %param.9) | copy-start | bytes 6291460
  0.6 12.8 %copy-start.3 = (s32[1,64,128]{2,1,0:T(8,128)S(1)}, s32[1,64,128]{2,1,0:T(8,128)}, u32[]{:S(2)}) copy-start(s32[1,64,128]{2,1,0:T(8,128)} %param.12) | copy-start | bytes 98308
  0.7 12.8 %copy-start.4 = (s32[1,64,2,4]{1,3,2,0:T(4,128)S(1)}, s32[1,64,2,4]{1,3,2,0:T(4,128)}, u32[]{:S(2)}) copy-start(s32[1,64,2,4]{1,3,2,0:T(4,128)} %param.11) | copy-start | bytes 6148
  0.7 12.8 %copy-start.6 = (f32[22,8,128]{2,1,0:T(8,128)S(1)}, f32[22,8,128]{2,1,0:T(8,128)}, u32[]{:S(2)}) copy-start(f32[22,8,128]{2,1,0:T(8,128)} %constant.6.clone.coef_ref) | copy-start | bytes 270340
  0.7 12.8 %copy-start.7 = (bf16[128,128]{1,0:T(8,128)(2,1)S(1)}, bf16[128,128]{1,0:T(8,128)(2,1)}, u32[]{:S(2)}) copy-start(bf16[128,128]{1,0:T(8,128)(2,1)} %constant.8.clone.near_ref) | copy-start | bytes 98308
  0.7 12.8 %copy-start.8 = (s32[3,8,128]{2,1,0:T(8,128)S(1)}, s32[3,8,128]{2,1,0:T(8,128)}, u32[]{:S(2)}) copy-start(s32[3,8,128]{2,1,0:T(8,128)} %constant.7.clone.rows_ref) | copy-start | bytes 36868
  10.5 7.4 %copy-start.1 = (f32[2,2,9]{2,1,0:T(2,128)S(1)}, f32[2,2,9]{2,1,0:T(2,128)}, u32[]{:S(2)}) copy-start(f32[2,2,9]{2,1,0:T(2,128)} %psf_ref.3) | copy-start | bytes 436
  10.5 9.5 %copy-start = (f32[4,2,128,128]{3,2,1,0:T(8,128)S(1)}, f32[4,2,128,128]{3,2,1,0:T(8,128)}, u32[]{:S(2)}) copy-start(f32[4,2,128,128]{3,2,1,0:T(8,128)} %get-tuple-element.27.keep_ref) | copy-start | bytes 1572868
  10.5 9.5 %collective-permute-start = (bf16[4,2,128,128]{3,2,1,0:T(8,128)(2,1)}, bf16[4,2,128,128]{3,2,1,0:T(8,128)(2,1)S(1)}, u32[]{:S(2)}, u32[]{:S(2)}) collective-permute-start(bf16[4,2,128,128]{3,2,1,0:T(8,128)(2,1)} %get-tuple-element.28), channel_id=1, source_target_pairs={{0,16},{16,0},{1,17},{17,1},{2,18},{18,2},{3,19},{19,3},{4,20},{20... | collective-permute-start | bytes 786440 | tf_op jit(solution)/shard_map/ppermute | solution.py:558
  20.7 8.9 %collective-permute-start.1 = (bf16[2,128,128]{2,1,0:T(8,128)(2,1)S(1)}, bf16[2,128,128]{2,1,0:T(8,128)(2,1)S(1)}, u32[]{:S(2)}, u32[]{:S(2)}) collective-permute-start(bf16[2,128,128]{2,1,0:T(8,128)(2,1)S(1)} %get-tuple-element.31), channel_id=1, source_target_pairs={{0,4},{4,8},{8,12},{12,0},{1,5},{5,9},{9,13},{13,1},{2,6},{6,10},{... | collective-permute-start | bytes 196616 | tf_op jit(solution)/shard_map/ppermute | solution.py:562
  22.6 7.0 %collective-permute-start.2 = (bf16[2,128,128]{2,1,0:T(8,128)(2,1)S(1)}, bf16[2,128,128]{2,1,0:T(8,128)(2,1)S(1)}, u32[]{:S(2)}, u32[]{:S(2)}) collective-permute-start(bf16[2,128,128]{2,1,0:T(8,128)(2,1)S(1)} %get-tuple-element.32), channel_id=1, source_target_pairs={{0,8},{4,12},{8,0},{12,4},{1,9},{5,13},{9,1},{13,5},{2,10},{6,14},... | collective-permute-start | bytes 196616 | tf_op jit(solution)/shard_map/ppermute | solution.py:562
  25.2 4.5 %collective-permute-start.3 = (bf16[2,128,128]{2,1,0:T(8,128)(2,1)S(1)}, bf16[2,128,128]{2,1,0:T(8,128)(2,1)S(1)}, u32[]{:S(2)}, u32[]{:S(2)}) collective-permute-start(bf16[2,128,128]{2,1,0:T(8,128)(2,1)S(1)} %get-tuple-element.33), channel_id=1, source_target_pairs={{0,12},{4,0},{8,4},{12,8},{1,13},{5,1},{9,5},{13,9},{2,14},{6,2},{... | collective-permute-start | bytes 196616 | tf_op jit(solution)/shard_map/ppermute | solution.py:562
  30.5 5.6 %collective-permute-start.4 = (f32[128,128]{1,0:T(8,128)S(1)}, f32[128,128]{1,0:T(8,128)S(1)}, u32[]{:S(2)}, u32[]{:S(2)}) collective-permute-start(f32[128,128]{1,0:T(8,128)S(1)} %get-tuple-element.34.own_ref), channel_id=1, source_target_pairs={{0,16},{16,0},{1,17},{17,1},{2,18},{18,2},{3,19},{19,3},{4,20},{20... | collective-permute-start | bytes 196616 | tf_op jit(solution)/shard_map/ppermute | solution.py:558
  32.2 3.9 %collective-permute-start.6 = (bf16[16,128]{1,0:T(8,128)(2,1)S(1)}, bf16[16,128]{1,0:T(8,128)(2,1)S(1)}, u32[]{:S(2)}, u32[]{:S(2)}) collective-permute-start(bf16[16,128]{1,0:T(8,128)(2,1)S(1)} %get-tuple-element.35), channel_id=1, source_target_pairs={{0,19},{1,16},{2,17},{3,18},{16,1},{17,2},{18,3},{19,0},{4,23},{5,... | collective-permute-start | bytes 12296 | tf_op jit(solution)/shard_map/ppermute | solution.py:568
  32.2 3.9 %collective-permute-start.5 = (bf16[16,128]{1,0:T(8,128)(2,1)S(1)}, bf16[16,128]{1,0:T(8,128)(2,1)S(1)}, u32[]{:S(2)}, u32[]{:S(2)}) collective-permute-start(bf16[16,128]{1,0:T(8,128)(2,1)S(1)} %get-tuple-element.35), channel_id=1, source_target_pairs={{0,3},{1,0},{2,1},{3,2},{16,17},{17,18},{18,19},{19,16},{4,7},{5,4... | collective-permute-start | bytes 12296 | tf_op jit(solution)/shard_map/ppermute | solution.py:568
  37.5 9.4 %copy-start.5 = (s32[1,64,1]{1,2,0:T(1,128)S(1)}, s32[1,64,1]{1,2,0:T(1,128)}, u32[]{:S(2)}) copy-start(s32[1,64,1]{1,2,0:T(1,128)} %param.10) | copy-start | bytes 772
  37.5 7.7 %collective-permute-start.9 = (bf16[2,128,128]{2,1,0:T(8,128)(2,1)S(1)}, bf16[2,128,128]{2,1,0:T(8,128)(2,1)S(1)}, u32[]{:S(2)}, u32[]{:S(2)}) collective-permute-start(bf16[2,128,128]{2,1,0:T(8,128)(2,1)S(1)} %get-tuple-element.36.rest_0_), channel_id=1, source_target_pairs={{0,12},{4,0},{8,4},{12,8},{1,13},{5,1},{9,5},{13,9},{2,14},{6,2},{... | collective-permute-start | bytes 196616 | tf_op jit(solution)/shard_map/ppermute | solution.py:562
  40.3 6.6 %collective-permute-start.8 = (bf16[2,128,128]{2,1,0:T(8,128)(2,1)S(1)}, bf16[2,128,128]{2,1,0:T(8,128)(2,1)S(1)}, u32[]{:S(2)}, u32[]{:S(2)}) collective-permute-start(bf16[2,128,128]{2,1,0:T(8,128)(2,1)S(1)} %get-tuple-element.36.rest_0_), channel_id=1, source_target_pairs={{0,8},{4,12},{8,0},{12,4},{1,9},{5,13},{9,1},{13,5},{2,10},{6,14},... | collective-permute-start | bytes 196616 | tf_op jit(solution)/shard_map/ppermute | solution.py:562
  40.3 6.6 %collective-permute-start.7 = (bf16[2,128,128]{2,1,0:T(8,128)(2,1)S(1)}, bf16[2,128,128]{2,1,0:T(8,128)(2,1)S(1)}, u32[]{:S(2)}, u32[]{:S(2)}) collective-permute-start(bf16[2,128,128]{2,1,0:T(8,128)(2,1)S(1)} %get-tuple-element.36.rest_0_), channel_id=1, source_target_pairs={{0,4},{4,8},{8,12},{12,0},{1,5},{5,9},{9,13},{13,1},{2,6},{6,10},{... | collective-permute-start | bytes 196616 | tf_op jit(solution)/shard_map/ppermute | solution.py:562

commit v6 on v5

--- a/solution.py
+++ b/solution.py
@@ -13,7 +13,7 @@
 DEGREE = 10
 F32 = jnp.float32
 BF16 = jnp.bfloat16
-GROUP1 = 8
+GROUP1 = 16
 STEP2 = 8
 LAG2 = (0, 4, 8, 12)
 GROUP3 = 8
@@ -151,14 +151,26 @@
                 (tap_y,), whole_y = taps_of(affine_ref[0, k, 1, b], affine_ref[0, k, 3, b], coef_ref, False)
                 (tap_x,), whole_x = taps_of(affine_ref[0, k, 0, b], affine_ref[0, k, 2, b], coef_ref, False)
                 work.append([b, k, mask_row, masked, tap_y, whole_y, tap_x, whole_x])
+        zero = jnp.zeros((side, side), BF16)
+
+        def corner(a, c):
+            return jnp.concatenate([jnp.concatenate([a, zero], axis=1), jnp.concatenate([zero, c], axis=1)], axis=0)
+
+        duos = [(work[4 * g + k], work[4 * g + 2 + k]) for g in range(GROUP1 // 2) for k in range(2)]
         passes = []
-        for b, k, mask_row, masked, tap_y, whole_y, tap_x, whole_x in work:
-            (ly_t,) = spread([tap_y], whole_y, rows_ref, near_ref)
-            passes.append(dot_t(ly_t, masked).astype(BF16))
-        warps = []
-        for (b, k, mask_row, masked, tap_y, whole_y, tap_x, whole_x), row_pass in zip(work, passes):
-            (lx_t,) = spread([tap_x], whole_x, rows_ref, near_ref)
-            warps.append(dot(jnp.concatenate([row_pass, mask_rows(mask_row)], axis=0), lx_t))
+        for one, two in duos:
+            (ly_a,) = spread([one[4]], one[5], rows_ref, near_ref)
+            (ly_b,) = spread([two[4]], two[5], rows_ref, near_ref)
+            both = dot_t(jnp.concatenate([ly_a, ly_b], axis=0), corner(one[3], two[3]))
+            passes.append(both.astype(BF16))
+        warps = {}
+        for (one, two), row_pass in zip(duos, passes):
+            (lx_a,) = spread([one[6]], one[7], rows_ref, near_ref)
+            (lx_b,) = spread([two[6]], two[7], rows_ref, near_ref)
+            extra = jnp.concatenate([mask_rows(one[2]), mask_rows(two[2])], axis=1)
+            both = dot(jnp.concatenate([row_pass, extra], axis=0), corner(lx_a, lx_b))
+            warps[id(one)], warps[id(two)] = both[:, :side], both[:, side:]
+        warps = [warps[id(item)] for item in work]
         for (b, k, mask_row, masked, tap_y, whole_y, tap_x, whole_x), both in zip(work, warps):
             tile = target_ref[0, 0, b]
             weight = weight_ref[0, b]
@@ -408,7 +420,7 @@
     return jnp.concatenate([high, (total - high.astype(F32)).astype(BF16)], axis=1)
 
 
-def bands_kernel(psf_ref, after_ref, inner_ref, outer_ref, token_ref):
+def bands_kernel(psf_ref, after_ref, inner_ref, outer_ref, rows_ref, token_ref):
     token_ref[0] = after_ref[0]
     side = inner_ref.shape[1]
     along = lax.broadcasted_iota(jnp.int32, (side, side), 0)
@@ -419,15 +431,23 @@
         taps = [psf_ref[k, 1, q] for q in range(TAPS)]
         inner_ref[k] = band_of(taps, along - across + RAD)
         outer_ref[k] = band_of(taps, edge - across[:16] + RAD)
+        wide = (side, side + 32)
+        below = lax.broadcasted_iota(jnp.int32, wide, 1) - lax.broadcasted_iota(jnp.int32, wide, 0) - 16 + RAD
+        total = jnp.zeros(wide, F32)
+        for q in range(TAPS):
+            total = jnp.where(below == q, psf_ref[k, 0, q], total)
+        high = total.astype(BF16)
+        rows_ref[k, 0:side, :] = high
+        rows_ref[k, side : 2 * side, :] = (total - high.astype(F32)).astype(BF16)
 
 
 def bands_of(psf, after, side=128):
     return pl.pallas_call(
         bands_kernel,
         out_shape=[jax.ShapeDtypeStruct((2, rows, 2 * side), BF16) for rows in (side, 16)]
-        + [jax.ShapeDtypeStruct((1,), jnp.int32)],
+        + [jax.ShapeDtypeStruct((2, 2 * side, side + 32), BF16), jax.ShapeDtypeStruct((1,), jnp.int32)],
         in_specs=[smem(), smem()],
-        out_specs=[vmem(), vmem(), smem()],
+        out_specs=[vmem(), vmem(), vmem(), smem()],
         compiler_params=pltpu.CompilerParams(vmem_limit_bytes=TINY_BYTES),
         name="bands",
     )(psf, after)
@@ -486,31 +506,24 @@
     )(*bands, tiles, edges)
 
 
-def gradient_kernel(tiles, target_ref, psf_ref, *rest):
+def gradient_kernel(tiles, target_ref, band_ref, *rest):
     skies = rest[:tiles]
     chunk_refs, (out_ref, smooth, model) = rest[tiles:-3], rest[-3:]
     side = 128
     for k in range(2):
-        smooth[k, 0:8, :] = jnp.zeros((8, side), F32)
-        smooth[k, 8 + tiles * side : 16 + tiles * side, :] = jnp.zeros((8, side), F32)
+        smooth[k, 0:16, :] = jnp.zeros((16, side), BF16)
+        smooth[k, 16 + tiles * side : 32 + tiles * side, :] = jnp.zeros((16, side), BF16)
         for turn in range(tiles):
             tile = lax.rem(lax.axis_index("tx") + tiles - turn, tiles)
-            smooth[k, pl.ds(pl.multiple_of(8 + tile * side, 8), side), :] = skies[turn][k].astype(F32)
-        chunk = 64
-
-        def rows(c, carry, k=k):
-            start = pl.multiple_of(c * chunk, chunk)
-            seen = smooth[k, pl.ds(start, chunk + 16), :]
-            total = psf_ref[k, 0, 0] * seen[4 : 4 + chunk]
-            for p in range(1, TAPS):
-                total = total + psf_ref[k, 0, p] * seen[4 + p : 4 + p + chunk]
-            model[k, pl.ds(start, chunk), :] = total.astype(BF16).astype(F32)
-            return carry
-
-        lax.fori_loop(0, tiles * side // chunk, rows, 0, unroll=2)
-
-    lane = lax.broadcasted_iota(jnp.int32, out_ref.shape[1:], 2)
-    gathered = jnp.zeros(out_ref.shape[1:], F32)
+            smooth[k, pl.ds(pl.multiple_of(16 + tile * side, 16), side), :] = skies[turn][k]
+        for tile in range(tiles):
+            both = dot(band_ref[k], smooth[k, tile * side : (tile + 1) * side + 32, :])
+            total = both[:side] + both[side:]
+            model[k, tile * side : (tile + 1) * side, :] = total.astype(BF16).astype(F32)
+
+    count = out_ref.shape[3]
+    lane = lax.broadcasted_iota(jnp.int32, (8, count), 1)
+    gathered = jnp.zeros((8, count), F32)
     first = 0
     for slope_ref, part_ref in zip(chunk_refs[::2], chunk_refs[1::2]):
 
@@ -527,31 +540,32 @@
                 found.append((j, rows))
             for j, rows in found:
                 total = jnp.sum(part_ref[j] - jnp.concatenate(rows, axis=0), axis=1, keepdims=True) * (1.0 / side)
-                gathered = jnp.where(lane == first + j, total.reshape(2, 4, 1), gathered)
+                gathered = jnp.where(lane == first + j, total, gathered)
             return gathered
 
         gathered = lax.fori_loop(0, slope_ref.shape[0] // GROUP3, body, gathered)
         first += slope_ref.shape[0]
-    out_ref[0] = gathered
-
-
-def gradients_of(target, psf, skies, chunks):
+    out_ref[0, 0] = gathered[0:4]
+    out_ref[0, 1] = gathered[4:8]
+
+
+def gradients_of(target, row_bands, skies, chunks):
     side = skies[0].shape[1]
     tiles, count = len(skies), target.shape[2]
     arrays = [array for pair_of in chunks for array in pair_of]
     return pl.pallas_call(
         functools.partial(gradient_kernel, tiles),
         out_shape=jax.ShapeDtypeStruct((1, 2, 4, count), F32),
-        in_specs=[smem(), smem()] + [vmem()] * (tiles + len(arrays)),
+        in_specs=[smem()] + [vmem()] * (1 + tiles + len(arrays)),
         out_specs=vmem(),
         scratch_shapes=[
-            pltpu.VMEM((2, tiles * side + 16, side), F32),
+            pltpu.VMEM((2, tiles * side + 32, side), BF16),
             pltpu.VMEM((2, tiles * side, side), F32),
         ],
         compiler_params=pltpu.CompilerParams(vmem_limit_bytes=SMALL_BYTES),
         cost_estimate=pl.CostEstimate(flops=int(4e9), bytes_accessed=int(20e6), transcendentals=0),
         name="gradients",
-    )(target, psf, *skies, *arrays)
+    )(target, row_bands, *skies, *arrays)
 
 
 def swap(cells):
@@ -588,7 +602,7 @@
         first += size * scale
     if small:
         keep, send = sums
-        *bands, token = bands_of(psf, tokens[0])
+        *bands, row_bands, token = bands_of(psf, tokens[0])
         totals = pair(keep, swap(send), token)
         got = [totals[0]] + [turned(totals[dz], dz, tiles) for dz in range(1, tiles)]
         piece, edge = coadd_of(tokens[1], got)
@@ -606,10 +620,11 @@
         flipped = jnp.swapaxes(both, 1, 2).astype(BF16)
         left = lax.ppermute(flipped[:, side - 8 :], "ty", [(y, y + 1) for y in range(columns - 1)])
         right = lax.ppermute(flipped[:, :8], "ty", [(y + 1, y) for y in range(columns - 1)])
-        sky = whole_sky(bands_of(psf, tokens[0])[:2], both, jnp.concatenate([left, right], axis=1))
+        *bands, row_bands, _ = bands_of(psf, tokens[0])
+        sky = whole_sky(bands, both, jnp.concatenate([left, right], axis=1))
         gathered = lax.all_gather(sky, "tx", axis=0)
         skies = [lax.dynamic_index_in_dim(gathered, (me + tiles - turn) % tiles, 0, False) for turn in range(tiles)]
-    gradients = gradients_of(block_tile, psf, skies, chunks)
+    gradients = gradients_of(block_tile, row_bands, skies, chunks)
     return gradients.transpose(0, 3, 1, 2), coadd_tile
 
 

time: 52.2 us -> 49.8 us (0.954)
  Pallas kernels: 31.1 us -> 28.8 us
    pallas_call x1, Pallas kernels: 9.76 us -> 7.74 us  [tile_sums(): pl.pallas_call(functools.partial(sums_kernel, tiles, packed, step_blocks)...]
  transfers between devices with their start and end apart: 10 -> 10, of which waited for: 4 -> 4; matrix products, arithmetic and copies ran while one was open for 0% -> 0% of each run, Pallas kernels for 26% -> 27%
where the time goes in v6:
time: 49.8 us; the launch traced here: 49.6 us
  Pallas kernels  28.8 us (58%)
  starting transfers between devices  15.6 us (31%)
  waiting for transfers between devices  4.37 us (9%)
  between operations  0.79 us (2%)
    pallas_call x3, Pallas kernels, slopes_of(): pl.pallas_call(functools.partial(slopes_kernel, step_blocks, start), grid...  11.7 us
    ppermute x6, starting transfers between devices, turned(): lax.ppermute(cells, 'tx', [(z, (z + dz) % tiles) for z in range(tiles)])  9.16 us
    pallas_call x1, Pallas kernels, tile_sums(): pl.pallas_call(functools.partial(sums_kernel, tiles, packed, step_blocks)...  7.74 us
    ppermute x2, starting transfers between devices, swap(): return lax.ppermute(cells, 'exp', [(0, 1), (1, 0)])  4.66 us
    pallas_call x1, Pallas kernels, gradients_of(): pl.pallas_call(functools.partial(gradient_kernel, tiles), out_shape=jax.S...  4.65 us
    ppermute x2, waiting for transfers between devices, to_sides(): return lax.ppermute(edge, ('exp', 'ty'), perm)  2.16 us
    ppermute x6, waiting for transfers between devices, turned(): lax.ppermute(cells, 'tx', [(z, (z + dz) % tiles) for z in range(tiles)])  1.84 us
    ppermute x2, starting transfers between devices, to_sides(): return lax.ppermute(edge, ('exp', 'ty'), perm)  1.78 us
  transfers between devices with their start and end apart: 10, of which 4 were waited for; matrix products, arithmetic and copies ran while one was open for 0% of the time, Pallas kernels for 27%

profile of v6, /device:TPU:0, one launch (start us, length us, event | category | flops | bytes accessed | tf_op | source)
XLA Modules:
  0.0 49.6 jit_solution(2128860057741517023)
XLA Ops:
  0.6 0.0 copy-start.2
  0.6 0.0 copy-start.3
  0.7 0.0 copy-start.4
  0.7 0.0 copy-start.6
  0.7 0.0 copy-start.7
  0.7 0.0 copy-start.8
  0.7 7.7 %tile_sums.1 = (f32[4,2,128,128]{3,2,1,0:T(8,128)}, bf16[4,2,128,128]{3,2,1,0:T(8,128)(2,1)}) custom-call(s32[1,2,4,64]{3,2,1,0:T(4,128)} %bitcast.13, s32[1,1,64]{2,1,0:T(1,128)} %bitcast.17, f32[1,64]{1,0:T(1,128)} %weight_ref.1, f32[22,8,128]{2,1,0:T(8,128)} %constant.6.clone.coef_ref, s32[3,8,128]{2,1,0:T(8,128)} %constant.7.clone.rows_ref, ...), custom_call_target="tpu_custom_call" | custom-call | flops 8000000000 | bytes 3000000 | tf_op jit(solution)/shard_map/tile_sums/pallas_call | solution.py:241
  8.4 0.0 copy-start.1
  8.4 0.0 copy-start
  8.4 3.0 %collective-permute-start = (bf16[4,2,128,128]{3,2,1,0:T(8,128)(2,1)}, bf16[4,2,128,128]{3,2,1,0:T(8,128)(2,1)S(1)}, u32[]{:S(2)}, u32[]{:S(2)}) collective-permute-start(bf16[4,2,128,128]{3,2,1,0:T(8,128)(2,1)} %get-tuple-element.30), channel_id=1, source_target_pairs={{0,16},{16,0},{1,17},{17,1},{2,18},{18,2},{3,19},{19,3},{4,20},{20... | collective-permute-start | bytes 786440 | tf_op jit(solution)/shard_map/ppermute | solution.py:572
  11.4 0.0 copy-done.2
  11.4 0.0 copy-done.3
  11.5 0.0 copy-done.4
  11.5 0.0 copy-done.6
  11.5 0.0 copy-done.7
  11.5 0.0 copy-done.8
  11.5 4.4 %slopes.3 = (bf16[24,4,128,128]{3,2,1,0:T(8,128)(2,1)S(1)}, f32[24,8,128]{2,1,0:T(8,128)S(1)}, s32[1]{0:T(128)}) custom-call(s32[1,2,4,64]{3,2,1,0:T(4,128)S(1)} %bitcast.14, f32[22,8,128]{2,1,0:T(8,128)S(1)} %copy-done.6, s32[3,8,128]{2,1,0:T(8,128)S(1)} %copy-done.8, bf16[128,128]{1,0:T(8,128)(2,1)S(1)} %copy-done.7, s32[64,128]{1,0:T(8,128)S(1)} %bitcast.10, ...), custom_call_target="tpu_custom_call" | custom-call | flops 3600000000 | bytes 7200000 | tf_op jit(solution)/shard_map/slopes/pallas_call | solution.py:359
  15.8 0.0 copy-done.1
  15.8 1.7 %bands.1 = (bf16[2,128,256]{2,1,0:T(8,128)(2,1)S(1)}, bf16[2,16,256]{2,1,0:T(8,128)(2,1)S(1)}, bf16[2,256,160]{2,1,0:T(8,128)(2,1)S(1)}, s32[1]{0:T(128)}) custom-call(f32[2,2,9]{2,1,0:T(2,128)S(1)} %copy-done.1, s32[1]{0:T(128)} %get-tuple-element.24.after_ref), custom_call_target="tpu_custom_call" | custom-call | tf_op jit(solution)/shard_map/bands/pallas_call | solution.py:445
  17.6 0.4 collective-permute-done.got_ref
  18.0 0.0 copy-done
  18.0 0.7 %pair.1 = (f32[2,128,128]{2,1,0:T(8,128)S(1)}, bf16[2,128,128]{2,1,0:T(8,128)(2,1)S(1)}, bf16[2,128,128]{2,1,0:T(8,128)(2,1)S(1)}, bf16[2,128,128]{2,1,0:T(8,128)(2,1)S(1)}) custom-call(f32[4,2,128,128]{3,2,1,0:T(8,128)S(1)} %copy-done, bf16[4,2,128,128]{3,2,1,0:T(8,128)(2,1)S(1)} %collective-permute-done.got_ref, s32[1]{0:T(128)} %get-tuple-element.31.after_ref), custom_call_target="tpu_custom_call" | custom-call | tf_op jit(solution)/shard_map/pair/pallas_call | solution.py:276
  18.7 1.9 %collective-permute-start.1 = (bf16[2,128,128]{2,1,0:T(8,128)(2,1)S(1)}, bf16[2,128,128]{2,1,0:T(8,128)(2,1)S(1)}, u32[]{:S(2)}, u32[]{:S(2)}) collective-permute-start(bf16[2,128,128]{2,1,0:T(8,128)(2,1)S(1)} %get-tuple-element.33), channel_id=1, source_target_pairs={{0,4},{4,8},{8,12},{12,0},{1,5},{5,9},{9,13},{13,1},{2,6},{6,10},{... | collective-permute-start | bytes 196616 | tf_op jit(solution)/shard_map/ppermute | solution.py:576
  20.5 2.6 %collective-permute-start.2 = (bf16[2,128,128]{2,1,0:T(8,128)(2,1)S(1)}, bf16[2,128,128]{2,1,0:T(8,128)(2,1)S(1)}, u32[]{:S(2)}, u32[]{:S(2)}) collective-permute-start(bf16[2,128,128]{2,1,0:T(8,128)(2,1)S(1)} %get-tuple-element.34), channel_id=1, source_target_pairs={{0,8},{4,12},{8,0},{12,4},{1,9},{5,13},{9,1},{13,5},{2,10},{6,14},... | collective-permute-start | bytes 196616 | tf_op jit(solution)/shard_map/ppermute | solution.py:576
  23.1 1.3 %collective-permute-start.3 = (bf16[2,128,128]{2,1,0:T(8,128)(2,1)S(1)}, bf16[2,128,128]{2,1,0:T(8,128)(2,1)S(1)}, u32[]{:S(2)}, u32[]{:S(2)}) collective-permute-start(bf16[2,128,128]{2,1,0:T(8,128)(2,1)S(1)} %get-tuple-element.35), channel_id=1, source_target_pairs={{0,12},{4,0},{8,4},{12,8},{1,13},{5,1},{9,5},{13,9},{2,14},{6,2},{... | collective-permute-start | bytes 196616 | tf_op jit(solution)/shard_map/ppermute | solution.py:576
  24.5 3.1 %slopes.4 = (bf16[16,4,128,128]{3,2,1,0:T(8,128)(2,1)S(1)}, f32[16,8,128]{2,1,0:T(8,128)S(1)}, s32[1]{0:T(128)}) custom-call(s32[1,2,4,64]{3,2,1,0:T(4,128)S(1)} %bitcast.15, f32[22,8,128]{2,1,0:T(8,128)S(1)} %copy-done.6, s32[3,8,128]{2,1,0:T(8,128)S(1)} %copy-done.8, bf16[128,128]{1,0:T(8,128)(2,1)S(1)} %copy-done.7, s32[64,128]{1,0:T(8,128)S(1)} %bitcast.11, ...), custom_call_target="tpu_custom_call" | custom-call | flops 2400000000 | bytes 4800000 | tf_op jit(solution)/shard_map/slopes/pallas_call | solution.py:359
  27.6 0.0 collective-permute-done.1.refs_1_
  27.6 0.0 collective-permute-done.2.refs_2_
  27.6 0.1 collective-permute-done.3.refs_3_
  27.7 0.8 %coadd.1 = (f32[128,128]{1,0:T(8,128)S(1)}, bf16[16,128]{1,0:T(8,128)(2,1)S(1)}) custom-call(s32[1]{0:T(128)} %get-tuple-element.28.after_ref, f32[2,128,128]{2,1,0:T(8,128)S(1)} %get-tuple-element.32.refs_0_, bf16[2,128,128]{2,1,0:T(8,128)(2,1)S(1)} %collective-permute-done.1.refs_1_, bf16[2,128,128]{2,1,0:T(8,128)(2,1)S(1)} %collective-permute-done.2.refs_2_, ...), custom_call_target="tpu_custom_call" | custom-call | tf_op jit(solution)/shard_map/coadd/pallas_call | solution.py:405
  28.5 1.7 %collective-permute-start.4 = (f32[128,128]{1,0:T(8,128)S(1)}, f32[128,128]{1,0:T(8,128)S(1)}, u32[]{:S(2)}, u32[]{:S(2)}) collective-permute-start(f32[128,128]{1,0:T(8,128)S(1)} %get-tuple-element.36.own_ref), channel_id=1, source_target_pairs={{0,16},{16,0},{1,17},{17,1},{2,18},{18,2},{3,19},{19,3},{4,20},{20... | collective-permute-start | bytes 196616 | tf_op jit(solution)/shard_map/ppermute | solution.py:572
  30.1 0.0 collective-permute-start.6
  30.1 1.8 %collective-permute-start.5 = (bf16[16,128]{1,0:T(8,128)(2,1)S(1)}, bf16[16,128]{1,0:T(8,128)(2,1)S(1)}, u32[]{:S(2)}, u32[]{:S(2)}) collective-permute-start(bf16[16,128]{1,0:T(8,128)(2,1)S(1)} %get-tuple-element.37), channel_id=1, source_target_pairs={{0,3},{1,0},{2,1},{3,2},{16,17},{17,18},{18,19},{19,16},{4,7},{5,4... | collective-permute-start | bytes 12296 | tf_op jit(solution)/shard_map/ppermute | solution.py:582
  31.9 2.2 %collective-permute-done.6.far_ref = bf16[16,128]{1,0:T(8,128)(2,1)S(1)} collective-permute-done((bf16[16,128]{1,0:T(8,128)(2,1)S(1)}, bf16[16,128]{1,0:T(8,128)(2,1)S(1)}, u32[]{:S(2)}, u32[]{:S(2)}) %collective-permute-start.6) | collective-permute-done | bytes 4128 | tf_op jit(solution)/shard_map/ppermute | solution.py:582
  34.1 0.0 collective-permute-done.5.edge_ref
  34.1 0.0 collective-permute-done.4.other_ref
  34.1 1.4 %join.1 = (bf16[2,128,128]{2,1,0:T(8,128)(2,1)S(1)}, f32[128,128]{1,0:T(8,128)}) custom-call(bf16[2,128,256]{2,1,0:T(8,128)(2,1)S(1)} %get-tuple-element.26.inner_ref, bf16[2,16,256]{2,1,0:T(8,128)(2,1)S(1)} %get-tuple-element.27.outer_ref, f32[128,128]{1,0:T(8,128)S(1)} %get-tuple-element.36.own_ref, f32[128,128]{1,0:T(8,128)S(1)} %collective-permute-done.4.other_ref, ...), custom_call_target="tpu_custom_call" | custom-call | tf_op jit(solution)/shard_map/join/pallas_call | solution.py:483
  35.5 0.0 copy-start.5
  35.5 2.8 %collective-permute-start.9 = (bf16[2,128,128]{2,1,0:T(8,128)(2,1)S(1)}, bf16[2,128,128]{2,1,0:T(8,128)(2,1)S(1)}, u32[]{:S(2)}, u32[]{:S(2)}) collective-permute-start(bf16[2,128,128]{2,1,0:T(8,128)(2,1)S(1)} %get-tuple-element.38.rest_0_), channel_id=1, source_target_pairs={{0,12},{4,0},{8,4},{12,8},{1,13},{5,1},{9,5},{13,9},{2,14},{6,2},{... | collective-permute-start | bytes 196616 | tf_op jit(solution)/shard_map/ppermute | solution.py:576
  38.3 0.0 collective-permute-start.8
  38.3 0.6 %collective-permute-start.7 = (bf16[2,128,128]{2,1,0:T(8,128)(2,1)S(1)}, bf16[2,128,128]{2,1,0:T(8,128)(2,1)S(1)}, u32[]{:S(2)}, u32[]{:S(2)}) collective-permute-start(bf16[2,128,128]{2,1,0:T(8,128)(2,1)S(1)} %get-tuple-element.38.rest_0_), channel_id=1, source_target_pairs={{0,4},{4,8},{8,12},{12,0},{1,5},{5,9},{9,13},{13,1},{2,6},{6,10},{... | collective-permute-start | bytes 196616 | tf_op jit(solution)/shard_map/ppermute | solution.py:576
  38.9 4.3 %slopes.5 = (bf16[24,4,128,128]{3,2,1,0:T(8,128)(2,1)S(1)}, f32[24,8,128]{2,1,0:T(8,128)S(1)}, s32[1]{0:T(128)}) custom-call(s32[1,2,4,64]{3,2,1,0:T(4,128)S(1)} %bitcast.16, f32[22,8,128]{2,1,0:T(8,128)S(1)} %copy-done.6, s32[3,8,128]{2,1,0:T(8,128)S(1)} %copy-done.8, bf16[128,128]{1,0:T(8,128)(2,1)S(1)} %copy-done.7, s32[64,128]{1,0:T(8,128)S(1)} %bitcast.12, ...), custom_call_target="tpu_custom_call" | custom-call | flops 3600000000 | bytes 7200000 | tf_op jit(solution)/shard_map/slopes/pallas_call | solution.py:359
  43.2 0.0 collective-permute-done.9.rest_3_
  43.2 1.8 %collective-permute-done.8.rest_2_ = bf16[2,128,128]{2,1,0:T(8,128)(2,1)S(1)} collective-permute-done((bf16[2,128,128]{2,1,0:T(8,128)(2,1)S(1)}, bf16[2,128,128]{2,1,0:T(8,128)(2,1)S(1)}, u32[]{:S(2)}, u32[]{:S(2)}) %collective-permute-start.8) | collective-permute-done | bytes 65568 | tf_op jit(solution)/shard_map/ppermute | solution.py:576
  44.9 0.0 collective-permute-done.7.rest_1_
  44.9 0.0 copy-done.5
  45.0 4.6 %gradients.1 = f32[1,2,4,64]{3,2,1,0:T(4,128)} custom-call(s32[1,1,64]{2,1,0:T(1,128)S(1)} %bitcast.18, bf16[2,256,160]{2,1,0:T(8,128)(2,1)S(1)} %get-tuple-element.25.band_ref, bf16[2,128,128]{2,1,0:T(8,128)(2,1)S(1)} %get-tuple-element.38.rest_0_, bf16[2,128,128]{2,1,0:T(8,128)(2,1)S(1)} %collective-permute-done.7.rest_1_, ...), custom_call_target="tpu_custom_call" | custom-call | flops 4000000000 | bytes 20000000 | tf_op jit(solution)/shard_map/gradients/pallas_call | solution.py:556
Async XLA Ops:
  0.6 10.8 %copy-start.2 = (bf16[1,64,128,128]{3,2,1,0:T(8,128)(2,1)S(1)}, bf16[1,64,128,128]{3,2,1,0:T(8,128)(2,1)}, u32[]{:S(2)}) copy-start(bf16[1,64,128,128]{3,2,1,0:T(8,128)(2,1)} %param.9) | copy-start | bytes 6291460
  0.6 10.8 %copy-start.3 = (s32[1,64,128]{2,1,0:T(8,128)S(1)}, s32[1,64,128]{2,1,0:T(8,128)}, u32[]{:S(2)}) copy-start(s32[1,64,128]{2,1,0:T(8,128)} %param.12) | copy-start | bytes 98308
  0.7 10.8 %copy-start.4 = (s32[1,64,2,4]{1,3,2,0:T(4,128)S(1)}, s32[1,64,2,4]{1,3,2,0:T(4,128)}, u32[]{:S(2)}) copy-start(s32[1,64,2,4]{1,3,2,0:T(4,128)} %param.11) | copy-start | bytes 6148
  0.7 10.8 %copy-start.6 = (f32[22,8,128]{2,1,0:T(8,128)S(1)}, f32[22,8,128]{2,1,0:T(8,128)}, u32[]{:S(2)}) copy-start(f32[22,8,128]{2,1,0:T(8,128)} %constant.6.clone.coef_ref) | copy-start | bytes 270340
  0.7 10.8 %copy-start.7 = (bf16[128,128]{1,0:T(8,128)(2,1)S(1)}, bf16[128,128]{1,0:T(8,128)(2,1)}, u32[]{:S(2)}) copy-start(bf16[128,128]{1,0:T(8,128)(2,1)} %constant.8.clone.near_ref) | copy-start | bytes 98308
  0.7 10.8 %copy-start.8 = (s32[3,8,128]{2,1,0:T(8,128)S(1)}, s32[3,8,128]{2,1,0:T(8,128)}, u32[]{:S(2)}) copy-start(s32[3,8,128]{2,1,0:T(8,128)} %constant.7.clone.rows_ref) | copy-start | bytes 36868
  8.4 7.4 %copy-start.1 = (f32[2,2,9]{2,1,0:T(2,128)S(1)}, f32[2,2,9]{2,1,0:T(2,128)}, u32[]{:S(2)}) copy-start(f32[2,2,9]{2,1,0:T(2,128)} %psf_ref.1) | copy-start | bytes 436
  8.4 9.5 %copy-start = (f32[4,2,128,128]{3,2,1,0:T(8,128)S(1)}, f32[4,2,128,128]{3,2,1,0:T(8,128)}, u32[]{:S(2)}) copy-start(f32[4,2,128,128]{3,2,1,0:T(8,128)} %get-tuple-element.29.keep_ref) | copy-start | bytes 1572868
  8.4 9.5 %collective-permute-start = (bf16[4,2,128,128]{3,2,1,0:T(8,128)(2,1)}, bf16[4,2,128,128]{3,2,1,0:T(8,128)(2,1)S(1)}, u32[]{:S(2)}, u32[]{:S(2)}) collective-permute-start(bf16[4,2,128,128]{3,2,1,0:T(8,128)(2,1)} %get-tuple-element.30), channel_id=1, source_target_pairs={{0,16},{16,0},{1,17},{17,1},{2,18},{18,2},{3,19},{19,3},{4,20},{20... | collective-permute-start | bytes 786440 | tf_op jit(solution)/shard_map/ppermute | solution.py:572
  18.7 8.9 %collective-permute-start.1 = (bf16[2,128,128]{2,1,0:T(8,128)(2,1)S(1)}, bf16[2,128,128]{2,1,0:T(8,128)(2,1)S(1)}, u32[]{:S(2)}, u32[]{:S(2)}) collective-permute-start(bf16[2,128,128]{2,1,0:T(8,128)(2,1)S(1)} %get-tuple-element.33), channel_id=1, source_target_pairs={{0,4},{4,8},{8,12},{12,0},{1,5},{5,9},{9,13},{13,1},{2,6},{6,10},{... | collective-permute-start | bytes 196616 | tf_op jit(solution)/shard_map/ppermute | solution.py:576
  20.5 7.0 %collective-permute-start.2 = (bf16[2,128,128]{2,1,0:T(8,128)(2,1)S(1)}, bf16[2,128,128]{2,1,0:T(8,128)(2,1)S(1)}, u32[]{:S(2)}, u32[]{:S(2)}) collective-permute-start(bf16[2,128,128]{2,1,0:T(8,128)(2,1)S(1)} %get-tuple-element.34), channel_id=1, source_target_pairs={{0,8},{4,12},{8,0},{12,4},{1,9},{5,13},{9,1},{13,5},{2,10},{6,14},... | collective-permute-start | bytes 196616 | tf_op jit(solution)/shard_map/ppermute | solution.py:576
  23.1 4.5 %collective-permute-start.3 = (bf16[2,128,128]{2,1,0:T(8,128)(2,1)S(1)}, bf16[2,128,128]{2,1,0:T(8,128)(2,1)S(1)}, u32[]{:S(2)}, u32[]{:S(2)}) collective-permute-start(bf16[2,128,128]{2,1,0:T(8,128)(2,1)S(1)} %get-tuple-element.35), channel_id=1, source_target_pairs={{0,12},{4,0},{8,4},{12,8},{1,13},{5,1},{9,5},{13,9},{2,14},{6,2},{... | collective-permute-start | bytes 196616 | tf_op jit(solution)/shard_map/ppermute | solution.py:576
  28.5 5.6 %collective-permute-start.4 = (f32[128,128]{1,0:T(8,128)S(1)}, f32[128,128]{1,0:T(8,128)S(1)}, u32[]{:S(2)}, u32[]{:S(2)}) collective-permute-start(f32[128,128]{1,0:T(8,128)S(1)} %get-tuple-element.36.own_ref), channel_id=1, source_target_pairs={{0,16},{16,0},{1,17},{17,1},{2,18},{18,2},{3,19},{19,3},{4,20},{20... | collective-permute-start | bytes 196616 | tf_op jit(solution)/shard_map/ppermute | solution.py:572
  30.1 3.9 %collective-permute-start.6 = (bf16[16,128]{1,0:T(8,128)(2,1)S(1)}, bf16[16,128]{1,0:T(8,128)(2,1)S(1)}, u32[]{:S(2)}, u32[]{:S(2)}) collective-permute-start(bf16[16,128]{1,0:T(8,128)(2,1)S(1)} %get-tuple-element.37), channel_id=1, source_target_pairs={{0,19},{1,16},{2,17},{3,18},{16,1},{17,2},{18,3},{19,0},{4,23},{5,... | collective-permute-start | bytes 12296 | tf_op jit(solution)/shard_map/ppermute | solution.py:582
  30.1 3.9 %collective-permute-start.5 = (bf16[16,128]{1,0:T(8,128)(2,1)S(1)}, bf16[16,128]{1,0:T(8,128)(2,1)S(1)}, u32[]{:S(2)}, u32[]{:S(2)}) collective-permute-start(bf16[16,128]{1,0:T(8,128)(2,1)S(1)} %get-tuple-element.37), channel_id=1, source_target_pairs={{0,3},{1,0},{2,1},{3,2},{16,17},{17,18},{18,19},{19,16},{4,7},{5,4... | collective-permute-start | bytes 12296 | tf_op jit(solution)/shard_map/ppermute | solution.py:582
  35.5 9.4 %copy-start.5 = (s32[1,64,1]{1,2,0:T(1,128)S(1)}, s32[1,64,1]{1,2,0:T(1,128)}, u32[]{:S(2)}) copy-start(s32[1,64,1]{1,2,0:T(1,128)} %param.10) | copy-start | bytes 772
  35.5 7.7 %collective-permute-start.9 = (bf16[2,128,128]{2,1,0:T(8,128)(2,1)S(1)}, bf16[2,128,128]{2,1,0:T(8,128)(2,1)S(1)}, u32[]{:S(2)}, u32[]{:S(2)}) collective-permute-start(bf16[2,128,128]{2,1,0:T(8,128)(2,1)S(1)} %get-tuple-element.38.rest_0_), channel_id=1, source_target_pairs={{0,12},{4,0},{8,4},{12,8},{1,13},{5,1},{9,5},{13,9},{2,14},{6,2},{... | collective-permute-start | bytes 196616 | tf_op jit(solution)/shard_map/ppermute | solution.py:576
  38.3 6.7 %collective-permute-start.8 = (bf16[2,128,128]{2,1,0:T(8,128)(2,1)S(1)}, bf16[2,128,128]{2,1,0:T(8,128)(2,1)S(1)}, u32[]{:S(2)}, u32[]{:S(2)}) collective-permute-start(bf16[2,128,128]{2,1,0:T(8,128)(2,1)S(1)} %get-tuple-element.38.rest_0_), channel_id=1, source_target_pairs={{0,8},{4,12},{8,0},{12,4},{1,9},{5,13},{9,1},{13,5},{2,10},{6,14},... | collective-permute-start | bytes 196616 | tf_op jit(solution)/shard_map/ppermute | solution.py:576
  38.3 6.7 %collective-permute-start.7 = (bf16[2,128,128]{2,1,0:T(8,128)(2,1)S(1)}, bf16[2,128,128]{2,1,0:T(8,128)(2,1)S(1)}, u32[]{:S(2)}, u32[]{:S(2)}) collective-permute-start(bf16[2,128,128]{2,1,0:T(8,128)(2,1)S(1)} %get-tuple-element.38.rest_0_), channel_id=1, source_target_pairs={{0,4},{4,8},{8,12},{12,0},{1,5},{5,9},{9,13},{13,1},{2,6},{6,10},{... | collective-permute-start | bytes 196616 | tf_op jit(solution)/shard_map/ppermute | solution.py:576

commit v7 on v6

--- a/solution.py
+++ b/solution.py
@@ -383,7 +383,7 @@
 
 def coadd_kernel(after_ref, *refs):
     del after_ref
-    parts, (piece_ref, edge_ref) = refs[:-2], refs[-2:]
+    parts, (piece_ref, short_ref, edge_ref) = refs[:-3], refs[-3:]
     num, den = parts[0][0], parts[0][1]
     for part in parts[1:]:
         num = num + part[0].astype(F32)
@@ -393,6 +393,7 @@
     first = num / (1.0 + den)
     piece = (num + jnp.where(left, 0.0, pltpu.roll(first, side // 2, 1))) / (1.0 + den)
     piece_ref[...] = piece
+    short_ref[...] = piece.astype(BF16)
     flipped = jnp.transpose(piece)
     half = side // 2
     outer = jnp.concatenate([flipped[0:8], flipped[half : half + 8]], axis=0)
@@ -404,9 +405,13 @@
     side = parts[0].shape[2]
     return pl.pallas_call(
         coadd_kernel,
-        out_shape=[jax.ShapeDtypeStruct((side, side), F32), jax.ShapeDtypeStruct((16, side), BF16)],
+        out_shape=[
+            jax.ShapeDtypeStruct((side, side), F32),
+            jax.ShapeDtypeStruct((side, side), BF16),
+            jax.ShapeDtypeStruct((16, side), BF16),
+        ],
         in_specs=[smem()] + [vmem()] * len(parts),
-        out_specs=[vmem(), vmem()],
+        out_specs=[vmem()] * 3,
         compiler_params=pltpu.CompilerParams(vmem_limit_bytes=TINY_BYTES),
         name="coadd",
     )(after, *parts)
@@ -461,10 +466,10 @@
     return both[:, :side] + both[:, side:] + dot(low, inner[:, :side])
 
 
-def join_kernel(inner_ref, outer_ref, own_ref, other_ref, edge_ref, far_ref, after_ref, sky_ref, tile_ref):
+def join_kernel(inner_ref, outer_ref, own_ref, other_ref, edge_ref, far_ref, after_ref, sky_ref):
     del after_ref
     here = lax.axis_index("exp") == 0
-    own, other = own_ref[...], other_ref[...]
+    own, other = own_ref[...], other_ref[...].astype(F32)
     tiles = halves_of(jnp.where(here, own, other), jnp.where(here, other, own))
     edge, far = edge_ref[...].astype(F32), far_ref[...].astype(F32)
     left, right = jnp.where(here, far, edge), jnp.where(here, edge, far)
@@ -475,19 +480,35 @@
         at = slice(8 * k, 8 * k + 8)
         edges = jnp.concatenate([left[at], right[at]], axis=0).astype(BF16)
         sky_ref[k] = smoothed(tiles[k], edges, inner_ref[k], outer_ref[k]).astype(BF16)
-    tile_ref[...] = tiles[1]
 
 
 def join(bands, own, other, edge, far, after):
     side = own.shape[1]
     return pl.pallas_call(
         join_kernel,
-        out_shape=[jax.ShapeDtypeStruct((2, side, side), BF16), jax.ShapeDtypeStruct((side, side), F32)],
+        out_shape=jax.ShapeDtypeStruct((2, side, side), BF16),
         in_specs=[vmem()] * 6 + [smem()],
-        out_specs=[vmem(), vmem()],
+        out_specs=vmem(),
         compiler_params=pltpu.CompilerParams(vmem_limit_bytes=TINY_BYTES),
         name="join",
     )(*bands, own, other, edge, far, after)
+
+
+def tile_kernel(own_ref, other_ref, tile_ref):
+    here = lax.axis_index("exp") == 0
+    own, other = own_ref[...], other_ref[...]
+    tile_ref[...] = halves_of(jnp.where(here, own, other), jnp.where(here, other, own))[1]
+
+
+def tile_of(own, other):
+    return pl.pallas_call(
+        tile_kernel,
+        out_shape=jax.ShapeDtypeStruct(own.shape, F32),
+        in_specs=[vmem(), vmem()],
+        out_specs=vmem(),
+        compiler_params=pltpu.CompilerParams(vmem_limit_bytes=TINY_BYTES),
+        name="tile",
+    )(own, other)
 
 
 def whole_kernel(inner_ref, outer_ref, tile_ref, edge_ref, sky_ref):
@@ -605,10 +626,11 @@
         *bands, row_bands, token = bands_of(psf, tokens[0])
         totals = pair(keep, swap(send), token)
         got = [totals[0]] + [turned(totals[dz], dz, tiles) for dz in range(1, tiles)]
-        piece, edge = coadd_of(tokens[1], got)
-        other = swap(piece)
+        piece, short, edge = coadd_of(tokens[1], got)
+        other = swap(short)
         near, far = to_sides(edge, columns, 0), to_sides(edge, columns, 1)
-        sky, coadd_tile = join(bands, piece, other, near, far, tokens[-2])
+        coadd_tile = tile_of(piece, swap(piece))
+        sky = join(bands, piece, other, near, far, tokens[-2])
         skies = [sky] + [turned(sky, dz, tiles) for dz in range(1, tiles)]
     else:
         me = lax.axis_index("tx")

time: 49.8 us -> 49.4 us (level)
  waiting for transfers between devices: 4.37 us -> 2.25 us
  starting transfers between devices: 15.6 us -> 17 us
    ppermute x2, waiting for transfers between devices: 2.16 us -> 0.84 us  [to_sides(): return lax.ppermute(edge, ('exp', 'ty'), perm)]
    ppermute x2 -> x3, starting transfers between devices: 4.66 us -> 5.98 us  [swap(): return lax.ppermute(cells, 'exp', [(0, 1), (1, 0)])]
    ppermute x6, waiting for transfers between devices: 1.84 us -> 1.04 us  [turned(): lax.ppermute(cells, 'tx', [(z, (z + dz) % tiles) for z in range(tiles)])]
    pallas_call x1 -> x2, Pallas kernels: 1.44 us -> 1.69 us  [the longest x1 0.96 us: join(): pl.pallas_call(join_kernel, out_shape=jax.ShapeDtypeStruct((2, side, side...]
  transfers between devices with their start and end apart: 10 -> 11, of which waited for: 4 -> 4; matrix products, arithmetic and copies ran while one was open for 0% -> 0% of each run, Pallas kernels for 27% -> 31%
where the time goes in v7:
time: 49.4 us; the launch traced here: 49.2 us
  Pallas kernels  29 us (59%)
  starting transfers between devices  17 us (34%)
  waiting for transfers between devices  2.25 us (5%)
  between operations  0.81 us (2%)
    pallas_call x3, Pallas kernels, slopes_of(): pl.pallas_call(functools.partial(slopes_kernel, step_blocks, start), grid...  11.7 us
    ppermute x6, starting transfers between devices, turned(): lax.ppermute(cells, 'tx', [(z, (z + dz) % tiles) for z in range(tiles)])  9.29 us
    pallas_call x1, Pallas kernels, tile_sums(): pl.pallas_call(functools.partial(sums_kernel, tiles, packed, step_blocks)...  7.74 us
    ppermute x3, starting transfers between devices, swap(): return lax.ppermute(cells, 'exp', [(0, 1), (1, 0)])  5.98 us
    pallas_call x1, Pallas kernels, gradients_of(): pl.pallas_call(functools.partial(gradient_kernel, tiles), out_shape=jax.S...  4.65 us
    ppermute x2, starting transfers between devices, to_sides(): return lax.ppermute(edge, ('exp', 'ty'), perm)  1.78 us
    pallas_call x1, Pallas kernels, bands_of(): pl.pallas_call(bands_kernel, out_shape=[jax.ShapeDtypeStruct((2, rows, 2...  1.74 us
    ppermute x6, waiting for transfers between devices, turned(): lax.ppermute(cells, 'tx', [(z, (z + dz) % tiles) for z in range(tiles)])  1.04 us
  transfers between devices with their start and end apart: 11, of which 4 were waited for; matrix products, arithmetic and copies ran while one was open for 0% of the time, Pallas kernels for 31%

profile of v7, /device:TPU:0, one launch (start us, length us, event | category | flops | bytes accessed | tf_op | source)
XLA Modules:
  0.0 49.2 jit_solution(13175796621199591481)
XLA Ops:
  0.6 0.0 copy-start.2
  0.6 0.0 copy-start.3
  0.7 0.0 copy-start.4
  0.7 0.0 copy-start.6
  0.7 0.0 copy-start.7
  0.7 0.0 copy-start.8
  0.7 7.7 %tile_sums.1 = (f32[4,2,128,128]{3,2,1,0:T(8,128)}, bf16[4,2,128,128]{3,2,1,0:T(8,128)(2,1)}) custom-call(s32[1,2,4,64]{3,2,1,0:T(4,128)} %bitcast.13, s32[1,1,64]{2,1,0:T(1,128)} %bitcast.17, f32[1,64]{1,0:T(1,128)} %weight_ref.1, f32[22,8,128]{2,1,0:T(8,128)} %constant.6.clone.coef_ref, s32[3,8,128]{2,1,0:T(8,128)} %constant.7.clone.rows_ref, ...), custom_call_target="tpu_custom_call" | custom-call | flops 8000000000 | bytes 3000000 | tf_op jit(solution)/shard_map/tile_sums/pallas_call | solution.py:241
  8.4 3.0 %collective-permute-start = (bf16[4,2,128,128]{3,2,1,0:T(8,128)(2,1)}, bf16[4,2,128,128]{3,2,1,0:T(8,128)(2,1)S(1)}, u32[]{:S(2)}, u32[]{:S(2)}) collective-permute-start(bf16[4,2,128,128]{3,2,1,0:T(8,128)(2,1)} %get-tuple-element.29), channel_id=1, source_target_pairs={{0,16},{16,0},{1,17},{17,1},{2,18},{18,2},{3,19},{19,3},{4,20},{20... | collective-permute-start | bytes 786440 | tf_op jit(solution)/shard_map/ppermute | solution.py:593
  11.4 0.0 copy-done.2
  11.4 0.0 copy-done.3
  11.5 0.0 copy-done.4
  11.5 0.0 copy-done.6
  11.5 0.0 copy-done.7
  11.5 0.0 copy-done.8
  11.5 4.4 %slopes.3 = (bf16[24,4,128,128]{3,2,1,0:T(8,128)(2,1)S(1)}, f32[24,8,128]{2,1,0:T(8,128)S(1)}, s32[1]{0:T(128)}) custom-call(s32[1,2,4,64]{3,2,1,0:T(4,128)S(1)} %bitcast.14, f32[22,8,128]{2,1,0:T(8,128)S(1)} %copy-done.6, s32[3,8,128]{2,1,0:T(8,128)S(1)} %copy-done.8, bf16[128,128]{1,0:T(8,128)(2,1)S(1)} %copy-done.7, s32[64,128]{1,0:T(8,128)S(1)} %bitcast.10, ...), custom_call_target="tpu_custom_call" | custom-call | flops 3600000000 | bytes 7200000 | tf_op jit(solution)/shard_map/slopes/pallas_call | solution.py:359
  15.8 0.0 copy-done.1
  15.8 1.7 %bands.1 = (bf16[2,128,256]{2,1,0:T(8,128)(2,1)S(1)}, bf16[2,16,256]{2,1,0:T(8,128)(2,1)S(1)}, bf16[2,256,160]{2,1,0:T(8,128)(2,1)S(1)}, s32[1]{0:T(128)}) custom-call(f32[2,2,9]{2,1,0:T(2,128)S(1)} %copy-done.1, s32[1]{0:T(128)} %get-tuple-element.23.after_ref), custom_call_target="tpu_custom_call" | custom-call | tf_op jit(solution)/shard_map/bands/pallas_call | solution.py:450
  17.6 0.4 collective-permute-done.got_ref
  18.0 0.0 copy-done
  18.0 0.7 %pair.1 = (f32[2,128,128]{2,1,0:T(8,128)S(1)}, bf16[2,128,128]{2,1,0:T(8,128)(2,1)S(1)}, bf16[2,128,128]{2,1,0:T(8,128)(2,1)S(1)}, bf16[2,128,128]{2,1,0:T(8,128)(2,1)S(1)}) custom-call(f32[4,2,128,128]{3,2,1,0:T(8,128)S(1)} %copy-done, bf16[4,2,128,128]{3,2,1,0:T(8,128)(2,1)S(1)} %collective-permute-done.got_ref, s32[1]{0:T(128)} %get-tuple-element.30.after_ref), custom_call_target="tpu_custom_call" | custom-call | tf_op jit(solution)/shard_map/pair/pallas_call | solution.py:276
  18.7 1.9 %collective-permute-start.1 = (bf16[2,128,128]{2,1,0:T(8,128)(2,1)S(1)}, bf16[2,128,128]{2,1,0:T(8,128)(2,1)S(1)}, u32[]{:S(2)}, u32[]{:S(2)}) collective-permute-start(bf16[2,128,128]{2,1,0:T(8,128)(2,1)S(1)} %get-tuple-element.32), channel_id=1, source_target_pairs={{0,4},{4,8},{8,12},{12,0},{1,5},{5,9},{9,13},{13,1},{2,6},{6,10},{... | collective-permute-start | bytes 196616 | tf_op jit(solution)/shard_map/ppermute | solution.py:597
  20.5 2.6 %collective-permute-start.2 = (bf16[2,128,128]{2,1,0:T(8,128)(2,1)S(1)}, bf16[2,128,128]{2,1,0:T(8,128)(2,1)S(1)}, u32[]{:S(2)}, u32[]{:S(2)}) collective-permute-start(bf16[2,128,128]{2,1,0:T(8,128)(2,1)S(1)} %get-tuple-element.33), channel_id=1, source_target_pairs={{0,8},{4,12},{8,0},{12,4},{1,9},{5,13},{9,1},{13,5},{2,10},{6,14},... | collective-permute-start | bytes 196616 | tf_op jit(solution)/shard_map/ppermute | solution.py:597
  23.1 1.3 %collective-permute-start.3 = (bf16[2,128,128]{2,1,0:T(8,128)(2,1)S(1)}, bf16[2,128,128]{2,1,0:T(8,128)(2,1)S(1)}, u32[]{:S(2)}, u32[]{:S(2)}) collective-permute-start(bf16[2,128,128]{2,1,0:T(8,128)(2,1)S(1)} %get-tuple-element.34), channel_id=1, source_target_pairs={{0,12},{4,0},{8,4},{12,8},{1,13},{5,1},{9,5},{13,9},{2,14},{6,2},{... | collective-permute-start | bytes 196616 | tf_op jit(solution)/shard_map/ppermute | solution.py:597
  24.5 3.1 %slopes.4 = (bf16[16,4,128,128]{3,2,1,0:T(8,128)(2,1)S(1)}, f32[16,8,128]{2,1,0:T(8,128)S(1)}, s32[1]{0:T(128)}) custom-call(s32[1,2,4,64]{3,2,1,0:T(4,128)S(1)} %bitcast.15, f32[22,8,128]{2,1,0:T(8,128)S(1)} %copy-done.6, s32[3,8,128]{2,1,0:T(8,128)S(1)} %copy-done.8, bf16[128,128]{1,0:T(8,128)(2,1)S(1)} %copy-done.7, s32[64,128]{1,0:T(8,128)S(1)} %bitcast.11, ...), custom_call_target="tpu_custom_call" | custom-call | flops 2400000000 | bytes 4800000 | tf_op jit(solution)/shard_map/slopes/pallas_call | solution.py:359
  27.6 0.0 collective-permute-done.1.refs_1_
  27.6 0.0 collective-permute-done.2.refs_2_
  27.6 0.1 collective-permute-done.3.refs_3_
  27.7 0.8 %coadd.1 = (f32[128,128]{1,0:T(8,128)S(1)}, bf16[128,128]{1,0:T(8,128)(2,1)S(1)}, bf16[16,128]{1,0:T(8,128)(2,1)S(1)}) custom-call(s32[1]{0:T(128)} %get-tuple-element.27.after_ref, f32[2,128,128]{2,1,0:T(8,128)S(1)} %get-tuple-element.31.refs_0_, bf16[2,128,128]{2,1,0:T(8,128)(2,1)S(1)} %collective-permute-done.1.refs_1_, ...), custom_call_target="tpu_custom_call" | custom-call | tf_op jit(solution)/shard_map/coadd/pallas_call | solution.py:406
  28.5 1.7 %collective-permute-start.4 = (bf16[128,128]{1,0:T(8,128)(2,1)S(1)}, bf16[128,128]{1,0:T(8,128)(2,1)S(1)}, u32[]{:S(2)}, u32[]{:S(2)}) collective-permute-start(bf16[128,128]{1,0:T(8,128)(2,1)S(1)} %get-tuple-element.36), channel_id=1, source_target_pairs={{0,16},{16,0},{1,17},{17,1},{2,18},{18,2},{3,19},{19,3},{4,20},{20... | collective-permute-start | bytes 98312 | tf_op jit(solution)/shard_map/ppermute | solution.py:593
  30.1 0.0 collective-permute-start.6
  30.1 1.8 %collective-permute-start.5 = (bf16[16,128]{1,0:T(8,128)(2,1)S(1)}, bf16[16,128]{1,0:T(8,128)(2,1)S(1)}, u32[]{:S(2)}, u32[]{:S(2)}) collective-permute-start(bf16[16,128]{1,0:T(8,128)(2,1)S(1)} %get-tuple-element.37), channel_id=1, source_target_pairs={{0,3},{1,0},{2,1},{3,2},{16,17},{17,18},{18,19},{19,16},{4,7},{5,4... | collective-permute-start | bytes 12296 | tf_op jit(solution)/shard_map/ppermute | solution.py:603
  31.9 1.3 %collective-permute-start.10 = (f32[128,128]{1,0:T(8,128)S(1)}, f32[128,128]{1,0:T(8,128)S(1)}, u32[]{:S(2)}, u32[]{:S(2)}) collective-permute-start(f32[128,128]{1,0:T(8,128)S(1)} %get-tuple-element.35.own_ref), channel_id=1, source_target_pairs={{0,16},{16,0},{1,17},{17,1},{2,18},{18,2},{3,19},{19,3},{4,20},{20... | collective-permute-start | bytes 196616 | tf_op jit(solution)/shard_map/ppermute | solution.py:593
  33.2 0.8 %collective-permute-done.6.far_ref = bf16[16,128]{1,0:T(8,128)(2,1)S(1)} collective-permute-done((bf16[16,128]{1,0:T(8,128)(2,1)S(1)}, bf16[16,128]{1,0:T(8,128)(2,1)S(1)}, u32[]{:S(2)}, u32[]{:S(2)}) %collective-permute-start.6) | collective-permute-done | bytes 4128 | tf_op jit(solution)/shard_map/ppermute | solution.py:603
  34.1 0.0 collective-permute-done.5.edge_ref
  34.1 0.0 collective-permute-done.4.other_ref
  34.1 1.0 %join.1.rest_0_ = bf16[2,128,128]{2,1,0:T(8,128)(2,1)S(1)} custom-call(bf16[2,128,256]{2,1,0:T(8,128)(2,1)S(1)} %get-tuple-element.25.inner_ref, bf16[2,16,256]{2,1,0:T(8,128)(2,1)S(1)} %get-tuple-element.26.outer_ref, f32[128,128]{1,0:T(8,128)S(1)} %get-tuple-element.35.own_ref, bf16[128,128]{1,0:T(8,128)(2,1)S(1)} %collective-permute-done.4.other_ref, ...), custom_call_target="tpu_custom_call" | custom-call | tf_op jit(solution)/shard_map/join/pallas_call | solution.py:487
  35.0 0.0 copy-start.5
  35.0 2.8 %collective-permute-start.9 = (bf16[2,128,128]{2,1,0:T(8,128)(2,1)S(1)}, bf16[2,128,128]{2,1,0:T(8,128)(2,1)S(1)}, u32[]{:S(2)}, u32[]{:S(2)}) collective-permute-start(bf16[2,128,128]{2,1,0:T(8,128)(2,1)S(1)} %join.1.rest_0_), channel_id=1, source_target_pairs={{0,12},{4,0},{8,4},{12,8},{1,13},{5,1},{9,5},{13,9},{2,14},{6,2},{... | collective-permute-start | bytes 196616 | tf_op jit(solution)/shard_map/ppermute | solution.py:597
  37.9 0.0 collective-permute-start.8
  37.9 0.6 %collective-permute-start.7 = (bf16[2,128,128]{2,1,0:T(8,128)(2,1)S(1)}, bf16[2,128,128]{2,1,0:T(8,128)(2,1)S(1)}, u32[]{:S(2)}, u32[]{:S(2)}) collective-permute-start(bf16[2,128,128]{2,1,0:T(8,128)(2,1)S(1)} %join.1.rest_0_), channel_id=1, source_target_pairs={{0,4},{4,8},{8,12},{12,0},{1,5},{5,9},{9,13},{13,1},{2,6},{6,10},{... | collective-permute-start | bytes 196616 | tf_op jit(solution)/shard_map/ppermute | solution.py:597
  38.5 4.3 %slopes.5 = (bf16[24,4,128,128]{3,2,1,0:T(8,128)(2,1)S(1)}, f32[24,8,128]{2,1,0:T(8,128)S(1)}, s32[1]{0:T(128)}) custom-call(s32[1,2,4,64]{3,2,1,0:T(4,128)S(1)} %bitcast.16, f32[22,8,128]{2,1,0:T(8,128)S(1)} %copy-done.6, s32[3,8,128]{2,1,0:T(8,128)S(1)} %copy-done.8, bf16[128,128]{1,0:T(8,128)(2,1)S(1)} %copy-done.7, s32[64,128]{1,0:T(8,128)S(1)} %bitcast.12, ...), custom_call_target="tpu_custom_call" | custom-call | flops 3600000000 | bytes 7200000 | tf_op jit(solution)/shard_map/slopes/pallas_call | solution.py:359
  42.8 0.0 collective-permute-done.10.other_ref
  42.9 0.7 %tile.1 = f32[128,128]{1,0:T(8,128)} custom-call(f32[128,128]{1,0:T(8,128)S(1)} %get-tuple-element.35.own_ref, f32[128,128]{1,0:T(8,128)S(1)} %collective-permute-done.10.other_ref), custom_call_target="tpu_custom_call" | custom-call | tf_op jit(solution)/shard_map/tile/pallas_call | solution.py:504
  43.6 0.0 collective-permute-done.9.rest_3_
  43.6 0.9 %collective-permute-done.8.rest_2_ = bf16[2,128,128]{2,1,0:T(8,128)(2,1)S(1)} collective-permute-done((bf16[2,128,128]{2,1,0:T(8,128)(2,1)S(1)}, bf16[2,128,128]{2,1,0:T(8,128)(2,1)S(1)}, u32[]{:S(2)}, u32[]{:S(2)}) %collective-permute-start.8) | collective-permute-done | bytes 65568 | tf_op jit(solution)/shard_map/ppermute | solution.py:597
  44.5 0.0 collective-permute-done.7.rest_1_
  44.5 0.0 copy-done.5
  44.5 4.6 %gradients.1 = f32[1,2,4,64]{3,2,1,0:T(4,128)} custom-call(s32[1,1,64]{2,1,0:T(1,128)S(1)} %bitcast.18, bf16[2,256,160]{2,1,0:T(8,128)(2,1)S(1)} %get-tuple-element.24.band_ref, bf16[2,128,128]{2,1,0:T(8,128)(2,1)S(1)} %join.1.rest_0_, bf16[2,128,128]{2,1,0:T(8,128)(2,1)S(1)} %collective-permute-done.7.rest_1_, ...), custom_call_target="tpu_custom_call" | custom-call | flops 4000000000 | bytes 20000000 | tf_op jit(solution)/shard_map/gradients/pallas_call | solution.py:577
  (2 shorter events, 0.0 us)
Async XLA Ops:
  0.6 10.8 %copy-start.2 = (bf16[1,64,128,128]{3,2,1,0:T(8,128)(2,1)S(1)}, bf16[1,64,128,128]{3,2,1,0:T(8,128)(2,1)}, u32[]{:S(2)}) copy-start(bf16[1,64,128,128]{3,2,1,0:T(8,128)(2,1)} %param.9) | copy-start | bytes 6291460
  0.6 10.8 %copy-start.3 = (s32[1,64,128]{2,1,0:T(8,128)S(1)}, s32[1,64,128]{2,1,0:T(8,128)}, u32[]{:S(2)}) copy-start(s32[1,64,128]{2,1,0:T(8,128)} %param.12) | copy-start | bytes 98308
  0.7 10.8 %copy-start.4 = (s32[1,64,2,4]{1,3,2,0:T(4,128)S(1)}, s32[1,64,2,4]{1,3,2,0:T(4,128)}, u32[]{:S(2)}) copy-start(s32[1,64,2,4]{1,3,2,0:T(4,128)} %param.11) | copy-start | bytes 6148
  0.7 10.8 %copy-start.6 = (f32[22,8,128]{2,1,0:T(8,128)S(1)}, f32[22,8,128]{2,1,0:T(8,128)}, u32[]{:S(2)}) copy-start(f32[22,8,128]{2,1,0:T(8,128)} %constant.6.clone.coef_ref) | copy-start | bytes 270340
  0.7 10.8 %copy-start.7 = (bf16[128,128]{1,0:T(8,128)(2,1)S(1)}, bf16[128,128]{1,0:T(8,128)(2,1)}, u32[]{:S(2)}) copy-start(bf16[128,128]{1,0:T(8,128)(2,1)} %constant.8.clone.near_ref) | copy-start | bytes 98308
  0.7 10.8 %copy-start.8 = (s32[3,8,128]{2,1,0:T(8,128)S(1)}, s32[3,8,128]{2,1,0:T(8,128)}, u32[]{:S(2)}) copy-start(s32[3,8,128]{2,1,0:T(8,128)} %constant.7.clone.rows_ref) | copy-start | bytes 36868
  8.4 7.4 %copy-start.1 = (f32[2,2,9]{2,1,0:T(2,128)S(1)}, f32[2,2,9]{2,1,0:T(2,128)}, u32[]{:S(2)}) copy-start(f32[2,2,9]{2,1,0:T(2,128)} %psf_ref.1) | copy-start | bytes 436
  8.4 9.5 %copy-start = (f32[4,2,128,128]{3,2,1,0:T(8,128)S(1)}, f32[4,2,128,128]{3,2,1,0:T(8,128)}, u32[]{:S(2)}) copy-start(f32[4,2,128,128]{3,2,1,0:T(8,128)} %get-tuple-element.28.keep_ref) | copy-start | bytes 1572868
  8.4 9.5 %collective-permute-start = (bf16[4,2,128,128]{3,2,1,0:T(8,128)(2,1)}, bf16[4,2,128,128]{3,2,1,0:T(8,128)(2,1)S(1)}, u32[]{:S(2)}, u32[]{:S(2)}) collective-permute-start(bf16[4,2,128,128]{3,2,1,0:T(8,128)(2,1)} %get-tuple-element.29), channel_id=1, source_target_pairs={{0,16},{16,0},{1,17},{17,1},{2,18},{18,2},{3,19},{19,3},{4,20},{20... | collective-permute-start | bytes 786440 | tf_op jit(solution)/shard_map/ppermute | solution.py:593
  18.7 8.9 %collective-permute-start.1 = (bf16[2,128,128]{2,1,0:T(8,128)(2,1)S(1)}, bf16[2,128,128]{2,1,0:T(8,128)(2,1)S(1)}, u32[]{:S(2)}, u32[]{:S(2)}) collective-permute-start(bf16[2,128,128]{2,1,0:T(8,128)(2,1)S(1)} %get-tuple-element.32), channel_id=1, source_target_pairs={{0,4},{4,8},{8,12},{12,0},{1,5},{5,9},{9,13},{13,1},{2,6},{6,10},{... | collective-permute-start | bytes 196616 | tf_op jit(solution)/shard_map/ppermute | solution.py:597
  20.5 7.0 %collective-permute-start.2 = (bf16[2,128,128]{2,1,0:T(8,128)(2,1)S(1)}, bf16[2,128,128]{2,1,0:T(8,128)(2,1)S(1)}, u32[]{:S(2)}, u32[]{:S(2)}) collective-permute-start(bf16[2,128,128]{2,1,0:T(8,128)(2,1)S(1)} %get-tuple-element.33), channel_id=1, source_target_pairs={{0,8},{4,12},{8,0},{12,4},{1,9},{5,13},{9,1},{13,5},{2,10},{6,14},... | collective-permute-start | bytes 196616 | tf_op jit(solution)/shard_map/ppermute | solution.py:597
  23.1 4.5 %collective-permute-start.3 = (bf16[2,128,128]{2,1,0:T(8,128)(2,1)S(1)}, bf16[2,128,128]{2,1,0:T(8,128)(2,1)S(1)}, u32[]{:S(2)}, u32[]{:S(2)}) collective-permute-start(bf16[2,128,128]{2,1,0:T(8,128)(2,1)S(1)} %get-tuple-element.34), channel_id=1, source_target_pairs={{0,12},{4,0},{8,4},{12,8},{1,13},{5,1},{9,5},{13,9},{2,14},{6,2},{... | collective-permute-start | bytes 196616 | tf_op jit(solution)/shard_map/ppermute | solution.py:597
  28.5 5.6 %collective-permute-start.4 = (bf16[128,128]{1,0:T(8,128)(2,1)S(1)}, bf16[128,128]{1,0:T(8,128)(2,1)S(1)}, u32[]{:S(2)}, u32[]{:S(2)}) collective-permute-start(bf16[128,128]{1,0:T(8,128)(2,1)S(1)} %get-tuple-element.36), channel_id=1, source_target_pairs={{0,16},{16,0},{1,17},{17,1},{2,18},{18,2},{3,19},{19,3},{4,20},{20... | collective-permute-start | bytes 98312 | tf_op jit(solution)/shard_map/ppermute | solution.py:593
  30.1 3.9 %collective-permute-start.6 = (bf16[16,128]{1,0:T(8,128)(2,1)S(1)}, bf16[16,128]{1,0:T(8,128)(2,1)S(1)}, u32[]{:S(2)}, u32[]{:S(2)}) collective-permute-start(bf16[16,128]{1,0:T(8,128)(2,1)S(1)} %get-tuple-element.37), channel_id=1, source_target_pairs={{0,19},{1,16},{2,17},{3,18},{16,1},{17,2},{18,3},{19,0},{4,23},{5,... | collective-permute-start | bytes 12296 | tf_op jit(solution)/shard_map/ppermute | solution.py:603
  30.1 3.9 %collective-permute-start.5 = (bf16[16,128]{1,0:T(8,128)(2,1)S(1)}, bf16[16,128]{1,0:T(8,128)(2,1)S(1)}, u32[]{:S(2)}, u32[]{:S(2)}) collective-permute-start(bf16[16,128]{1,0:T(8,128)(2,1)S(1)} %get-tuple-element.37), channel_id=1, source_target_pairs={{0,3},{1,0},{2,1},{3,2},{16,17},{17,18},{18,19},{19,16},{4,7},{5,4... | collective-permute-start | bytes 12296 | tf_op jit(solution)/shard_map/ppermute | solution.py:603
  31.9 10.9 %collective-permute-start.10 = (f32[128,128]{1,0:T(8,128)S(1)}, f32[128,128]{1,0:T(8,128)S(1)}, u32[]{:S(2)}, u32[]{:S(2)}) collective-permute-start(f32[128,128]{1,0:T(8,128)S(1)} %get-tuple-element.35.own_ref), channel_id=1, source_target_pairs={{0,16},{16,0},{1,17},{17,1},{2,18},{18,2},{3,19},{19,3},{4,20},{20... | collective-permute-start | bytes 196616 | tf_op jit(solution)/shard_map/ppermute | solution.py:593
  35.0 9.5 %copy-start.5 = (s32[1,64,1]{1,2,0:T(1,128)S(1)}, s32[1,64,1]{1,2,0:T(1,128)}, u32[]{:S(2)}) copy-start(s32[1,64,1]{1,2,0:T(1,128)} %param.10) | copy-start | bytes 772
  35.0 8.5 %collective-permute-start.9 = (bf16[2,128,128]{2,1,0:T(8,128)(2,1)S(1)}, bf16[2,128,128]{2,1,0:T(8,128)(2,1)S(1)}, u32[]{:S(2)}, u32[]{:S(2)}) collective-permute-start(bf16[2,128,128]{2,1,0:T(8,128)(2,1)S(1)} %join.1.rest_0_), channel_id=1, source_target_pairs={{0,12},{4,0},{8,4},{12,8},{1,13},{5,1},{9,5},{13,9},{2,14},{6,2},{... | collective-permute-start | bytes 196616 | tf_op jit(solution)/shard_map/ppermute | solution.py:597
  37.9 6.7 %collective-permute-start.8 = (bf16[2,128,128]{2,1,0:T(8,128)(2,1)S(1)}, bf16[2,128,128]{2,1,0:T(8,128)(2,1)S(1)}, u32[]{:S(2)}, u32[]{:S(2)}) collective-permute-start(bf16[2,128,128]{2,1,0:T(8,128)(2,1)S(1)} %join.1.rest_0_), channel_id=1, source_target_pairs={{0,8},{4,12},{8,0},{12,4},{1,9},{5,13},{9,1},{13,5},{2,10},{6,14},... | collective-permute-start | bytes 196616 | tf_op jit(solution)/shard_map/ppermute | solution.py:597
  37.9 6.7 %collective-permute-start.7 = (bf16[2,128,128]{2,1,0:T(8,128)(2,1)S(1)}, bf16[2,128,128]{2,1,0:T(8,128)(2,1)S(1)}, u32[]{:S(2)}, u32[]{:S(2)}) collective-permute-start(bf16[2,128,128]{2,1,0:T(8,128)(2,1)S(1)} %join.1.rest_0_), channel_id=1, source_target_pairs={{0,4},{4,8},{8,12},{12,0},{1,5},{5,9},{9,13},{13,1},{2,6},{6,10},{... | collective-permute-start | bytes 196616 | tf_op jit(solution)/shard_map/ppermute | solution.py:597

commit v8 on v7

--- a/solution.py
+++ b/solution.py
@@ -564,7 +564,7 @@
                 gathered = jnp.where(lane == first + j, total, gathered)
             return gathered
 
-        gathered = lax.fori_loop(0, slope_ref.shape[0] // GROUP3, body, gathered)
+        gathered = lax.fori_loop(0, slope_ref.shape[0] // GROUP3, body, gathered, unroll=True)
         first += slope_ref.shape[0]
     out_ref[0, 0] = gathered[0:4]
     out_ref[0, 1] = gathered[4:8]

time: 49.4 us -> 48.7 us (0.986)
  Pallas kernels: 29 us -> 28.4 us
    pallas_call x1, Pallas kernels: 4.65 us -> 4.01 us  [gradients_of(): pl.pallas_call(functools.partial(gradient_kernel, tiles), out_shape=jax.S...]
where the time goes in v8:
time: 48.7 us; the launch traced here: 48.6 us
  Pallas kernels  28.4 us (58%)
  starting transfers between devices  17 us (35%)
  waiting for transfers between devices  2.25 us (5%)
  between operations  0.81 us (2%)
    pallas_call x3, Pallas kernels, slopes_of(): pl.pallas_call(functools.partial(slopes_kernel, step_blocks, start), grid...  11.7 us
    ppermute x6, starting transfers between devices, turned(): lax.ppermute(cells, 'tx', [(z, (z + dz) % tiles) for z in range(tiles)])  9.29 us
    pallas_call x1, Pallas kernels, tile_sums(): pl.pallas_call(functools.partial(sums_kernel, tiles, packed, step_blocks)...  7.74 us
    ppermute x3, starting transfers between devices, swap(): return lax.ppermute(cells, 'exp', [(0, 1), (1, 0)])  5.98 us
    pallas_call x1, Pallas kernels, gradients_of(): pl.pallas_call(functools.partial(gradient_kernel, tiles), out_shape=jax.S...  4.01 us
    ppermute x2, starting transfers between devices, to_sides(): return lax.ppermute(edge, ('exp', 'ty'), perm)  1.78 us
    pallas_call x1, Pallas kernels, bands_of(): pl.pallas_call(bands_kernel, out_shape=[jax.ShapeDtypeStruct((2, rows, 2...  1.74 us
    ppermute x6, waiting for transfers between devices, turned(): lax.ppermute(cells, 'tx', [(z, (z + dz) % tiles) for z in range(tiles)])  1.04 us
  transfers between devices with their start and end apart: 11, of which 4 were waited for; matrix products, arithmetic and copies ran while one was open for 0% of the time, Pallas kernels for 31%

profile of v8, /device:TPU:0, one launch (start us, length us, event | category | flops | bytes accessed | tf_op | source)
XLA Modules:
  0.0 48.6 jit_solution(16708289139966318879)
XLA Ops:
  0.6 0.0 copy-start.2
  0.6 0.0 copy-start.3
  0.7 0.0 copy-start.4
  0.7 0.0 copy-start.6
  0.7 0.0 copy-start.7
  0.7 0.0 copy-start.8
  0.7 7.7 %tile_sums.1 = (f32[4,2,128,128]{3,2,1,0:T(8,128)}, bf16[4,2,128,128]{3,2,1,0:T(8,128)(2,1)}) custom-call(s32[1,2,4,64]{3,2,1,0:T(4,128)} %bitcast.13, s32[1,1,64]{2,1,0:T(1,128)} %bitcast.17, f32[1,64]{1,0:T(1,128)} %weight_ref.1, f32[22,8,128]{2,1,0:T(8,128)} %constant.6.clone.coef_ref, s32[3,8,128]{2,1,0:T(8,128)} %constant.7.clone.rows_ref, ...), custom_call_target="tpu_custom_call" | custom-call | flops 8000000000 | bytes 3000000 | tf_op jit(solution)/shard_map/tile_sums/pallas_call | solution.py:241
  8.4 3.0 %collective-permute-start = (bf16[4,2,128,128]{3,2,1,0:T(8,128)(2,1)}, bf16[4,2,128,128]{3,2,1,0:T(8,128)(2,1)S(1)}, u32[]{:S(2)}, u32[]{:S(2)}) collective-permute-start(bf16[4,2,128,128]{3,2,1,0:T(8,128)(2,1)} %get-tuple-element.29), channel_id=1, source_target_pairs={{0,16},{16,0},{1,17},{17,1},{2,18},{18,2},{3,19},{19,3},{4,20},{20... | collective-permute-start | bytes 786440 | tf_op jit(solution)/shard_map/ppermute | solution.py:593
  11.4 0.0 copy-done.2
  11.4 0.0 copy-done.3
  11.5 0.0 copy-done.4
  11.5 0.0 copy-done.6
  11.5 0.0 copy-done.7
  11.5 0.0 copy-done.8
  11.5 4.4 %slopes.3 = (bf16[24,4,128,128]{3,2,1,0:T(8,128)(2,1)S(1)}, f32[24,8,128]{2,1,0:T(8,128)S(1)}, s32[1]{0:T(128)}) custom-call(s32[1,2,4,64]{3,2,1,0:T(4,128)S(1)} %bitcast.14, f32[22,8,128]{2,1,0:T(8,128)S(1)} %copy-done.6, s32[3,8,128]{2,1,0:T(8,128)S(1)} %copy-done.8, bf16[128,128]{1,0:T(8,128)(2,1)S(1)} %copy-done.7, s32[64,128]{1,0:T(8,128)S(1)} %bitcast.10, ...), custom_call_target="tpu_custom_call" | custom-call | flops 3600000000 | bytes 7200000 | tf_op jit(solution)/shard_map/slopes/pallas_call | solution.py:359
  15.8 0.0 copy-done.1
  15.8 1.7 %bands.1 = (bf16[2,128,256]{2,1,0:T(8,128)(2,1)S(1)}, bf16[2,16,256]{2,1,0:T(8,128)(2,1)S(1)}, bf16[2,256,160]{2,1,0:T(8,128)(2,1)S(1)}, s32[1]{0:T(128)}) custom-call(f32[2,2,9]{2,1,0:T(2,128)S(1)} %copy-done.1, s32[1]{0:T(128)} %get-tuple-element.23.after_ref), custom_call_target="tpu_custom_call" | custom-call | tf_op jit(solution)/shard_map/bands/pallas_call | solution.py:450
  17.6 0.4 collective-permute-done.got_ref
  18.0 0.0 copy-done
  18.0 0.7 %pair.1 = (f32[2,128,128]{2,1,0:T(8,128)S(1)}, bf16[2,128,128]{2,1,0:T(8,128)(2,1)S(1)}, bf16[2,128,128]{2,1,0:T(8,128)(2,1)S(1)}, bf16[2,128,128]{2,1,0:T(8,128)(2,1)S(1)}) custom-call(f32[4,2,128,128]{3,2,1,0:T(8,128)S(1)} %copy-done, bf16[4,2,128,128]{3,2,1,0:T(8,128)(2,1)S(1)} %collective-permute-done.got_ref, s32[1]{0:T(128)} %get-tuple-element.30.after_ref), custom_call_target="tpu_custom_call" | custom-call | tf_op jit(solution)/shard_map/pair/pallas_call | solution.py:276
  18.7 1.9 %collective-permute-start.1 = (bf16[2,128,128]{2,1,0:T(8,128)(2,1)S(1)}, bf16[2,128,128]{2,1,0:T(8,128)(2,1)S(1)}, u32[]{:S(2)}, u32[]{:S(2)}) collective-permute-start(bf16[2,128,128]{2,1,0:T(8,128)(2,1)S(1)} %get-tuple-element.32), channel_id=1, source_target_pairs={{0,4},{4,8},{8,12},{12,0},{1,5},{5,9},{9,13},{13,1},{2,6},{6,10},{... | collective-permute-start | bytes 196616 | tf_op jit(solution)/shard_map/ppermute | solution.py:597
  20.5 2.6 %collective-permute-start.2 = (bf16[2,128,128]{2,1,0:T(8,128)(2,1)S(1)}, bf16[2,128,128]{2,1,0:T(8,128)(2,1)S(1)}, u32[]{:S(2)}, u32[]{:S(2)}) collective-permute-start(bf16[2,128,128]{2,1,0:T(8,128)(2,1)S(1)} %get-tuple-element.33), channel_id=1, source_target_pairs={{0,8},{4,12},{8,0},{12,4},{1,9},{5,13},{9,1},{13,5},{2,10},{6,14},... | collective-permute-start | bytes 196616 | tf_op jit(solution)/shard_map/ppermute | solution.py:597
  23.1 1.3 %collective-permute-start.3 = (bf16[2,128,128]{2,1,0:T(8,128)(2,1)S(1)}, bf16[2,128,128]{2,1,0:T(8,128)(2,1)S(1)}, u32[]{:S(2)}, u32[]{:S(2)}) collective-permute-start(bf16[2,128,128]{2,1,0:T(8,128)(2,1)S(1)} %get-tuple-element.34), channel_id=1, source_target_pairs={{0,12},{4,0},{8,4},{12,8},{1,13},{5,1},{9,5},{13,9},{2,14},{6,2},{... | collective-permute-start | bytes 196616 | tf_op jit(solution)/shard_map/ppermute | solution.py:597
  24.5 3.1 %slopes.4 = (bf16[16,4,128,128]{3,2,1,0:T(8,128)(2,1)S(1)}, f32[16,8,128]{2,1,0:T(8,128)S(1)}, s32[1]{0:T(128)}) custom-call(s32[1,2,4,64]{3,2,1,0:T(4,128)S(1)} %bitcast.15, f32[22,8,128]{2,1,0:T(8,128)S(1)} %copy-done.6, s32[3,8,128]{2,1,0:T(8,128)S(1)} %copy-done.8, bf16[128,128]{1,0:T(8,128)(2,1)S(1)} %copy-done.7, s32[64,128]{1,0:T(8,128)S(1)} %bitcast.11, ...), custom_call_target="tpu_custom_call" | custom-call | flops 2400000000 | bytes 4800000 | tf_op jit(solution)/shard_map/slopes/pallas_call | solution.py:359
  27.6 0.0 collective-permute-done.1.refs_1_
  27.6 0.0 collective-permute-done.2.refs_2_
  27.6 0.1 collective-permute-done.3.refs_3_
  27.7 0.8 %coadd.1 = (f32[128,128]{1,0:T(8,128)S(1)}, bf16[128,128]{1,0:T(8,128)(2,1)S(1)}, bf16[16,128]{1,0:T(8,128)(2,1)S(1)}) custom-call(s32[1]{0:T(128)} %get-tuple-element.27.after_ref, f32[2,128,128]{2,1,0:T(8,128)S(1)} %get-tuple-element.31.refs_0_, bf16[2,128,128]{2,1,0:T(8,128)(2,1)S(1)} %collective-permute-done.1.refs_1_, ...), custom_call_target="tpu_custom_call" | custom-call | tf_op jit(solution)/shard_map/coadd/pallas_call | solution.py:406
  28.5 1.7 %collective-permute-start.4 = (bf16[128,128]{1,0:T(8,128)(2,1)S(1)}, bf16[128,128]{1,0:T(8,128)(2,1)S(1)}, u32[]{:S(2)}, u32[]{:S(2)}) collective-permute-start(bf16[128,128]{1,0:T(8,128)(2,1)S(1)} %get-tuple-element.36), channel_id=1, source_target_pairs={{0,16},{16,0},{1,17},{17,1},{2,18},{18,2},{3,19},{19,3},{4,20},{20... | collective-permute-start | bytes 98312 | tf_op jit(solution)/shard_map/ppermute | solution.py:593
  30.1 0.0 collective-permute-start.6
  30.1 1.8 %collective-permute-start.5 = (bf16[16,128]{1,0:T(8,128)(2,1)S(1)}, bf16[16,128]{1,0:T(8,128)(2,1)S(1)}, u32[]{:S(2)}, u32[]{:S(2)}) collective-permute-start(bf16[16,128]{1,0:T(8,128)(2,1)S(1)} %get-tuple-element.37), channel_id=1, source_target_pairs={{0,3},{1,0},{2,1},{3,2},{16,17},{17,18},{18,19},{19,16},{4,7},{5,4... | collective-permute-start | bytes 12296 | tf_op jit(solution)/shard_map/ppermute | solution.py:603
  31.9 1.3 %collective-permute-start.10 = (f32[128,128]{1,0:T(8,128)S(1)}, f32[128,128]{1,0:T(8,128)S(1)}, u32[]{:S(2)}, u32[]{:S(2)}) collective-permute-start(f32[128,128]{1,0:T(8,128)S(1)} %get-tuple-element.35.own_ref), channel_id=1, source_target_pairs={{0,16},{16,0},{1,17},{17,1},{2,18},{18,2},{3,19},{19,3},{4,20},{20... | collective-permute-start | bytes 196616 | tf_op jit(solution)/shard_map/ppermute | solution.py:593
  33.2 0.8 %collective-permute-done.6.far_ref = bf16[16,128]{1,0:T(8,128)(2,1)S(1)} collective-permute-done((bf16[16,128]{1,0:T(8,128)(2,1)S(1)}, bf16[16,128]{1,0:T(8,128)(2,1)S(1)}, u32[]{:S(2)}, u32[]{:S(2)}) %collective-permute-start.6) | collective-permute-done | bytes 4128 | tf_op jit(solution)/shard_map/ppermute | solution.py:603
  34.1 0.0 collective-permute-done.5.edge_ref
  34.1 0.0 collective-permute-done.4.other_ref
  34.1 1.0 %join.1.rest_0_ = bf16[2,128,128]{2,1,0:T(8,128)(2,1)S(1)} custom-call(bf16[2,128,256]{2,1,0:T(8,128)(2,1)S(1)} %get-tuple-element.25.inner_ref, bf16[2,16,256]{2,1,0:T(8,128)(2,1)S(1)} %get-tuple-element.26.outer_ref, f32[128,128]{1,0:T(8,128)S(1)} %get-tuple-element.35.own_ref, bf16[128,128]{1,0:T(8,128)(2,1)S(1)} %collective-permute-done.4.other_ref, ...), custom_call_target="tpu_custom_call" | custom-call | tf_op jit(solution)/shard_map/join/pallas_call | solution.py:487
  35.0 0.0 copy-start.5
  35.0 2.8 %collective-permute-start.9 = (bf16[2,128,128]{2,1,0:T(8,128)(2,1)S(1)}, bf16[2,128,128]{2,1,0:T(8,128)(2,1)S(1)}, u32[]{:S(2)}, u32[]{:S(2)}) collective-permute-start(bf16[2,128,128]{2,1,0:T(8,128)(2,1)S(1)} %join.1.rest_0_), channel_id=1, source_target_pairs={{0,12},{4,0},{8,4},{12,8},{1,13},{5,1},{9,5},{13,9},{2,14},{6,2},{... | collective-permute-start | bytes 196616 | tf_op jit(solution)/shard_map/ppermute | solution.py:597
  37.9 0.0 collective-permute-start.8
  37.9 0.6 %collective-permute-start.7 = (bf16[2,128,128]{2,1,0:T(8,128)(2,1)S(1)}, bf16[2,128,128]{2,1,0:T(8,128)(2,1)S(1)}, u32[]{:S(2)}, u32[]{:S(2)}) collective-permute-start(bf16[2,128,128]{2,1,0:T(8,128)(2,1)S(1)} %join.1.rest_0_), channel_id=1, source_target_pairs={{0,4},{4,8},{8,12},{12,0},{1,5},{5,9},{9,13},{13,1},{2,6},{6,10},{... | collective-permute-start | bytes 196616 | tf_op jit(solution)/shard_map/ppermute | solution.py:597
  38.5 4.3 %slopes.5 = (bf16[24,4,128,128]{3,2,1,0:T(8,128)(2,1)S(1)}, f32[24,8,128]{2,1,0:T(8,128)S(1)}, s32[1]{0:T(128)}) custom-call(s32[1,2,4,64]{3,2,1,0:T(4,128)S(1)} %bitcast.16, f32[22,8,128]{2,1,0:T(8,128)S(1)} %copy-done.6, s32[3,8,128]{2,1,0:T(8,128)S(1)} %copy-done.8, bf16[128,128]{1,0:T(8,128)(2,1)S(1)} %copy-done.7, s32[64,128]{1,0:T(8,128)S(1)} %bitcast.12, ...), custom_call_target="tpu_custom_call" | custom-call | flops 3600000000 | bytes 7200000 | tf_op jit(solution)/shard_map/slopes/pallas_call | solution.py:359
  42.8 0.0 collective-permute-done.10.other_ref
  42.9 0.7 %tile.1 = f32[128,128]{1,0:T(8,128)} custom-call(f32[128,128]{1,0:T(8,128)S(1)} %get-tuple-element.35.own_ref, f32[128,128]{1,0:T(8,128)S(1)} %collective-permute-done.10.other_ref), custom_call_target="tpu_custom_call" | custom-call | tf_op jit(solution)/shard_map/tile/pallas_call | solution.py:504
  43.6 0.0 collective-permute-done.9.rest_3_
  43.6 0.9 %collective-permute-done.8.rest_2_ = bf16[2,128,128]{2,1,0:T(8,128)(2,1)S(1)} collective-permute-done((bf16[2,128,128]{2,1,0:T(8,128)(2,1)S(1)}, bf16[2,128,128]{2,1,0:T(8,128)(2,1)S(1)}, u32[]{:S(2)}, u32[]{:S(2)}) %collective-permute-start.8) | collective-permute-done | bytes 65568 | tf_op jit(solution)/shard_map/ppermute | solution.py:597
  44.5 0.0 collective-permute-done.7.rest_1_
  44.5 0.0 copy-done.5
  44.5 4.0 %gradients.1 = f32[1,2,4,64]{3,2,1,0:T(4,128)} custom-call(s32[1,1,64]{2,1,0:T(1,128)S(1)} %bitcast.18, bf16[2,256,160]{2,1,0:T(8,128)(2,1)S(1)} %get-tuple-element.24.band_ref, bf16[2,128,128]{2,1,0:T(8,128)(2,1)S(1)} %join.1.rest_0_, bf16[2,128,128]{2,1,0:T(8,128)(2,1)S(1)} %collective-permute-done.7.rest_1_, ...), custom_call_target="tpu_custom_call" | custom-call | flops 4000000000 | bytes 20000000 | tf_op jit(solution)/shard_map/gradients/pallas_call | solution.py:577
  (2 shorter events, 0.0 us)
Async XLA Ops:
  0.6 10.8 %copy-start.2 = (bf16[1,64,128,128]{3,2,1,0:T(8,128)(2,1)S(1)}, bf16[1,64,128,128]{3,2,1,0:T(8,128)(2,1)}, u32[]{:S(2)}) copy-start(bf16[1,64,128,128]{3,2,1,0:T(8,128)(2,1)} %param.9) | copy-start | bytes 6291460
  0.6 10.8 %copy-start.3 = (s32[1,64,128]{2,1,0:T(8,128)S(1)}, s32[1,64,128]{2,1,0:T(8,128)}, u32[]{:S(2)}) copy-start(s32[1,64,128]{2,1,0:T(8,128)} %param.12) | copy-start | bytes 98308
  0.7 10.8 %copy-start.4 = (s32[1,64,2,4]{1,3,2,0:T(4,128)S(1)}, s32[1,64,2,4]{1,3,2,0:T(4,128)}, u32[]{:S(2)}) copy-start(s32[1,64,2,4]{1,3,2,0:T(4,128)} %param.11) | copy-start | bytes 6148
  0.7 10.8 %copy-start.6 = (f32[22,8,128]{2,1,0:T(8,128)S(1)}, f32[22,8,128]{2,1,0:T(8,128)}, u32[]{:S(2)}) copy-start(f32[22,8,128]{2,1,0:T(8,128)} %constant.6.clone.coef_ref) | copy-start | bytes 270340
  0.7 10.8 %copy-start.7 = (bf16[128,128]{1,0:T(8,128)(2,1)S(1)}, bf16[128,128]{1,0:T(8,128)(2,1)}, u32[]{:S(2)}) copy-start(bf16[128,128]{1,0:T(8,128)(2,1)} %constant.8.clone.near_ref) | copy-start | bytes 98308
  0.7 10.8 %copy-start.8 = (s32[3,8,128]{2,1,0:T(8,128)S(1)}, s32[3,8,128]{2,1,0:T(8,128)}, u32[]{:S(2)}) copy-start(s32[3,8,128]{2,1,0:T(8,128)} %constant.7.clone.rows_ref) | copy-start | bytes 36868
  8.4 7.4 %copy-start.1 = (f32[2,2,9]{2,1,0:T(2,128)S(1)}, f32[2,2,9]{2,1,0:T(2,128)}, u32[]{:S(2)}) copy-start(f32[2,2,9]{2,1,0:T(2,128)} %psf_ref.1) | copy-start | bytes 436
  8.4 9.5 %copy-start = (f32[4,2,128,128]{3,2,1,0:T(8,128)S(1)}, f32[4,2,128,128]{3,2,1,0:T(8,128)}, u32[]{:S(2)}) copy-start(f32[4,2,128,128]{3,2,1,0:T(8,128)} %get-tuple-element.28.keep_ref) | copy-start | bytes 1572868
  8.4 9.5 %collective-permute-start = (bf16[4,2,128,128]{3,2,1,0:T(8,128)(2,1)}, bf16[4,2,128,128]{3,2,1,0:T(8,128)(2,1)S(1)}, u32[]{:S(2)}, u32[]{:S(2)}) collective-permute-start(bf16[4,2,128,128]{3,2,1,0:T(8,128)(2,1)} %get-tuple-element.29), channel_id=1, source_target_pairs={{0,16},{16,0},{1,17},{17,1},{2,18},{18,2},{3,19},{19,3},{4,20},{20... | collective-permute-start | bytes 786440 | tf_op jit(solution)/shard_map/ppermute | solution.py:593
  18.7 8.9 %collective-permute-start.1 = (bf16[2,128,128]{2,1,0:T(8,128)(2,1)S(1)}, bf16[2,128,128]{2,1,0:T(8,128)(2,1)S(1)}, u32[]{:S(2)}, u32[]{:S(2)}) collective-permute-start(bf16[2,128,128]{2,1,0:T(8,128)(2,1)S(1)} %get-tuple-element.32), channel_id=1, source_target_pairs={{0,4},{4,8},{8,12},{12,0},{1,5},{5,9},{9,13},{13,1},{2,6},{6,10},{... | collective-permute-start | bytes 196616 | tf_op jit(solution)/shard_map/ppermute | solution.py:597
  20.5 7.0 %collective-permute-start.2 = (bf16[2,128,128]{2,1,0:T(8,128)(2,1)S(1)}, bf16[2,128,128]{2,1,0:T(8,128)(2,1)S(1)}, u32[]{:S(2)}, u32[]{:S(2)}) collective-permute-start(bf16[2,128,128]{2,1,0:T(8,128)(2,1)S(1)} %get-tuple-element.33), channel_id=1, source_target_pairs={{0,8},{4,12},{8,0},{12,4},{1,9},{5,13},{9,1},{13,5},{2,10},{6,14},... | collective-permute-start | bytes 196616 | tf_op jit(solution)/shard_map/ppermute | solution.py:597
  23.1 4.5 %collective-permute-start.3 = (bf16[2,128,128]{2,1,0:T(8,128)(2,1)S(1)}, bf16[2,128,128]{2,1,0:T(8,128)(2,1)S(1)}, u32[]{:S(2)}, u32[]{:S(2)}) collective-permute-start(bf16[2,128,128]{2,1,0:T(8,128)(2,1)S(1)} %get-tuple-element.34), channel_id=1, source_target_pairs={{0,12},{4,0},{8,4},{12,8},{1,13},{5,1},{9,5},{13,9},{2,14},{6,2},{... | collective-permute-start | bytes 196616 | tf_op jit(solution)/shard_map/ppermute | solution.py:597
  28.5 5.6 %collective-permute-start.4 = (bf16[128,128]{1,0:T(8,128)(2,1)S(1)}, bf16[128,128]{1,0:T(8,128)(2,1)S(1)}, u32[]{:S(2)}, u32[]{:S(2)}) collective-permute-start(bf16[128,128]{1,0:T(8,128)(2,1)S(1)} %get-tuple-element.36), channel_id=1, source_target_pairs={{0,16},{16,0},{1,17},{17,1},{2,18},{18,2},{3,19},{19,3},{4,20},{20... | collective-permute-start | bytes 98312 | tf_op jit(solution)/shard_map/ppermute | solution.py:593
  30.1 3.9 %collective-permute-start.6 = (bf16[16,128]{1,0:T(8,128)(2,1)S(1)}, bf16[16,128]{1,0:T(8,128)(2,1)S(1)}, u32[]{:S(2)}, u32[]{:S(2)}) collective-permute-start(bf16[16,128]{1,0:T(8,128)(2,1)S(1)} %get-tuple-element.37), channel_id=1, source_target_pairs={{0,19},{1,16},{2,17},{3,18},{16,1},{17,2},{18,3},{19,0},{4,23},{5,... | collective-permute-start | bytes 12296 | tf_op jit(solution)/shard_map/ppermute | solution.py:603
  30.1 3.9 %collective-permute-start.5 = (bf16[16,128]{1,0:T(8,128)(2,1)S(1)}, bf16[16,128]{1,0:T(8,128)(2,1)S(1)}, u32[]{:S(2)}, u32[]{:S(2)}) collective-permute-start(bf16[16,128]{1,0:T(8,128)(2,1)S(1)} %get-tuple-element.37), channel_id=1, source_target_pairs={{0,3},{1,0},{2,1},{3,2},{16,17},{17,18},{18,19},{19,16},{4,7},{5,4... | collective-permute-start | bytes 12296 | tf_op jit(solution)/shard_map/ppermute | solution.py:603
  31.9 10.9 %collective-permute-start.10 = (f32[128,128]{1,0:T(8,128)S(1)}, f32[128,128]{1,0:T(8,128)S(1)}, u32[]{:S(2)}, u32[]{:S(2)}) collective-permute-start(f32[128,128]{1,0:T(8,128)S(1)} %get-tuple-element.35.own_ref), channel_id=1, source_target_pairs={{0,16},{16,0},{1,17},{17,1},{2,18},{18,2},{3,19},{19,3},{4,20},{20... | collective-permute-start | bytes 196616 | tf_op jit(solution)/shard_map/ppermute | solution.py:593
  35.0 9.5 %copy-start.5 = (s32[1,64,1]{1,2,0:T(1,128)S(1)}, s32[1,64,1]{1,2,0:T(1,128)}, u32[]{:S(2)}) copy-start(s32[1,64,1]{1,2,0:T(1,128)} %param.10) | copy-start | bytes 772
  35.0 8.5 %collective-permute-start.9 = (bf16[2,128,128]{2,1,0:T(8,128)(2,1)S(1)}, bf16[2,128,128]{2,1,0:T(8,128)(2,1)S(1)}, u32[]{:S(2)}, u32[]{:S(2)}) collective-permute-start(bf16[2,128,128]{2,1,0:T(8,128)(2,1)S(1)} %join.1.rest_0_), channel_id=1, source_target_pairs={{0,12},{4,0},{8,4},{12,8},{1,13},{5,1},{9,5},{13,9},{2,14},{6,2},{... | collective-permute-start | bytes 196616 | tf_op jit(solution)/shard_map/ppermute | solution.py:597
  37.9 6.7 %collective-permute-start.8 = (bf16[2,128,128]{2,1,0:T(8,128)(2,1)S(1)}, bf16[2,128,128]{2,1,0:T(8,128)(2,1)S(1)}, u32[]{:S(2)}, u32[]{:S(2)}) collective-permute-start(bf16[2,128,128]{2,1,0:T(8,128)(2,1)S(1)} %join.1.rest_0_), channel_id=1, source_target_pairs={{0,8},{4,12},{8,0},{12,4},{1,9},{5,13},{9,1},{13,5},{2,10},{6,14},... | collective-permute-start | bytes 196616 | tf_op jit(solution)/shard_map/ppermute | solution.py:597
  37.9 6.7 %collective-permute-start.7 = (bf16[2,128,128]{2,1,0:T(8,128)(2,1)S(1)}, bf16[2,128,128]{2,1,0:T(8,128)(2,1)S(1)}, u32[]{:S(2)}, u32[]{:S(2)}) collective-permute-start(bf16[2,128,128]{2,1,0:T(8,128)(2,1)S(1)} %join.1.rest_0_), channel_id=1, source_target_pairs={{0,4},{4,8},{8,12},{12,0},{1,5},{5,9},{9,13},{13,1},{2,6},{6,10},{... | collective-permute-start | bytes 196616 | tf_op jit(solution)/shard_map/ppermute | solution.py:597
